TPU v7x, 32 devices: a whole 2x2x4 slice. The times are simulated.
32 devices in a mesh: frag: 2 (over x), pair: 16 (over z, y, core).
Axes of the slice: x: 2, y: 2, z: 4, core: 2. Of those that a mesh axis runs over, the one named last changes fastest.
Arguments:
- amplitudes: float32 [256, 4096], P(('frag', 'pair')), parts along dimension 0, may hold values from -6 to 6
- integrals: float32 [256, 4096], P(('frag', 'pair')), parts along dimension 0, may hold values from -6 to 6
- virtual: float32 [256, 64], P(('frag', 'pair')), parts along dimension 0, may hold values from 0.3 to 3
- occupied: float32 [256], P(('frag', 'pair')), parts along dimension 0, may hold values from -2 to -0.4
- coupling: float32 [256, 16], P(('frag', 'pair')), parts along dimension 0, may hold values from -3 to 3
- degree: int32 [256], P(('frag', 'pair')), parts along dimension 0, may hold values from 1 to 16, as said below
- position: int32 [256, 16], P(('frag', 'pair')), parts along dimension 0, may hold values from 0 to 31
- request: int32 [32, 32], P(('frag', 'pair')), parts along dimension 0, may hold values from 0 to 7
- pnos: bfloat16 [256, 64, 256], P(('frag', 'pair')), parts along dimension 0, may hold values from -1.5 to 1.5
- domains: int32 [256, 16], P(('frag', 'pair')), parts along dimension 0, may hold values from 0 to 31, as said below
Outputs:
- new_amplitudes: float32 [256, 4096], P(('frag', 'pair')), parts along dimension 0
- residual: float32 [256, 4096], P(('frag', 'pair')), parts along dimension 0
There are 2 independent parts, one for each index of `frag`. A program takes and returns all parts, laid end to end along the dimension named above; each array names one. Nothing has to cross between parts.
Inputs may be any that keep to these rules, and one draw needn't show every extreme that they name: `degree`: every pair has at least one coupling, and some pair has 16. `domains`: the 16 atoms of a pair's domain are distinct.
All inputs are finite; a program needn't handle non-finite values.
Results may differ from a plain program's by a relative error of at most 0.0003.
Values may be sent and summed in bfloat16 or wider, within the bound.
No kernel may reach another device: no remote copies, remote signals or barrier semaphores. Data moves between devices by JAX's collectives and lax.ppermute only.
A program may use at most 128 MiB of HBM per device.

v0:
```python
import jax
import jax.numpy as jnp
from jax import lax
from jax.sharding import PartitionSpec as P

SWEEPS = 2


def orbital_ids(atoms, per_atom):
    offsets = jnp.arange(per_atom, dtype=jnp.int32)
    return (atoms[:, :, None] * per_atom + offsets[None, None, :]).reshape(atoms.shape[0], -1)


def intersection(own_pnos, own_ids, other_pnos, other_atoms, per_atom):
    other_ids = orbital_ids(other_atoms, per_atom)
    match_table = (other_ids[:, :, None] == own_ids[:, None, :]).astype(jnp.bfloat16)
    mapped = jnp.einsum(
        "sqz,szy->sqy", other_pnos, match_table, preferred_element_type=jnp.float32
    ).astype(jnp.bfloat16)
    return jnp.einsum("spy,sqy->spq", own_pnos, mapped, preferred_element_type=jnp.float32)


def transform(intersection_mat, partner_block):
    left_half = jnp.einsum(
        "spq,sqr->spr", intersection_mat, partner_block, precision=lax.Precision.HIGHEST
    )
    return jnp.einsum("spr,str->spt", left_half, intersection_mat, precision=lax.Precision.HIGHEST)


def on_device(
    amplitudes, integrals, virtual, occupied, coupling, degree, position, request, pnos, domains
):
    slot_count, block_size = amplitudes.shape
    pno_size = virtual.shape[1]
    coupling_depth = coupling.shape[1]
    per_atom = pnos.shape[2] // domains.shape[1]
    own_ids = orbital_ids(domains, per_atom)
    wanted = lax.all_to_all(request, "pair", split_axis=1, concat_axis=0, tiled=True).reshape(-1)
    denominator = (virtual[:, :, None] + virtual[:, None, :] - occupied[:, None, None]).reshape(
        slot_count, block_size
    )
    live_mask = jnp.arange(coupling_depth, dtype=jnp.int32)[None, :] < degree[:, None]
    weight = jnp.where(live_mask, coupling, jnp.zeros_like(coupling))
    chosen_cols = position.T
    weight_cols = weight.T
    empty_sum = jnp.zeros((slot_count, block_size), jnp.float32)

    def add_term(running, amp_buffer, chosen, intersection_mat, weight_col):
        partner_block = amp_buffer[chosen].reshape(slot_count, pno_size, pno_size)
        product = transform(intersection_mat, partner_block).reshape(slot_count, block_size)
        return running + weight_col[:, None] * product

    current = amplitudes
    residual = empty_sum
    for sweep in range(SWEEPS):
        outgoing = jnp.take(current, wanted, axis=0)
        amp_buffer = lax.all_to_all(outgoing, "pair", split_axis=0, concat_axis=0, tiled=True)
        pno_buffer, atom_buffer = (
            lax.all_to_all(
                jnp.take(pnos, wanted, axis=0), "pair", split_axis=0, concat_axis=0, tiled=True
            ),
            lax.all_to_all(
                jnp.take(domains, wanted, axis=0), "pair", split_axis=0, concat_axis=0, tiled=True
            ),
        )

        def add_coupling(running, inputs):
            chosen, weight_col = inputs
            intersection_mat = intersection(
                pnos, own_ids, pno_buffer[chosen], atom_buffer[chosen], per_atom
            )
            return (add_term(running, amp_buffer, chosen, intersection_mat, weight_col), None)

        coupled_term, unused = lax.scan(add_coupling, empty_sum, (chosen_cols, weight_cols))
        residual = integrals + denominator * current - coupled_term
        current = current - residual / denominator
    return (current, residual)


def solution(mesh):
    return jax.shard_map(
        on_device,
        mesh=mesh,
        in_specs=(
            P(("frag", "pair"), None),
            P(("frag", "pair"), None),
            P(("frag", "pair"), None),
            P(("frag", "pair")),
            P(("frag", "pair"), None),
            P(("frag", "pair")),
            P(("frag", "pair"), None),
            P(("frag", "pair"), None),
            P(("frag", "pair"), None, None),
            P(("frag", "pair"), None),
        ),
        out_specs=(P(("frag", "pair"), None), P(("frag", "pair"), None)),
        check_vma=False,
    )
```

profile of v0, /device:TPU:0, one launch (start us, length us, event | category | flops | bytes accessed | tf_op | source)
XLA Modules:
  0.0 233.8 jit_solution(17613369916010136195)
XLA Ops:
  1.2 1.3 reduce.6
  2.6 13.6 %all_to_all.56 = s32[1,16,2]{2,0,1:T(1,128)S(1)} all-to-all(s32[1,16,2]{2,0,1:T(1,128)S(1)} %bitcast.68), channel_id=1, replica_groups=mesh['frag'=2,'pair'=16] {'pair'}, dimensions={1} | all-to-all | bytes 256 | tf_op jit(solution)/shard_map/all_to_all | solution.py:38
  16.1 0.7 reduce.7
  16.9 1.3 gather_fusion.7
  18.2 0.7 broadcast_select_fusion.3
  18.9 3.5 %all-to-all-start.2 = ((s32[16,2,16]{2,1,0:T(2,128)}), s32[16,2,16]{2,1,0:T(2,128)S(1)}, u32[]{:S(2)}, u32[]{:S(2)}) async-start(s32[16,2,16]{2,1,0:T(2,128)} %bitcast.3), calls=%async_computation.2 | async-start | bytes 32768 | tf_op jit(solution)/shard_map/all_to_all | solution.py:62
  22.4 0.7 gather_fusion.8
  23.3 1.1 all_to_all.45
  24.4 4.5 %all-to-all-done.2 = s32[16,2,16]{2,1,0:T(2,128)S(1)} async-done(((s32[16,2,16]{2,1,0:T(2,128)}), s32[16,2,16]{2,1,0:T(2,128)S(1)}, u32[]{:S(2)}, u32[]{:S(2)}) %all-to-all-start.2) | async-done | bytes 2080 | tf_op jit(solution)/shard_map/all_to_all | solution.py:62
  28.9 3.6 %all-to-all-start.3 = ((f32[16,2,4096]{2,1,0:T(2,128)}), f32[16,2,4096]{2,1,0:T(2,128)S(1)}, u32[]{:S(2)}, u32[]{:S(2)}) async-start(f32[16,2,4096]{2,1,0:T(2,128)} %all_to_all.45), calls=%async_computation.3 | async-start | bytes 1048576 | tf_op jit(solution)/shard_map/all_to_all | solution.py:57
  33.1 1.1 broadcast_select_fusion
  34.2 12.6 %all-to-all-done.3 = f32[16,2,4096]{2,1,0:T(2,128)S(1)} async-done(((f32[16,2,4096]{2,1,0:T(2,128)}), f32[16,2,4096]{2,1,0:T(2,128)S(1)}, u32[]{:S(2)}, u32[]{:S(2)}) %all-to-all-start.3) | async-done | bytes 524320 | tf_op jit(solution)/shard_map/all_to_all | solution.py:57
  46.9 4.0 %all-to-all-start.1 = ((bf16[32,64,256]{2,1,0:T(8,128)(2,1)}), bf16[32,64,256]{2,1,0:T(8,128)(2,1)S(1)}, u32[]{:S(2)}, u32[]{:S(2)}) async-start(bf16[32,64,256]{2,1,0:T(8,128)(2,1)} %broadcast_select_fusion), calls=%async_computation.1 | async-start | bytes 2097152 | tf_op jit(solution)/shard_map/all_to_all | solution.py:59
  51.7 22.1 %all-to-all-done.1 = bf16[32,64,256]{2,1,0:T(8,128)(2,1)S(1)} async-done(((bf16[32,64,256]{2,1,0:T(8,128)(2,1)}), bf16[32,64,256]{2,1,0:T(8,128)(2,1)S(1)}, u32[]{:S(2)}, u32[]{:S(2)}) %all-to-all-start.1) | async-done | bytes 1048608 | tf_op jit(solution)/shard_map/all_to_all | solution.py:59
  73.8 67.7 %while.22 = (s32[]{:T(128)}, f32[8,4096]{1,0:T(8,128)S(1)}, f32[16,8]{1,0:T(8,128)S(1)}, s32[16,8]{1,0:T(8,128)S(1)}, bf16[32,64,256]{2,1,0:T(8,128)(2,1)S(1)}, ...) while((s32[]{:T(128)}, f32[8,4096]{1,0:T(8,128)S(1)}, ...), condition=%wide.region_1.0_spmd.clone, body=%wide.region_0.4_spmd.clone.sunk | while | flops 134976672 | bytes 3239327 | solution.py:74
  75.5 0.7 fusion.76
  79.7 0.7 fusion.76
  88.1 0.7 fusion.76
  96.6 0.7 fusion.76
  117.8 0.7 fusion.76
  126.2 0.7 fusion.76
  141.6 0.7 gather_fusion.9
  142.5 1.1 all_to_all.48
  143.6 6.9 %all-to-all-start.4 = ((f32[16,2,4096]{2,1,0:T(2,128)}), f32[16,2,4096]{2,1,0:T(2,128)S(1)}, u32[]{:S(2)}, u32[]{:S(2)}) async-start(f32[16,2,4096]{2,1,0:T(2,128)} %all_to_all.48), calls=%async_computation.4 | async-start | bytes 1048576 | tf_op jit(solution)/shard_map/all_to_all | solution.py:57
  150.5 14.5 %all-to-all-done.4 = f32[16,2,4096]{2,1,0:T(2,128)S(1)} async-done(((f32[16,2,4096]{2,1,0:T(2,128)}), f32[16,2,4096]{2,1,0:T(2,128)S(1)}, u32[]{:S(2)}, u32[]{:S(2)}) %all-to-all-start.4) | async-done | bytes 524320 | tf_op jit(solution)/shard_map/all_to_all | solution.py:57
  165.3 67.7 %while.23 = (s32[]{:T(128)}, f32[8,4096]{1,0:T(8,128)S(1)}, f32[16,8]{1,0:T(8,128)S(1)}, s32[16,8]{1,0:T(8,128)S(1)}, bf16[32,64,256]{2,1,0:T(8,128)(2,1)S(1)}, ...) while((s32[]{:T(128)}, f32[8,4096]{1,0:T(8,128)S(1)}, ...), condition=%wide.region_3.7_spmd.clone, body=%wide.region_2.6_spmd.clone.sunk | while | flops 134976672 | bytes 3239327 | solution.py:74
  166.9 0.7 fusion.87
  175.4 0.7 fusion.87
  196.5 0.7 fusion.87
  205.0 0.7 fusion.87
  226.2 0.7 fusion.87
  233.0 0.8 divide_subtract_fusion
  (667 shorter events, 127.1 us)
Async XLA Ops:
  0.6 21.8 %copy-start = (f32[8,4096]{1,0:T(8,128)S(1)}, f32[8,4096]{1,0:T(8,128)}, u32[]{:S(2)}) copy-start(f32[8,4096]{1,0:T(8,128)} %param.20) | copy-start | bytes 393220
  18.9 10.0 %all-to-all-start.2 = ((s32[16,2,16]{2,1,0:T(2,128)}), s32[16,2,16]{2,1,0:T(2,128)S(1)}, u32[]{:S(2)}, u32[]{:S(2)}) async-start(s32[16,2,16]{2,1,0:T(2,128)} %bitcast.3), calls=%async_computation.2 | async-start | bytes 32768 | tf_op jit(solution)/shard_map/all_to_all | solution.py:62
  23.2 9.2 %copy-start.2 = (bf16[8,64,256]{2,1,0:T(8,128)(2,1)S(1)}, bf16[8,64,256]{2,1,0:T(8,128)(2,1)}, u32[]{:S(2)}) copy-start(bf16[8,64,256]{2,1,0:T(8,128)(2,1)} %param.28) | copy-start | bytes 786436
  28.9 18.0 %all-to-all-start.3 = ((f32[16,2,4096]{2,1,0:T(2,128)}), f32[16,2,4096]{2,1,0:T(2,128)S(1)}, u32[]{:S(2)}, u32[]{:S(2)}) async-start(f32[16,2,4096]{2,1,0:T(2,128)} %all_to_all.45), calls=%async_computation.3 | async-start | bytes 1048576 | tf_op jit(solution)/shard_map/all_to_all | solution.py:57
  34.2 16.7 %copy-start.5 = (f32[8,16]{1,0:T(8,128)S(1)}, f32[8,16]{1,0:T(8,128)}, u32[]{:S(2)}) copy-start(f32[8,16]{1,0:T(8,128)} %param.24) | copy-start | bytes 1540
  34.2 16.8 %copy-start.6 = (s32[8,16]{1,0:T(8,128)S(1)}, s32[8,16]{1,0:T(8,128)}, u32[]{:S(2)}) copy-start(s32[8,16]{1,0:T(8,128)} %param.26) | copy-start | bytes 1540
  34.2 16.9 %copy-start.4 = (f32[8,64]{1,0:T(8,128)S(1)}, f32[8,64]{1,0:T(8,128)}, u32[]{:S(2)}) copy-start(f32[8,64]{1,0:T(8,128)} %param.22) | copy-start | bytes 6148
  34.2 17.1 %copy-start.1 = (s32[8,16]{1,0:T(8,128)S(1)}, s32[8,16]{1,0:T(8,128)}, u32[]{:S(2)}) copy-start(s32[8,16]{1,0:T(8,128)} %param.29) | copy-start | bytes 1540
  34.2 17.1 %copy-start.8 = (s32[8]{0:T(128)S(1)}, s32[8]{0:T(128)}, u32[]{:S(2)}) copy-start(s32[8]{0:T(128)} %param.25) | copy-start | bytes 100
  46.9 27.0 %all-to-all-start.1 = ((bf16[32,64,256]{2,1,0:T(8,128)(2,1)}), bf16[32,64,256]{2,1,0:T(8,128)(2,1)S(1)}, u32[]{:S(2)}, u32[]{:S(2)}) async-start(bf16[32,64,256]{2,1,0:T(8,128)(2,1)} %broadcast_select_fusion), calls=%async_computation.1 | async-start | bytes 2097152 | tf_op jit(solution)/shard_map/all_to_all | solution.py:59
  73.8 67.7 %copy-start.3 = (f32[8,4096]{1,0:T(8,128)S(1)}, f32[8,4096]{1,0:T(8,128)}, u32[]{:S(2)}) copy-start(f32[8,4096]{1,0:T(8,128)} %param.21) | copy-start | bytes 393220
  73.8 67.7 %copy-start.7 = (f32[8]{0:T(128)S(1)}, f32[8]{0:T(128)}, u32[]{:S(2)}) copy-start(f32[8]{0:T(128)} %param.23) | copy-start | bytes 100
  143.6 21.3 %all-to-all-start.4 = ((f32[16,2,4096]{2,1,0:T(2,128)}), f32[16,2,4096]{2,1,0:T(2,128)S(1)}, u32[]{:S(2)}, u32[]{:S(2)}) async-start(f32[16,2,4096]{2,1,0:T(2,128)} %all_to_all.48), calls=%async_computation.4 | async-start | bytes 1048576 | tf_op jit(solution)/shard_map/all_to_all | solution.py:57
where the time goes:
time: 234 us
  local copies, waits for them, and re-layouts  80.4 us (34%)
  waiting for transfers between devices  53.7 us (23%)
  matrix products  52.5 us (22%)
  starting transfers between devices  18 us (8%)
  blocking collectives  13.6 us (6%)
  other arithmetic  11.1 us (5%)
  loops' own time  3.7 us (2%)
    all_to_all x2, waiting for transfers between devices, on_device(): lax.all_to_all(outgoing, 'pair', split_axis=0, concat_axis=0, tiled=True)  27.1 us
    all_to_all x1, waiting for transfers between devices, on_device(): lax.all_to_all(jnp.take(pnos, wanted, axis=0), 'pair', split_axis=0, conc...  22.1 us
    dot_general x32, matrix products, intersection(): jnp.einsum('spy,sqy->spq', own_pnos, mapped, preferred_element_type=jnp.f...  21.4 us
    gather x32, local copies, waits for them, and re-layouts, add_term(): partner_block = amp_buffer[chosen].reshape(slot_count, pno_size, pno_size)  19.2 us
    dot_general x32, matrix products, transform(): jnp.einsum('spq,sqr->spr', intersection_mat, partner_block, precision=lax...  18.9 us
    gather x32, local copies, waits for them, and re-layouts, add_coupling(): pno_buffer[chosen]  18 us
    gather x32, local copies, waits for them, and re-layouts, add_coupling(): atom_buffer[chosen]  17.8 us
    all_to_all x1, blocking collectives, on_device(): lax.all_to_all(request, 'pair', split_axis=1, concat_axis=0, tiled=True)  13.6 us
  transfers between devices with their start and end apart: 4, of which 4 were waited for; matrix products, arithmetic and copies ran while one was open for 1% of the time, Pallas kernels for 0%

commit v1 on v0

v1 whole, which is shorter than its diff:
```python
import functools
import jax
import jax.numpy as jnp
from jax import lax
from jax.experimental import pallas as pl
from jax.experimental.pallas import tpu as pltpu
from jax.sharding import Mesh, PartitionSpec as P

ATOMS = 32
CHUNK = 8
VMEM_LIMIT = 48 * 1024 * 1024
NT = (((1,), (1,)), ((), ()))


def split(value):
    high = value.astype(jnp.bfloat16)
    low = (value - high.astype(jnp.float32)).astype(jnp.bfloat16)
    return high, low


def sweep_chunk(half_ref, weight_ref, amp_ref, cat_ref, left_ref, acc_ref):
    pairs, rows2, lanes = cat_ref.shape
    size = rows2 // 2
    chunk = pl.program_id(0)
    near = amp_ref.shape[0] // 2
    group = lax.broadcasted_iota(jnp.int32, (size, 4 * size), 1) // size
    even = (group % 2 == 0).astype(jnp.float32).astype(jnp.bfloat16)
    odd = (group % 2 == 1).astype(jnp.float32).astype(jnp.bfloat16)
    for j in range(lanes // (2 * size)):
        cols = slice(j * 2 * size, (j + 1) * 2 * size)
        entry = chunk * (lanes // (2 * size)) + j
        source = (entry % 2 + half_ref[0]) % 2 * near + entry // 2
        amp = amp_ref[source]
        first, second = amp * even, amp * odd
        right = jnp.concatenate([first, second, first, second], axis=0)
        high = cat_ref[:, :size, cols].reshape(pairs * size, 2 * size)
        low = cat_ref[:, size:, cols].reshape(pairs * size, 2 * size)
        both = jnp.dot(
            jnp.concatenate([high, low], axis=1), right, preferred_element_type=jnp.float32
        )
        left = (both[:, : 2 * size] + both[:, 2 * size :]).reshape(pairs, size, 2 * size)
        left = left * weight_ref[0, :, cols].reshape(pairs, 1, 2 * size)
        left_high, left_low = split(left)
        left_ref[:, :size, cols] = left_high
        left_ref[:, size:, cols] = left_low
    for s in range(pairs):
        part = lax.dot_general(
            left_ref[s], cat_ref[s], NT, preferred_element_type=jnp.float32
        )
        acc_ref[s] = jnp.where(chunk == 0, part, acc_ref[s] + part)


def coupled_of(acc):
    size = acc.shape[0] // 2
    rows = acc[:size] + acc[size:]
    return rows[:, :size] + rows[:, size:]


def first_kernel(
    half_ref, wanted_ref, own_ref, pnos_ref, ids_ref, weight_ref, amp_ref, current_ref,
    integrals_ref, denominator_ref, cat_ref, new_ref, send_ref, full_ref, left_ref, acc_ref,
    even_ref, odd_ref,
):
    pairs, size, unused = current_ref.shape
    columns = own_ref.shape[1]
    width = pnos_ref.shape[2]

    row_ids = lax.broadcasted_iota(jnp.int32, (columns, width), 0)
    for p in range(pnos_ref.shape[0]):
        table = (row_ids == ids_ref[p]).astype(jnp.float32).astype(jnp.bfloat16)
        full_ref[p * size : (p + 1) * size, :] = lax.dot_general(
            pnos_ref[p], table, NT, preferred_element_type=jnp.float32
        ).astype(jnp.bfloat16)
    cross = lax.dot_general(own_ref[...], full_ref[...], NT, preferred_element_type=jnp.float32)
    high, low = split(cross)
    cat_ref[0, :, :size, :] = high.reshape(pairs, size, -1)
    cat_ref[0, :, size:, :] = low.reshape(pairs, size, -1)
    sweep_chunk(half_ref, weight_ref, amp_ref, cat_ref.at[0], left_ref, acc_ref)

    @pl.when(pl.program_id(0) == pl.num_programs(0) - 1)
    def finish():
        blank = jnp.zeros((size, size), jnp.float32)
        for s in range(pairs):
            denominator = denominator_ref[s]
            residual = integrals_ref[s] + denominator * current_ref[s] - coupled_of(acc_ref[s])
            new = current_ref[s] - residual / denominator
            new_ref[s] = new
            high, low = split(new)
            high, low = high.astype(jnp.float32), low.astype(jnp.float32)
            even_ref[s] = jnp.concatenate([high, blank, low, blank], axis=1).astype(jnp.bfloat16)
            odd_ref[s] = jnp.concatenate([blank, high, blank, low], axis=1).astype(jnp.bfloat16)

        def pack(d, carry):
            send_ref[d] = even_ref[wanted_ref[2 * d]] + odd_ref[wanted_ref[2 * d + 1]]
            return carry

        lax.fori_loop(0, send_ref.shape[0], pack, 0)


def second_kernel(
    half_ref, cat_ref, weight_ref, amp_ref, current_ref, integrals_ref, denominator_ref,
    new_ref, residual_ref, left_ref, acc_ref, new_rows_ref, residual_rows_ref,
):
    pairs, size, unused = current_ref.shape

    sweep_chunk(half_ref, weight_ref, amp_ref, cat_ref.at[0], left_ref, acc_ref)

    @pl.when(pl.program_id(0) == pl.num_programs(0) - 1)
    def finish():
        for s in range(pairs):
            denominator = denominator_ref[s]
            residual = integrals_ref[s] + denominator * current_ref[s] - coupled_of(acc_ref[s])
            rows = slice(s * size, (s + 1) * size)
            residual_rows_ref[rows, :] = residual
            new_rows_ref[rows, :] = current_ref[s] - residual / denominator
        for rows_ref, out_ref in ((residual_rows_ref, residual_ref), (new_rows_ref, new_ref)):
            for a in range(0, size, 2):
                out_ref[:, a * size : (a + 2) * size] = jnp.concatenate(
                    [rows_ref[pl.ds(a + i, pairs, stride=size), :] for i in range(2)], axis=1
                )


def smem():
    return pl.BlockSpec(memory_space=pltpu.SMEM)


def whole(shape):
    return pl.BlockSpec(shape, lambda i: (0,) * len(shape))


def by_chunk(shape):
    return pl.BlockSpec(shape, lambda i: (i,) + (0,) * (len(shape) - 1))


def params():
    return pltpu.CompilerParams(
        dimension_semantics=("arbitrary",), vmem_limit_bytes=VMEM_LIMIT
    )


def first_sweep(half, wanted, own, pnos, ids, weight, amp, current, integrals, denominator):
    pairs, size, unused = current.shape
    slots, unused, width = pnos.shape
    steps = slots // CHUNK
    sources = amp.shape[0]
    lanes = CHUNK * size
    block = (pairs, size, size)
    return pl.pallas_call(
        first_kernel,
        grid=(steps,),
        in_specs=[
            smem(), smem(), whole(own.shape), by_chunk((CHUNK, size, width)),
            by_chunk((CHUNK, 1, width)), by_chunk((1, pairs, lanes)), whole(amp.shape),
            whole(block), whole(block), whole(block),
        ],
        out_specs=[
            by_chunk((1, pairs, 2 * size, lanes)), whole(block), whole(amp.shape),
        ],
        out_shape=[
            jax.ShapeDtypeStruct((steps, pairs, 2 * size, lanes), jnp.bfloat16),
            jax.ShapeDtypeStruct(block, jnp.float32),
            jax.ShapeDtypeStruct(amp.shape, jnp.bfloat16),
        ],
        scratch_shapes=[
            pltpu.VMEM((lanes, own.shape[1]), jnp.bfloat16),
            pltpu.VMEM((pairs, 2 * size, lanes), jnp.bfloat16),
            pltpu.VMEM((pairs, 2 * size, 2 * size), jnp.float32),
            pltpu.VMEM((pairs, size, 4 * size), jnp.bfloat16),
            pltpu.VMEM((pairs, size, 4 * size), jnp.bfloat16),
        ],
        compiler_params=params(),
        name="first_sweep",
    )(half, wanted, own, pnos, ids, weight, amp, current, integrals, denominator)


def second_sweep(half, cat, weight, amp, current, integrals, denominator):
    pairs, size, unused = current.shape
    steps, lanes = cat.shape[0], cat.shape[3]
    block = (pairs, size, size)
    flat = (pairs, size * size)
    return pl.pallas_call(
        second_kernel,
        grid=(steps,),
        in_specs=[
            smem(), by_chunk((1,) + cat.shape[1:]), by_chunk((1, pairs, lanes)),
            whole(amp.shape), whole(block), whole(block), whole(block),
        ],
        out_specs=[whole(flat), whole(flat)],
        out_shape=[jax.ShapeDtypeStruct(flat, jnp.float32)] * 2,
        scratch_shapes=[
            pltpu.VMEM((pairs, 2 * size, lanes), jnp.bfloat16),
            pltpu.VMEM((pairs, 2 * size, 2 * size), jnp.float32),
            pltpu.VMEM((pairs * size, size), jnp.float32),
            pltpu.VMEM((pairs * size, size), jnp.float32),
        ],
        compiler_params=params(),
        name="second_sweep",
    )(half, cat, weight, amp, current, integrals, denominator)


def orbital_ids(atoms, per_atom):
    offsets = jnp.arange(per_atom, dtype=jnp.int32)
    return (atoms[:, :, None] * per_atom + offsets[None, None, :]).reshape(atoms.shape[0], -1)


def on_device(
    amplitudes, integrals, virtual, occupied, coupling, degree, position, request, pnos, domains
):
    pairs = amplitudes.shape[0]
    size = virtual.shape[1]
    depth = coupling.shape[1]
    per_atom = pnos.shape[2] // domains.shape[1]
    columns = ATOMS * per_atom
    slots = request.shape[1]
    sources = slots // 2
    near = sources // 2
    half = lax.axis_index("half").astype(jnp.int32)
    swap = [(0, 1), (1, 0)]
    block = (pairs, size, size)

    far_pnos = lax.ppermute(pnos, "half", swap)
    asked = request.reshape(2, near, 2).transpose(1, 0, 2)
    asked = lax.all_to_all(asked, "near", split_axis=0, concat_axis=0, tiled=True)
    here = lax.dynamic_index_in_dim(asked, half, 1, keepdims=False)
    there = lax.dynamic_index_in_dim(asked, 1 - half, 1, keepdims=False)
    from_far = lax.ppermute(there, "half", swap)
    wanted = jnp.where(
        half == 0, jnp.concatenate([here, from_far]), jnp.concatenate([from_far, here])
    ).reshape(-1)

    outgoing = jnp.stack([pnos[here], far_pnos[there]], axis=1)
    partner_pnos = lax.all_to_all(
        outgoing, "near", split_axis=0, concat_axis=0, tiled=True
    ).reshape(slots, size, -1)

    current = amplitudes.reshape(block)
    high = lax.reduce_precision(current, 8, 7)
    parts = jnp.stack([high, current - high], axis=0).astype(jnp.bfloat16)
    amp = parts[:, wanted].reshape(2, sources, 2, size, size)
    amp = amp.transpose(1, 3, 0, 2, 4).reshape(sources, size, 4 * size)
    amp = lax.all_to_all(amp, ("half", "near"), split_axis=0, concat_axis=0, tiled=True)

    all_domains = lax.all_gather(domains, ("half", "near"), tiled=True)
    slot = jnp.arange(slots, dtype=jnp.int32)
    slot_source = (slot // 2 % 2 + half) % 2 * near + slot // 4
    slot_entry = slot_source * 2 + slot % 2
    partner = slot_source * pairs + request[0, slot_entry]
    ids = orbital_ids(all_domains[partner], per_atom)[:, None, :]
    live = jnp.arange(depth, dtype=jnp.int32)[None, :] < degree[:, None]
    weight = jnp.where(live, coupling, jnp.zeros_like(coupling))
    hit = position[:, :, None] == slot_entry[None, None, :]
    slot_weight = jnp.sum(jnp.where(hit, weight[:, :, None], 0.0), axis=1)
    slot_weight = jnp.repeat(slot_weight, size, axis=1)
    slot_weight = slot_weight.reshape(pairs, slots // CHUNK, CHUNK * size).transpose(1, 0, 2)

    own_ids = orbital_ids(domains, per_atom)
    table = own_ids[:, :, None] == jnp.arange(columns, dtype=jnp.int32)[None, None, :]
    own = jnp.einsum(
        "sqz,szy->sqy", pnos, table.astype(jnp.bfloat16), preferred_element_type=jnp.float32
    ).astype(jnp.bfloat16).reshape(pairs * size, columns)

    denominator = virtual[:, :, None] + virtual[:, None, :] - occupied[:, None, None]
    integrals = integrals.reshape(block)
    half = half.reshape(1)
    cat, current, amp = first_sweep(
        half, wanted, own, partner_pnos, ids, slot_weight, amp, current, integrals, denominator
    )
    amp = lax.all_to_all(amp, ("half", "near"), split_axis=0, concat_axis=0, tiled=True)
    new, residual = second_sweep(
        half, cat, slot_weight, amp, current, integrals, denominator
    )
    return new, residual


def solution(mesh):
    count = mesh.shape["pair"]
    devices = mesh.devices.reshape(mesh.shape["frag"], 2, count // 2)
    split_mesh = Mesh(devices, ("frag", "half", "near"))
    rows = ("frag", "half", "near")
    return jax.shard_map(
        on_device,
        mesh=split_mesh,
        in_specs=(
            P(rows, None), P(rows, None), P(rows, None), P(rows), P(rows, None),
            P(rows), P(rows, None), P(rows, None), P(rows, None, None), P(rows, None),
        ),
        out_specs=(P(rows, None), P(rows, None)),
        check_vma=False,
    )
```

time: 234 us -> 115 us (0.49)
  local copies, waits for them, and re-layouts: 80.4 us -> 11.8 us
  matrix products: 52.5 us -> 1.08 us
  waiting for transfers between devices: 53.7 us -> 20.7 us
  blocking collectives: 13.6 us -> 44.1 us
  Pallas kernels: 0 us -> 13.1 us
  other arithmetic: 11.1 us -> 3.06 us
  loops' own time: 3.7 us -> 0 us
    gather x100 -> x6, local copies, waits for them, and re-layouts: 58.3 us -> 3.25 us  [the longest x2 1.16 us: on_device(): outgoing = jnp.stack([pnos[here], far_pnos[there]], axis=1)]
    dot_general x96 -> x1, matrix products: 52.5 us -> 1.08 us  [on_device(): jnp.einsum('sqz,szy->sqy', pnos, table.astype(jnp.bfloat16), preferred_el...]
    all_to_all x4 -> x3, waiting for transfers between devices: 53.7 us -> 12.7 us  [the longest x1 11.8 us: on_device(): lax.all_to_all(amp, ('half', 'near'), split_axis=0, concat_axis=0, tiled=...]
    all_gather x0 -> x1, blocking collectives: none -> 27.1 us  [on_device(): all_domains = lax.all_gather(domains, ('half', 'near'), tiled=True)]
    pallas_call x0 -> x2, Pallas kernels: none -> 13.1 us  [the longest x1 8.99 us: first_sweep(): pl.pallas_call(first_kernel, grid=(steps,), in_specs=[smem(), smem(), who...]
    ppermute x0 -> x2, waiting for transfers between devices: none -> 8.09 us  [the longest x1 8.09 us: on_device(): from_far = lax.ppermute(there, 'half', swap)]
    add x128 -> x6, local copies, waits for them, and re-layouts: 8.03 us -> 0.34 us  [orbital_ids(): atoms[:, :, None] * per_atom + offsets[None, None, :]]
    ppermute x0 -> x2, starting transfers between devices: none -> 5.25 us  [the longest x1 2.65 us: on_device(): far_pnos = lax.ppermute(pnos, 'half', swap)]
  transfers between devices with their start and end apart: 4 -> 5, of which waited for: 4 -> 3; matrix products, arithmetic and copies ran while one was open for 1% -> 10% of each run, Pallas kernels for 0% -> 0%
where the time goes in v1:
time: 115 us
  blocking collectives  44.1 us (38%)
  waiting for transfers between devices  20.7 us (18%)
  starting transfers between devices  20.2 us (18%)
  Pallas kernels  13.1 us (11%)
  local copies, waits for them, and re-layouts  11.8 us (10%)
  other arithmetic  3.06 us (3%)
    all_gather x1, blocking collectives, on_device(): all_domains = lax.all_gather(domains, ('half', 'near'), tiled=True)  27.1 us
    all_to_all x1, blocking collectives, on_device(): lax.all_to_all(amp, ('half', 'near'), split_axis=0, concat_axis=0, tiled=...  17.1 us
    all_to_all x1, waiting for transfers between devices, on_device(): lax.all_to_all(amp, ('half', 'near'), split_axis=0, concat_axis=0, tiled=...  11.8 us
    pallas_call x1, Pallas kernels, first_sweep(): pl.pallas_call(first_kernel, grid=(steps,), in_specs=[smem(), smem(), who...  8.99 us
    ppermute x1, waiting for transfers between devices, on_device(): from_far = lax.ppermute(there, 'half', swap)  8.09 us
    all_to_all x1, starting transfers between devices, on_device(): lax.all_to_all(amp, ('half', 'near'), split_axis=0, concat_axis=0, tiled=...  6.1 us
    all_to_all x1, starting transfers between devices, on_device(): lax.all_to_all(asked, 'near', split_axis=0, concat_axis=0, tiled=True)  5.26 us
    pallas_call x1, Pallas kernels, second_sweep(): pl.pallas_call(second_kernel, grid=(steps,), in_specs=[smem(), by_chunk((...  4.09 us
  transfers between devices with their start and end apart: 5, of which 3 were waited for; matrix products, arithmetic and copies ran while one was open for 10% of the time, Pallas kernels for 0%

profile of v1, /device:TPU:0, one launch (start us, length us, event | category | flops | bytes accessed | tf_op | source)
XLA Modules:
  0.0 115.0 jit_solution(14237899672526189317)
XLA Ops:
  0.6 0.5 broadcast.619
  1.1 1.3 %reduce.3 = s32[32]{0:T(128)S(1)} reduce(s32[1,32]{1,0:T(1,128)} %param.17, s32[]{:T(128)} %broadcast.619), dimensions={0}, to_apply=%param.17.reduce_sub_computation.3 | reduce | bytes 260 | tf_op args[7]
  2.6 0.6 copy.83
  3.2 5.3 %all-to-all-start = ((s32[8,2,2]{2,1,0:T(2,128)}), s32[8,2,2]{2,1,0:T(2,128)S(1)}, u32[]{:S(2)}, u32[]{:S(2)}) async-start(s32[8,2,2]{2,1,0:T(2,128)} %copy.83), calls=%async_computation | async-start | bytes 16384 | tf_op jit(solution)/shard_map/all_to_all | solution.py:223
  8.4 2.7 %collective-permute-start.1 = (bf16[8,64,256]{2,1,0:T(8,128)(2,1)}, bf16[8,64,256]{2,1,0:T(8,128)(2,1)S(1)}, u32[]{:S(2)}, u32[]{:S(2)}) collective-permute-start(bf16[8,64,256]{2,1,0:T(8,128)(2,1)} %param.18), channel_id=1, source_target_pairs={{0,8},{8,0},{1,9},{9,1},{2,10},{10,2},{3,11},{11,3},{4,12},{12,4},... | collective-permute-start | bytes 786440 | tf_op jit(solution)/shard_map/ppermute | solution.py:221
  11.1 1.0 reshape.444
  12.2 0.9 all-to-all-done
  13.2 2.6 %collective-permute-start = (s32[8,2]{0,1:T(2,128)S(1)}, s32[8,2]{0,1:T(2,128)S(1)}, u32[]{:S(2)}, u32[]{:S(2)}) collective-permute-start(s32[8,2]{0,1:T(2,128)S(1)} %bitcast.52), channel_id=1, source_target_pairs={{0,8},{8,0},{1,9},{9,1},{2,10},{10,2},{3,11},{11,3},{4,12},{12,4},... | collective-permute-start | bytes 200 | tf_op jit(solution)/shard_map/ppermute | solution.py:226
  15.9 8.1 %collective-permute-done = s32[8,2]{0,1:T(2,128)S(1)} collective-permute-done((s32[8,2]{0,1:T(2,128)S(1)}, s32[8,2]{0,1:T(2,128)S(1)}, u32[]{:S(2)}, u32[]{:S(2)}) %collective-permute-start) | collective-permute-done | bytes 96 | tf_op jit(solution)/shard_map/ppermute | solution.py:226
  24.3 0.7 gather_fusion.4
  25.0 1.1 copy.99
  26.1 1.5 %reshape.446 = bf16[16,64,256]{2,1,0:T(8,128)(2,1)} reshape(bf16[16,64,2,2,64]{4,3,2,1,0:T(2,128)(2,1)S(1)} %copy.99) | data formatting | bytes 1048576 | tf_op jit(solution)/shard_map/reshape | solution.py:240
  27.6 6.1 %all-to-all-start.2 = ((bf16[16,64,256]{2,1,0:T(8,128)(2,1)}), bf16[16,64,256]{2,1,0:T(8,128)(2,1)S(1)}, u32[]{:S(2)}, u32[]{:S(2)}) async-start(bf16[16,64,256]{2,1,0:T(8,128)(2,1)} %reshape.446), calls=%async_computation.2 | async-start | bytes 1048576 | tf_op jit(solution)/shard_map/all_to_all | solution.py:241
  34.1 0.6 gather_fusion
  34.8 0.6 gather_fusion.1
  35.4 1.1 pad_maximum_fusion
  36.4 11.8 %all-to-all-done.2.amp_ref = bf16[16,64,256]{2,1,0:T(8,128)(2,1)S(1)} async-done(((bf16[16,64,256]{2,1,0:T(8,128)(2,1)}), bf16[16,64,256]{2,1,0:T(8,128)(2,1)S(1)}, u32[]{:S(2)}, u32[]{:S(2)}) %all-to-all-start.2) | async-done | bytes 524320 | tf_op jit(solution)/shard_map/all_to_all | solution.py:241
  48.2 3.6 %all-to-all-start.1 = ((bf16[8,2,2,64,256]{4,3,2,1,0:T(8,128)(2,1)}), bf16[8,2,2,64,256]{4,3,2,1,0:T(8,128)(2,1)S(1)}, u32[]{:S(2)}, u32[]{:S(2)}) async-start(bf16[8,2,2,64,256]{4,3,2,1,0:T(8,128)(2,1)} %pad_maximum_fusion), calls=%async_computation.1 | async-start | bytes 2097152 | tf_op jit(solution)/shard_map/all_to_all | solution.py:232
  51.8 0.1 reshape.447.current_ref
  52.1 0.1 add.295
  52.3 0.1 select_reduce_fusion
  52.5 0.1 reshape_reshape.3
  52.6 0.1 reshape.448.integrals_ref
  52.7 27.1 %all_gather.3 = s32[128,16]{1,0:T(8,128)S(1)} all-gather(s32[8,16]{1,0:T(8,128)S(1)} %copy-done.6), channel_id=1, replica_groups=mesh['frag'=2,'half'=2,'near'=8] {'half','near'}, dimensions={0}, use_global_device_ids=true | all-gather | bytes 8704 | tf_op jit(solution)/shard_map/all_gather | solution.py:243
  79.8 0.1 add_subtract_fusion.denominator_ref
  79.9 1.1 fusion.2
  81.1 0.7 gather_fusion.2
  81.9 0.6 gather_fusion.3
  82.7 9.0 %first_sweep.1 = (bf16[4,8,128,512]{3,2,1,0:T(8,128)(2,1)}, f32[8,64,64]{2,1,0:T(8,128)S(1)}, bf16[16,64,256]{2,1,0:T(8,128)(2,1)S(1)}) custom-call(s32[1]{0:T(128)} %bitcast.half_ref, s32[32]{0:T(128)S(1)} %select_n.195.wanted_ref, bf16[512,512]{1,0:T(8,128)(2,1)S(1)} %bitcast.45, bf16[32,64,256]{2,1,0:T(8,128)(2,1)S(1)} %bitcast.42, ...), custom_call_target="tpu_custom_call" | custom-call | tf_op jit(solution)/shard_map/first_sweep/pallas_call | solution.py:148
  91.6 17.1 %all_to_all.20.amp_ref = bf16[16,64,256]{2,1,0:T(8,128)(2,1)S(1)} all-to-all(bf16[16,64,256]{2,1,0:T(8,128)(2,1)S(1)} %get-tuple-element.6), channel_id=1, replica_groups=mesh['frag'=2,'half'=2,'near'=8] {'half','near'}, dimensions={0} | all-to-all | bytes 1048576 | tf_op jit(solution)/shard_map/all_to_all | solution.py:268
  108.7 2.2 %copy-done = bf16[4,8,128,512]{3,2,1,0:T(8,128)(2,1)S(1)} copy-done((bf16[4,8,128,512]{3,2,1,0:T(8,128)(2,1)S(1)}, bf16[4,8,128,512]{3,2,1,0:T(8,128)(2,1)}, u32[]{:S(2)}) %copy-start) | copy-done | bytes 4194328
  110.9 4.1 %second_sweep.1 = (f32[8,4096]{1,0:T(8,128)}, f32[8,4096]{1,0:T(8,128)}) custom-call(s32[1]{0:T(128)} %bitcast.half_ref, bf16[4,8,128,512]{3,2,1,0:T(8,128)(2,1)S(1)} %copy-done, f32[4,8,512]{2,1,0:T(8,128)S(1)} %bitcast.44, bf16[16,64,256]{2,1,0:T(8,128)(2,1)S(1)} %all_to_all.20.amp_ref, f32[8,64,64]{2,1,0:T(8,128)S(1)} %get-tuple-element.7.current_ref, ...), custom_call_target="tpu_custom_call" | custom-call | tf_op jit(solution)/shard_map/second_sweep/pallas_call | solution.py:181
  (59 shorter events, 1.7 us)
Async XLA Ops:
  2.5 31.2 %copy-start.6 = (s32[8,16]{1,0:T(8,128)S(1)}, s32[8,16]{1,0:T(8,128)}, u32[]{:S(2)}) copy-start(s32[8,16]{1,0:T(8,128)} %param.19) | copy-start | bytes 1540
  3.2 9.9 %all-to-all-start = ((s32[8,2,2]{2,1,0:T(2,128)}), s32[8,2,2]{2,1,0:T(2,128)S(1)}, u32[]{:S(2)}, u32[]{:S(2)}) async-start(s32[8,2,2]{2,1,0:T(2,128)} %copy.83), calls=%async_computation | async-start | bytes 16384 | tf_op jit(solution)/shard_map/all_to_all | solution.py:223
  8.4 25.7 %copy-start.2 = (bf16[8,64,256]{2,1,0:T(8,128)(2,1)S(1)}, bf16[8,64,256]{2,1,0:T(8,128)(2,1)}, u32[]{:S(2)}) copy-start(bf16[8,64,256]{2,1,0:T(8,128)(2,1)} %param.18) | copy-start | bytes 786436
  8.4 26.3 %collective-permute-start.1 = (bf16[8,64,256]{2,1,0:T(8,128)(2,1)}, bf16[8,64,256]{2,1,0:T(8,128)(2,1)S(1)}, u32[]{:S(2)}, u32[]{:S(2)}) collective-permute-start(bf16[8,64,256]{2,1,0:T(8,128)(2,1)} %param.18), channel_id=1, source_target_pairs={{0,8},{8,0},{1,9},{9,1},{2,10},{10,2},{3,11},{11,3},{4,12},{12,4},... | collective-permute-start | bytes 786440 | tf_op jit(solution)/shard_map/ppermute | solution.py:221
  13.2 10.8 %collective-permute-start = (s32[8,2]{0,1:T(2,128)S(1)}, s32[8,2]{0,1:T(2,128)S(1)}, u32[]{:S(2)}, u32[]{:S(2)}) collective-permute-start(s32[8,2]{0,1:T(2,128)S(1)} %bitcast.52), channel_id=1, source_target_pairs={{0,8},{8,0},{1,9},{9,1},{2,10},{10,2},{3,11},{11,3},{4,12},{12,4},... | collective-permute-start | bytes 200 | tf_op jit(solution)/shard_map/ppermute | solution.py:226
  26.1 25.7 %copy-start.3 = (f32[8,4096]{1,0:T(8,128)S(1)}, f32[8,4096]{1,0:T(8,128)}, u32[]{:S(2)}) copy-start(f32[8,4096]{1,0:T(8,128)} %param.10) | copy-start | bytes 393220
  27.6 24.6 %copy-start.8 = (f32[8,16]{1,0:T(8,128)S(1)}, f32[8,16]{1,0:T(8,128)}, u32[]{:S(2)}) copy-start(f32[8,16]{1,0:T(8,128)} %param.14) | copy-start | bytes 1540
  27.6 24.6 %copy-start.10 = (s32[8]{0:T(128)S(1)}, s32[8]{0:T(128)}, u32[]{:S(2)}) copy-start(s32[8]{0:T(128)} %param.15) | copy-start | bytes 100
  27.6 24.6 %copy-start.7 = (s32[8,16]{1,0:T(8,128)S(1)}, s32[8,16]{1,0:T(8,128)}, u32[]{:S(2)}) copy-start(s32[8,16]{1,0:T(8,128)} %param.16) | copy-start | bytes 1540
  27.6 25.0 %copy-start.4 = (f32[8,4096]{1,0:T(8,128)S(1)}, f32[8,4096]{1,0:T(8,128)}, u32[]{:S(2)}) copy-start(f32[8,4096]{1,0:T(8,128)} %param.11) | copy-start | bytes 393220
  27.6 20.6 %all-to-all-start.2 = ((bf16[16,64,256]{2,1,0:T(8,128)(2,1)}), bf16[16,64,256]{2,1,0:T(8,128)(2,1)S(1)}, u32[]{:S(2)}, u32[]{:S(2)}) async-start(bf16[16,64,256]{2,1,0:T(8,128)(2,1)} %reshape.446), calls=%async_computation.2 | async-start | bytes 1048576 | tf_op jit(solution)/shard_map/all_to_all | solution.py:241
  33.7 46.0 %copy-start.5 = (f32[8,64]{1,0:T(8,128)S(1)}, f32[8,64]{1,0:T(8,128)}, u32[]{:S(2)}) copy-start(f32[8,64]{1,0:T(8,128)} %param.12) | copy-start | bytes 6148
  33.7 46.0 %copy-start.9 = (f32[8]{0:T(128)S(1)}, f32[8]{0:T(128)}, u32[]{:S(2)}) copy-start(f32[8]{0:T(128)} %param.13) | copy-start | bytes 100
  35.3 45.8 %copy-start.1 = (s32[1,32]{1,0:T(1,128)S(1)}, s32[1,32]{1,0:T(1,128)}, u32[]{:S(2)}) copy-start(s32[1,32]{1,0:T(1,128)} %param.17) | copy-start | bytes 388
  48.2 34.5 %all-to-all-start.1 = ((bf16[8,2,2,64,256]{4,3,2,1,0:T(8,128)(2,1)}), bf16[8,2,2,64,256]{4,3,2,1,0:T(8,128)(2,1)S(1)}, u32[]{:S(2)}, u32[]{:S(2)}) async-start(bf16[8,2,2,64,256]{4,3,2,1,0:T(8,128)(2,1)} %pad_maximum_fusion), calls=%async_computation.1 | async-start | bytes 2097152 | tf_op jit(solution)/shard_map/all_to_all | solution.py:232
  108.7 2.2 %copy-start = (bf16[4,8,128,512]{3,2,1,0:T(8,128)(2,1)S(1)}, bf16[4,8,128,512]{3,2,1,0:T(8,128)(2,1)}, u32[]{:S(2)}) copy-start(bf16[4,8,128,512]{3,2,1,0:T(8,128)(2,1)} %get-tuple-element.5.cat_ref) | copy-start | bytes 12582916

commit v2 on v1

v2 whole, which is shorter than its diff:
```python
import functools
import jax
import jax.numpy as jnp
from jax import lax
from jax.experimental import pallas as pl
from jax.experimental.pallas import tpu as pltpu
from jax.sharding import Mesh, PartitionSpec as P

ATOMS = 32
NEAR_STEP = 4
ATOM_ROWS = 16
VMEM_LIMIT = 48 * 1024 * 1024
NT = (((1,), (1,)), ((), ()))


def split(value):
    high = value.astype(jnp.bfloat16)
    low = (value - high.astype(jnp.float32)).astype(jnp.bfloat16)
    return high, low


def store_parts(value, even_ref, odd_ref, p):
    high, low = split(value)
    high, low = high.astype(jnp.float32), low.astype(jnp.float32)
    blank = jnp.zeros_like(high)
    even_ref[p] = jnp.concatenate([high, blank, low, blank], axis=1).astype(jnp.bfloat16)
    odd_ref[p] = jnp.concatenate([blank, high, blank, low], axis=1).astype(jnp.bfloat16)


def pack_kernel(
    column_ref, request_ref, pnos_ref, amp_ref, atoms_ref, out_ref, rows_ref, even_ref, odd_ref
):
    pairs, size, width = pnos_ref.shape
    for a in range(0, size, 2):
        both = amp_ref[:, a * size : (a + 2) * size]
        rows_ref[pl.ds(a, pairs, stride=size), :] = both[:, :size]
        rows_ref[pl.ds(a + 1, pairs, stride=size), :] = both[:, size:]
    for p in range(pairs):
        store_parts(rows_ref[p * size : (p + 1) * size, :], even_ref, odd_ref, p)
    first_row = lax.broadcasted_iota(jnp.int32, (ATOM_ROWS, width), 0) == 0

    def pack(n, carry):
        first = request_ref[n, 0, column_ref[0]]
        second = request_ref[n, 0, column_ref[0] + 1]
        out_ref[n, :size] = pnos_ref[first]
        out_ref[n, size : 2 * size] = pnos_ref[second]
        out_ref[n, 2 * size : 3 * size] = even_ref[first] + odd_ref[second]
        out_ref[n, 3 * size :] = jnp.where(
            first_row, atoms_ref[pl.ds(first, 1), :], atoms_ref[pl.ds(second, 1), :]
        ).astype(jnp.bfloat16)
        return carry

    lax.fori_loop(0, out_ref.shape[0], pack, 0)


def slot_weights(base, weight_ref, position_ref, slots, size):
    lane = lax.broadcasted_iota(jnp.int32, (1, slots * size), 1) // size + base
    total = jnp.zeros((weight_ref.shape[0], slots * size), jnp.float32)
    for c in range(weight_ref.shape[1]):
        hit = position_ref[:, c : c + 1] == lane
        total += jnp.where(hit, weight_ref[:, c : c + 1], 0.0)
    return total


def sweep_chunk(weights, amps, cat_ref, left_ref, acc_ref, before):
    pairs, rows2, lanes = cat_ref.shape
    size = rows2 // 2
    group = lax.broadcasted_iota(jnp.int32, (size, 4 * size), 1) // size
    even = (group % 2 == 0).astype(jnp.float32).astype(jnp.bfloat16)
    odd = (group % 2 == 1).astype(jnp.float32).astype(jnp.bfloat16)
    for j in range(lanes // (2 * size)):
        cols = slice(j * 2 * size, (j + 1) * 2 * size)
        amp = amps(j)
        first, second = amp * even, amp * odd
        right = jnp.concatenate([first, second, first, second], axis=0)
        high = cat_ref[:, :size, cols].reshape(pairs * size, 2 * size)
        low = cat_ref[:, size:, cols].reshape(pairs * size, 2 * size)
        both = jnp.dot(
            jnp.concatenate([high, low], axis=1), right, preferred_element_type=jnp.float32
        )
        left = (both[:, : 2 * size] + both[:, 2 * size :]).reshape(pairs, size, 2 * size)
        left = left * weights[:, cols].reshape(pairs, 1, 2 * size)
        left_high, left_low = split(left)
        left_ref[:, :size, cols] = left_high
        left_ref[:, size:, cols] = left_low
    for s in range(pairs):
        part = lax.dot_general(left_ref[s], cat_ref[s], NT, preferred_element_type=jnp.float32)
        acc_ref[s] = before(s) + part


def cross_chunk(own_ref, payload_ref, cat_ref, full_ref):
    columns = own_ref.shape[1]
    pairs, rows2, unused = cat_ref.shape
    size = rows2 // 2
    width = payload_ref.shape[2]
    row = lax.broadcasted_iota(jnp.int32, (columns, width), 0)
    column = lax.broadcasted_iota(jnp.int32, (1, width), 1)
    per_atom = columns // ATOMS
    for n in range(payload_ref.shape[0]):
        atoms = payload_ref[n, 3 * size :, :].astype(jnp.float32).astype(jnp.int32)
        for c in range(2):
            ids = atoms[c : c + 1, :] * per_atom + column % per_atom
            table = (row == ids).astype(jnp.float32).astype(jnp.bfloat16)
            start = (2 * n + c) * size
            full_ref[start : start + size, :] = lax.dot_general(
                payload_ref[n, c * size : (c + 1) * size, :], table, NT,
                preferred_element_type=jnp.float32,
            ).astype(jnp.bfloat16)
    cross = lax.dot_general(own_ref[...], full_ref[...], NT, preferred_element_type=jnp.float32)
    high, low = split(cross)
    cat_ref[:, :size, :] = high.reshape(pairs, size, -1)
    cat_ref[:, size:, :] = low.reshape(pairs, size, -1)


def coupled_of(acc):
    size = acc.shape[0] // 2
    rows = acc[:size] + acc[size:]
    return rows[:, :size] + rows[:, size:]


def near_chunk(base, own_ref, payload_ref, weight_ref, position_ref, cat_ref, full_ref, left_ref,
               acc_ref, before):
    size = cat_ref.shape[1] // 2
    slots = 2 * payload_ref.shape[0]
    cross_chunk(own_ref, payload_ref, cat_ref, full_ref)
    weights = slot_weights(
        base + pl.program_id(0) * slots, weight_ref, position_ref, slots, size
    )
    sweep_chunk(
        weights, lambda j: payload_ref[j, 2 * size : 3 * size, :], cat_ref, left_ref, acc_ref,
        before,
    )


def first_kernel(
    base_ref, own_ref, payload_ref, weight_ref, position_ref, cat_ref, out_ref, full_ref,
    left_ref, acc_ref,
):
    first = pl.program_id(0) == 0
    near_chunk(
        base_ref[0], own_ref, payload_ref, weight_ref, position_ref, cat_ref.at[0], full_ref,
        left_ref, acc_ref, lambda s: jnp.where(first, 0.0, acc_ref[s]),
    )

    @pl.when(pl.program_id(0) == pl.num_programs(0) - 1)
    def finish():
        out_ref[...] = acc_ref[...]


def first_end_kernel(
    base_ref, here_ref, there_ref, own_ref, payload_ref, weight_ref, position_ref, before_ref,
    current_ref, integrals_ref, denominator_ref, cat_ref, new_ref, send_ref, full_ref, left_ref,
    acc_ref, even_ref, odd_ref,
):
    pairs, size, unused = current_ref.shape
    near = here_ref.shape[0]
    first = pl.program_id(0) == 0
    near_chunk(
        base_ref[0], own_ref, payload_ref, weight_ref, position_ref, cat_ref.at[0], full_ref,
        left_ref, acc_ref, lambda s: jnp.where(first, before_ref[s], acc_ref[s]),
    )

    @pl.when(pl.program_id(0) == pl.num_programs(0) - 1)
    def finish():
        for s in range(pairs):
            denominator = denominator_ref[s]
            residual = integrals_ref[s] + denominator * current_ref[s] - coupled_of(acc_ref[s])
            new = current_ref[s] - residual / denominator
            new_ref[s] = new
            store_parts(new, even_ref, odd_ref, s)

        far_start = base_ref[0] // 2
        near_start = near - far_start
        column = base_ref[1]

        def pack(n, carry):
            for start, table_ref in ((near_start, here_ref), (far_start, there_ref)):
                first = table_ref[n, 0, column]
                second = table_ref[n, 0, column + 1]
                send_ref[start + n] = even_ref[first] + odd_ref[second]
            return carry

        lax.fori_loop(0, near, pack, 0)


def second_kernel(
    base_ref, near_cat_ref, far_cat_ref, weight_ref, position_ref, near_amp_ref, far_amp_ref,
    current_ref, integrals_ref, denominator_ref, new_ref, residual_ref, left_ref, acc_ref,
    new_rows_ref, residual_rows_ref,
):
    pairs, size, unused = current_ref.shape
    step = pl.program_id(0)
    slots = near_cat_ref.shape[3] // size
    first = step == 0
    parts = ((0, near_cat_ref, near_amp_ref), (1, far_cat_ref, far_amp_ref))
    for part, cat_ref, amp_ref in parts:
        weights = slot_weights(
            base_ref[part] + step * slots, weight_ref, position_ref, slots, size
        )
        if part == 0:
            before = lambda s: jnp.where(first, 0.0, acc_ref[s])
        else:
            before = lambda s: acc_ref[s]
        sweep_chunk(
            weights, lambda j: amp_ref[j], cat_ref.at[0], left_ref.at[part], acc_ref, before
        )

    @pl.when(step == pl.num_programs(0) - 1)
    def finish():
        for s in range(pairs):
            denominator = denominator_ref[s]
            residual = integrals_ref[s] + denominator * current_ref[s] - coupled_of(acc_ref[s])
            rows = slice(s * size, (s + 1) * size)
            residual_rows_ref[rows, :] = residual
            new_rows_ref[rows, :] = current_ref[s] - residual / denominator
        for rows_ref, out_ref in ((residual_rows_ref, residual_ref), (new_rows_ref, new_ref)):
            for a in range(0, size, 2):
                out_ref[:, a * size : (a + 2) * size] = jnp.concatenate(
                    [rows_ref[pl.ds(a + i, pairs, stride=size), :] for i in range(2)], axis=1
                )


def smem():
    return pl.BlockSpec(memory_space=pltpu.SMEM)


def whole(shape):
    return pl.BlockSpec(shape, lambda i, *refs: (0,) * len(shape))


def by_step(shape):
    return pl.BlockSpec(shape, lambda i, *refs: (i,) + (0,) * (len(shape) - 1))


def params():
    return pltpu.CompilerParams(
        dimension_semantics=("arbitrary",), vmem_limit_bytes=VMEM_LIMIT
    )


def pack_payload(column, requests, pnos, amplitudes, atoms):
    pairs, size, width = pnos.shape
    near = requests.shape[0]
    return pl.pallas_call(
        pack_kernel,
        in_specs=[smem(), smem()] + [pl.BlockSpec(memory_space=pltpu.VMEM)] * 3,
        out_specs=pl.BlockSpec(memory_space=pltpu.VMEM),
        out_shape=jax.ShapeDtypeStruct((near, 3 * size + ATOM_ROWS, width), jnp.bfloat16),
        scratch_shapes=[
            pltpu.VMEM((pairs * size, size), jnp.float32),
            pltpu.VMEM((pairs, size, 4 * size), jnp.bfloat16),
            pltpu.VMEM((pairs, size, 4 * size), jnp.bfloat16),
        ],
        compiler_params=pltpu.CompilerParams(vmem_limit_bytes=VMEM_LIMIT),
        name="pack_payload",
    )(column, requests, pnos, amplitudes, atoms)


def chunk_shapes(own, payload, pairs, size):
    near, rows, width = payload.shape
    lanes = 2 * NEAR_STEP * size
    cat = (near // NEAR_STEP, pairs, 2 * size, lanes)
    scratch = [
        pltpu.VMEM((lanes, own.shape[1]), jnp.bfloat16),
        pltpu.VMEM((pairs, 2 * size, lanes), jnp.bfloat16),
        pltpu.VMEM((pairs, 2 * size, 2 * size), jnp.float32),
    ]
    return cat, (NEAR_STEP, rows, width), (pairs, 2 * size, 2 * size), scratch


def first_sweep(base, own, payload, weight, position, size):
    pairs = weight.shape[0]
    cat, chunk, acc, scratch = chunk_shapes(own, payload, pairs, size)
    return pl.pallas_call(
        first_kernel,
        grid=(cat[0],),
        in_specs=[
            smem(), whole(own.shape), by_step(chunk), whole(weight.shape), whole(position.shape)
        ],
        out_specs=[by_step((1,) + cat[1:]), whole(acc)],
        out_shape=[
            jax.ShapeDtypeStruct(cat, jnp.bfloat16), jax.ShapeDtypeStruct(acc, jnp.float32)
        ],
        scratch_shapes=scratch,
        compiler_params=params(),
        name="first_sweep_near",
    )(base, own, payload, weight, position)


def first_sweep_end(
    base, here, there, own, payload, weight, position, before, current, integrals, denominator
):
    pairs, size, unused = current.shape
    cat, chunk, acc, scratch = chunk_shapes(own, payload, pairs, size)
    block = (pairs, size, size)
    parts = (pairs, size, 4 * size)
    send = (2 * here.shape[0],) + parts[1:]
    return pl.pallas_call(
        first_end_kernel,
        grid=(cat[0],),
        in_specs=[
            smem(), smem(), smem(), whole(own.shape), by_step(chunk), whole(weight.shape),
            whole(position.shape), whole(acc), whole(block), whole(block), whole(block),
        ],
        out_specs=[by_step((1,) + cat[1:]), whole(block), whole(send)],
        out_shape=[
            jax.ShapeDtypeStruct(cat, jnp.bfloat16),
            jax.ShapeDtypeStruct(block, jnp.float32),
            jax.ShapeDtypeStruct(send, jnp.bfloat16),
        ],
        scratch_shapes=scratch + [pltpu.VMEM(parts, jnp.bfloat16)] * 2,
        compiler_params=params(),
        name="first_sweep_far",
    )(base, here, there, own, payload, weight, position, before, current, integrals, denominator)


def second_sweep(
    base, near_cat, far_cat, weight, position, amp, current, integrals, denominator
):
    pairs, size, unused = current.shape
    steps, lanes = near_cat.shape[0], near_cat.shape[3]
    block = (pairs, size, size)
    flat = (pairs, size * size)
    cat = by_step((1,) + near_cat.shape[1:])
    amp_block = (NEAR_STEP,) + amp.shape[1:]
    grid_spec = pltpu.PrefetchScalarGridSpec(
        num_scalar_prefetch=1,
        grid=(steps,),
        in_specs=[
            cat, cat, whole(weight.shape), whole(position.shape),
            pl.BlockSpec(
                amp_block, lambda i, base: (base[0] // (2 * NEAR_STEP) + i, 0, 0)
            ),
            pl.BlockSpec(
                amp_block, lambda i, base: (base[1] // (2 * NEAR_STEP) + i, 0, 0)
            ),
            whole(block), whole(block), whole(block),
        ],
        out_specs=[whole(flat), whole(flat)],
        scratch_shapes=[
            pltpu.VMEM((2, pairs, 2 * size, lanes), jnp.bfloat16),
            pltpu.VMEM((pairs, 2 * size, 2 * size), jnp.float32),
            pltpu.VMEM((pairs * size, size), jnp.float32),
            pltpu.VMEM((pairs * size, size), jnp.float32),
        ],
    )
    return pl.pallas_call(
        second_kernel,
        grid_spec=grid_spec,
        out_shape=[jax.ShapeDtypeStruct(flat, jnp.float32)] * 2,
        compiler_params=params(),
        name="second_sweep",
    )(base, near_cat, far_cat, weight, position, amp, amp, current, integrals, denominator)


def on_device(
    amplitudes, integrals, virtual, occupied, coupling, degree, position, request, pnos, domains
):
    pairs = amplitudes.shape[0]
    size = virtual.shape[1]
    depth = coupling.shape[1]
    width = pnos.shape[2]
    per_atom = width // domains.shape[1]
    columns = ATOMS * per_atom
    slots = request.shape[1]
    near = slots // 4
    half = lax.axis_index("half").astype(jnp.int32)
    mine = lax.axis_index("near").astype(jnp.int32)
    swap = [(0, 1), (1, 0)]
    block = (pairs, size, size)

    far_pnos = lax.ppermute(pnos, "half", swap)
    far_amplitudes = lax.ppermute(amplitudes, "half", swap)
    atoms = jnp.repeat(domains, per_atom, axis=1)
    far_domains = lax.ppermute(domains, "half", swap)
    far_atoms = jnp.repeat(far_domains, per_atom, axis=1)
    here = jnp.broadcast_to(request[None], (near, 1, slots))
    here = lax.all_to_all(here, "near", split_axis=0, concat_axis=0, tiled=True)
    there = lax.ppermute(here, "half", swap)

    near_base = half * 2 * near
    far_base = (1 - half) * 2 * near
    near_column = near_base + 2 * mine
    far_column = far_base + 2 * mine
    outgoing = pack_payload(near_column.reshape(1), here, pnos, amplitudes, atoms.astype(jnp.float32))
    near_payload = lax.all_to_all(outgoing, "near", split_axis=0, concat_axis=0, tiled=True)
    outgoing = pack_payload(
        far_column.reshape(1), here, far_pnos, far_amplitudes, far_atoms.astype(jnp.float32)
    )
    far_payload = lax.all_to_all(outgoing, "near", split_axis=0, concat_axis=0, tiled=True)

    live = jnp.arange(depth, dtype=jnp.int32)[None, :] < degree[:, None]
    weight = jnp.where(live, coupling, jnp.zeros_like(coupling))

    own_ids = atoms * per_atom + jnp.arange(width, dtype=jnp.int32)[None, :] % per_atom
    table = own_ids[:, :, None] == jnp.arange(columns, dtype=jnp.int32)[None, None, :]
    own = jnp.einsum(
        "sqz,szy->sqy", pnos, table.astype(jnp.bfloat16), preferred_element_type=jnp.float32
    ).astype(jnp.bfloat16).reshape(pairs * size, columns)

    denominator = virtual[:, :, None] + virtual[:, None, :] - occupied[:, None, None]
    current = amplitudes.reshape(block)
    integrals = integrals.reshape(block)
    near_cat, before = first_sweep(
        near_base.reshape(1), own, near_payload, weight, position, size
    )
    far_cat, current, amp = first_sweep_end(
        jnp.stack([far_base, near_column]), here, there, own, far_payload, weight, position,
        before, current, integrals, denominator,
    )
    amp = lax.all_to_all(amp, ("half", "near"), split_axis=0, concat_axis=0, tiled=True)
    new, residual = second_sweep(
        jnp.stack([near_base, far_base]), near_cat, far_cat, weight, position, amp, current,
        integrals, denominator,
    )
    return new, residual


def solution(mesh):
    count = mesh.shape["pair"]
    devices = mesh.devices.reshape(mesh.shape["frag"], 2, count // 2)
    split_mesh = Mesh(devices, ("frag", "half", "near"))
    rows = ("frag", "half", "near")
    return jax.shard_map(
        on_device,
        mesh=split_mesh,
        in_specs=(
            P(rows, None), P(rows, None), P(rows, None), P(rows), P(rows, None),
            P(rows), P(rows, None), P(rows, None), P(rows, None, None), P(rows, None),
        ),
        out_specs=(P(rows, None), P(rows, None)),
        check_vma=False,
    )
```

time: 115 us -> 93.7 us (0.81)
  blocking collectives: 44.1 us -> 0 us
  waiting for transfers between devices: 20.7 us -> 34.4 us
  starting transfers between devices: 20.2 us -> 27.6 us
  Pallas kernels: 13.1 us -> 17.1 us
  local copies, waits for them, and re-layouts: 11.8 us -> 10.4 us
  other arithmetic: 3.06 us -> 1.71 us
    all_gather x1 -> x0, blocking collectives: 27.1 us -> none  [on_device(): all_domains = lax.all_gather(domains, ('half', 'near'), tiled=True)]
    all_to_all x1 -> x0, blocking collectives: 17.1 us -> none  [on_device(): lax.all_to_all(amp, ('half', 'near'), split_axis=0, concat_axis=0, tiled=...]
    all_to_all x1 -> x2, starting transfers between devices: 3.56 us -> 10.6 us  [on_device(): lax.all_to_all(outgoing, 'near', split_axis=0, concat_axis=0, tiled=True)]
    ppermute x1 -> x3, waiting for transfers between devices: 8.09 us -> 14.4 us  [the longest x1 13.1 us: on_device(): far_domains = lax.ppermute(domains, 'half', swap)]
    unnamed x23 -> x32, local copies, waits for them, and re-layouts: 2.75 us -> 8.38 us
    pallas_call x2 -> x5, Pallas kernels: 13.1 us -> 17.1 us  [the longest x1 5.42 us: first_sweep_end(): pl.pallas_call(first_end_kernel, grid=(cat[0],), in_specs=[smem(), smem()...]
    gather x6 -> x0, local copies, waits for them, and re-layouts: 3.25 us -> none  [the longest x2 1.16 us: on_device(): outgoing = jnp.stack([pnos[here], far_pnos[there]], axis=1)]
    all_to_all x1, waiting for transfers between devices: 0.89 us -> 3.63 us  [on_device(): here = lax.all_to_all(here, 'near', split_axis=0, concat_axis=0, tiled=True)]
  transfers between devices with their start and end apart: 5 -> 8, of which waited for: 3 -> 5; matrix products, arithmetic and copies ran while one was open for 10% -> 4% of each run, Pallas kernels for 0% -> 6%
where the time goes in v2:
time: 93.7 us; the launch traced here: 93.1 us
  waiting for transfers between devices  34.4 us (37%)
  starting transfers between devices  27.6 us (29%)
  Pallas kernels  17.1 us (18%)
  local copies, waits for them, and re-layouts  10.4 us (11%)
  other arithmetic  1.71 us (2%)
  matrix products  1.08 us (1%)
    all_to_all x1, waiting for transfers between devices, on_device(): lax.all_to_all(amp, ('half', 'near'), split_axis=0, concat_axis=0, tiled=...  14.4 us
    ppermute x1, waiting for transfers between devices, on_device(): far_domains = lax.ppermute(domains, 'half', swap)  13.1 us
    all_to_all x2, starting transfers between devices, on_device(): lax.all_to_all(outgoing, 'near', split_axis=0, concat_axis=0, tiled=True)  10.6 us
    unnamed x32, local copies, waits for them, and re-layouts  8.38 us
    pallas_call x1, Pallas kernels, first_sweep_end(): pl.pallas_call(first_end_kernel, grid=(cat[0],), in_specs=[smem(), smem()...  5.42 us
    all_to_all x1, starting transfers between devices, on_device(): here = lax.all_to_all(here, 'near', split_axis=0, concat_axis=0, tiled=True)  5.26 us
    pallas_call x1, Pallas kernels, second_sweep(): pl.pallas_call(second_kernel, grid_spec=grid_spec, out_shape=[jax.ShapeDt...  4.25 us
    all_to_all x1, starting transfers between devices, on_device(): lax.all_to_all(amp, ('half', 'near'), split_axis=0, concat_axis=0, tiled=...  4.16 us
  transfers between devices with their start and end apart: 8, of which 5 were waited for; matrix products, arithmetic and copies ran while one was open for 4% of the time, Pallas kernels for 6%

profile of v2, /device:TPU:0, one launch (start us, length us, event | category | flops | bytes accessed | tf_op | source)
XLA Modules:
  0.0 93.1 jit_solution(7011870691081478980)
XLA Ops:
  0.7 1.3 %broadcast_in_dim.14 = s32[8,1,32]{2,1,0:T(1,128)} broadcast(s32[32]{0:T(128)} %bitcast.11), dimensions={2} | broadcast | bytes 1152 | tf_op jit(solution)/shard_map/broadcast_in_dim | solution.py:377
  1.9 5.3 %all-to-all-start = ((s32[8,1,32]{2,1,0:T(1,128)}), s32[8,1,32]{2,1,0:T(1,128)S(1)}, u32[]{:S(2)}, u32[]{:S(2)}) async-start(s32[8,1,32]{2,1,0:T(1,128)} %broadcast_in_dim.14), calls=%async_computation | async-start | bytes 8192 | tf_op jit(solution)/shard_map/all_to_all | solution.py:378
  7.2 0.8 fusion.4
  8.1 3.6 %all-to-all-done.request_ref.here_ref = s32[8,1,32]{2,1,0:T(1,128)S(1)} async-done(((s32[8,1,32]{2,1,0:T(1,128)}), s32[8,1,32]{2,1,0:T(1,128)S(1)}, u32[]{:S(2)}, u32[]{:S(2)}) %all-to-all-start) | async-done | bytes 1056 | tf_op jit(solution)/shard_map/all_to_all | solution.py:378
  11.8 0.9 copy-done.4
  12.7 0.9 %copy-done.6 = bf16[8,64,256]{2,1,0:T(8,128)(2,1)S(1)} copy-done((bf16[8,64,256]{2,1,0:T(8,128)(2,1)S(1)}, bf16[8,64,256]{2,1,0:T(8,128)(2,1)}, u32[]{:S(2)}) %copy-start.6) | copy-done | bytes 262168
  13.6 2.0 %pack_payload.2 = bf16[8,208,256]{2,1,0:T(8,128)(2,1)} custom-call(s32[1]{0:T(128)} %bitcast.4.column_ref, s32[8,1,32]{2,1,0:T(1,128)S(1)} %all-to-all-done.request_ref.here_ref, bf16[8,64,256]{2,1,0:T(8,128)(2,1)S(1)} %copy-done.6, f32[8,4096]{1,0:T(8,128)S(1)} %copy-done.4, f32[8,256]{1,0:T(8,128)S(1)} %convert_element_type.20.atoms_ref), custom_call_target="tpu_custom_call" | custom-call | tf_op jit(solution)/shard_map/pack_payload/pallas_call | solution.py:244
  15.6 3.7 %all-to-all-start.1 = ((bf16[8,208,256]{2,1,0:T(8,128)(2,1)}), bf16[8,208,256]{2,1,0:T(8,128)(2,1)S(1)}, u32[]{:S(2)}, u32[]{:S(2)}) async-start(bf16[8,208,256]{2,1,0:T(8,128)(2,1)} %pack_payload.2), calls=%async_computation.1 | async-start | bytes 1703936 | tf_op jit(solution)/shard_map/all_to_all | solution.py:386
  19.3 2.7 %collective-permute-start.1 = (bf16[8,64,256]{2,1,0:T(8,128)(2,1)S(1)}, bf16[8,64,256]{2,1,0:T(8,128)(2,1)S(1)}, u32[]{:S(2)}, u32[]{:S(2)}) collective-permute-start(bf16[8,64,256]{2,1,0:T(8,128)(2,1)S(1)} %copy-done.7), channel_id=1, source_target_pairs={{0,8},{8,0},{1,9},{9,1},{2,10},{10,2},{3,11},{11,3},{4,12},{12,4},... | collective-permute-start | bytes 786440 | tf_op jit(solution)/shard_map/ppermute | solution.py:372
  22.0 0.3 collective-permute-start.2
  22.3 2.6 %collective-permute-start.3 = (s32[8,16]{1,0:T(8,128)S(1)}, s32[8,16]{1,0:T(8,128)S(1)}, u32[]{:S(2)}, u32[]{:S(2)}) collective-permute-start(s32[8,16]{1,0:T(8,128)S(1)} %copy-done.12), channel_id=1, source_target_pairs={{0,8},{8,0},{1,9},{9,1},{2,10},{10,2},{3,11},{11,3},{4,12},{12,4},... | collective-permute-start | bytes 1544 | tf_op jit(solution)/shard_map/ppermute | solution.py:375
  24.9 13.1 %collective-permute-done.3 = s32[8,16]{1,0:T(8,128)S(1)} collective-permute-done((s32[8,16]{1,0:T(8,128)S(1)}, s32[8,16]{1,0:T(8,128)S(1)}, u32[]{:S(2)}, u32[]{:S(2)}) %collective-permute-start.3) | collective-permute-done | bytes 544 | tf_op jit(solution)/shard_map/ppermute | solution.py:375
  38.3 2.0 %pack_payload.3 = bf16[8,208,256]{2,1,0:T(8,128)(2,1)} custom-call(s32[1]{0:T(128)} %bitcast.7.column_ref, s32[8,1,32]{2,1,0:T(1,128)S(1)} %all-to-all-done.request_ref.here_ref, bf16[8,64,256]{2,1,0:T(8,128)(2,1)S(1)} %collective-permute-done.1.pnos_ref, f32[8,4096]{1,0:T(8,128)S(1)} %collective-permute-done.2.amp_ref, ...), custom_call_target="tpu_custom_call" | custom-call | tf_op jit(solution)/shard_map/pack_payload/pallas_call | solution.py:244
  40.2 7.0 %all-to-all-start.2 = ((bf16[8,208,256]{2,1,0:T(8,128)(2,1)}), bf16[8,208,256]{2,1,0:T(8,128)(2,1)S(1)}, u32[]{:S(2)}, u32[]{:S(2)}) async-start(bf16[8,208,256]{2,1,0:T(8,128)(2,1)} %pack_payload.3), calls=%async_computation.2 | async-start | bytes 1703936 | tf_op jit(solution)/shard_map/all_to_all | solution.py:390
  47.5 0.1 add_subtract_fusion.denominator_ref
  47.6 1.1 %fusion.2 = bf16[8,512,64]{1,2,0:T(8,128)(2,1)S(1)} fusion(bf16[8,64,256]{2,1,0:T(8,128)(2,1)S(1)} %copy-done.7, s32[8,256]{1,0:T(8,128)S(1)} %broadcast_add_fusion), kind=kOutput, calls=%fused_computation.3 | convolution fusion | flops 135528448 | bytes 794624 | tf_op jit(solution)/shard_map/sqz,szy->sqy/dot_general | solution.py:397
  48.7 1.9 %collective-permute-start = (s32[8,1,32]{2,1,0:T(1,128)S(1)}, s32[8,1,32]{2,1,0:T(1,128)S(1)}, u32[]{:S(2)}, u32[]{:S(2)}) collective-permute-start(s32[8,1,32]{2,1,0:T(1,128)S(1)} %all-to-all-done.request_ref.here_ref), channel_id=1, source_target_pairs={{0,8},{8,0},{1,9},{9,1},{2,10},{10,2},{3,11},{11,3},{4,12},{12,4},... | collective-permute-start | bytes 3080 | tf_op jit(solution)/shard_map/ppermute | solution.py:379
  50.7 0.7 pad_add_fusion.1.base_ref
  51.3 0.1 reshape.69.current_ref
  51.4 0.1 reshape.70.integrals_ref
  51.6 3.5 %first_sweep_near.1 = (bf16[2,8,128,512]{3,2,1,0:T(8,128)(2,1)S(1)}, f32[8,128,128]{2,1,0:T(8,128)S(1)}) custom-call(s32[1]{0:T(128)} %bitcast.base_ref, bf16[512,512]{1,0:T(8,128)(2,1)S(1)} %bitcast.9, bf16[8,208,256]{2,1,0:T(8,128)(2,1)S(1)} %all-to-all-done.1.payload_ref, f32[8,16]{1,0:T(8,128)S(1)} %fusion.3.weight_ref, s32[8,16]{1,0:T(8,128)S(1)} %copy-done.8), custom_call_target="tpu_custom_call" | custom-call | tf_op jit(solution)/shard_map/first_sweep_near/pallas_call | solution.py:274
  55.1 1.3 %copy-done = bf16[2,8,128,512]{3,2,1,0:T(8,128)(2,1)} copy-done((bf16[2,8,128,512]{3,2,1,0:T(8,128)(2,1)}, bf16[2,8,128,512]{3,2,1,0:T(8,128)(2,1)S(1)}, u32[]{:S(2)}) %copy-start) | copy-done | bytes 2097176
  56.4 1.2 %collective-permute-done.there_ref = s32[8,1,32]{2,1,0:T(1,128)S(1)} collective-permute-done((s32[8,1,32]{2,1,0:T(1,128)S(1)}, s32[8,1,32]{2,1,0:T(1,128)S(1)}, u32[]{:S(2)}, u32[]{:S(2)}) %collective-permute-start) | collective-permute-done | bytes 1056 | tf_op jit(solution)/shard_map/ppermute | solution.py:379
  57.6 2.0 %all-to-all-done.2.payload_ref = bf16[8,208,256]{2,1,0:T(8,128)(2,1)S(1)} async-done(((bf16[8,208,256]{2,1,0:T(8,128)(2,1)}), bf16[8,208,256]{2,1,0:T(8,128)(2,1)S(1)}, u32[]{:S(2)}, u32[]{:S(2)}) %all-to-all-start.2) | async-done | bytes 852000 | tf_op jit(solution)/shard_map/all_to_all | solution.py:390
  59.7 0.7 copy-done.9
  60.3 5.4 %first_sweep_far.1 = (bf16[2,8,128,512]{3,2,1,0:T(8,128)(2,1)S(1)}, f32[8,64,64]{2,1,0:T(8,128)S(1)}, bf16[16,64,256]{2,1,0:T(8,128)(2,1)}) custom-call(s32[2]{0:T(128)S(1)} %copy-done.9, s32[8,1,32]{2,1,0:T(1,128)S(1)} %all-to-all-done.request_ref.here_ref, s32[8,1,32]{2,1,0:T(1,128)S(1)} %collective-permute-done.there_ref, bf16[512,512]{1,0:T(8,128)(2,1)S(1)} %bitcast.10, ...), custom_call_target="tpu_custom_call" | custom-call | tf_op jit(solution)/shard_map/first_sweep_far/pallas_call | solution.py:298
  65.7 1.3 %copy-done.2 = bf16[2,8,128,512]{3,2,1,0:T(8,128)(2,1)} copy-done((bf16[2,8,128,512]{3,2,1,0:T(8,128)(2,1)}, bf16[2,8,128,512]{3,2,1,0:T(8,128)(2,1)S(1)}, u32[]{:S(2)}) %copy-start.2) | copy-done | bytes 2097176
  67.0 4.2 %all-to-all-start.3 = ((bf16[16,64,256]{2,1,0:T(8,128)(2,1)}), bf16[16,64,256]{2,1,0:T(8,128)(2,1)S(1)}, u32[]{:S(2)}, u32[]{:S(2)}) async-start(bf16[16,64,256]{2,1,0:T(8,128)(2,1)} %get-tuple-element.10), calls=%async_computation.3 | async-start | bytes 1048576 | tf_op jit(solution)/shard_map/all_to_all | solution.py:411
  71.3 14.4 %all-to-all-done.3.near_amp_ref.far_amp_ref = bf16[16,64,256]{2,1,0:T(8,128)(2,1)S(1)} async-done(((bf16[16,64,256]{2,1,0:T(8,128)(2,1)}), bf16[16,64,256]{2,1,0:T(8,128)(2,1)S(1)}, u32[]{:S(2)}, u32[]{:S(2)}) %all-to-all-start.3) | async-done | bytes 524320 | tf_op jit(solution)/shard_map/all_to_all | solution.py:411
  85.7 1.6 %copy-done.1 = bf16[2,8,128,512]{3,2,1,0:T(8,128)(2,1)S(1)} copy-done((bf16[2,8,128,512]{3,2,1,0:T(8,128)(2,1)S(1)}, bf16[2,8,128,512]{3,2,1,0:T(8,128)(2,1)}, u32[]{:S(2)}) %copy-start.1) | copy-done | bytes 2097176
  87.3 1.6 %copy-done.3 = bf16[2,8,128,512]{3,2,1,0:T(8,128)(2,1)S(1)} copy-done((bf16[2,8,128,512]{3,2,1,0:T(8,128)(2,1)S(1)}, bf16[2,8,128,512]{3,2,1,0:T(8,128)(2,1)}, u32[]{:S(2)}) %copy-start.3) | copy-done | bytes 2097176
  88.9 4.2 %second_sweep.1 = (f32[8,4096]{1,0:T(8,128)}, f32[8,4096]{1,0:T(8,128)}) custom-call(s32[2]{0:T(128)S(1)} %pad_add_fusion.base_ref, bf16[2,8,128,512]{3,2,1,0:T(8,128)(2,1)S(1)} %copy-done.1, bf16[2,8,128,512]{3,2,1,0:T(8,128)(2,1)S(1)} %copy-done.3, f32[8,16]{1,0:T(8,128)S(1)} %fusion.3.weight_ref, s32[8,16]{1,0:T(8,128)S(1)} %copy-done.8, ...), custom_call_target="tpu_custom_call" | custom-call | tf_op jit(solution)/shard_map/second_sweep/pallas_call | solution.py:347
  (39 shorter events, 0.7 us)
Async XLA Ops:
  0.6 21.7 %copy-start.12 = (s32[8,16]{1,0:T(8,128)S(1)}, s32[8,16]{1,0:T(8,128)}, u32[]{:S(2)}) copy-start(s32[8,16]{1,0:T(8,128)} %param.19) | copy-start | bytes 1540
  0.6 21.4 %copy-start.5 = (f32[8,4096]{1,0:T(8,128)S(1)}, f32[8,4096]{1,0:T(8,128)}, u32[]{:S(2)}) copy-start(f32[8,4096]{1,0:T(8,128)} %amp_ref.1) | copy-start | bytes 393220
  1.9 9.8 %all-to-all-start = ((s32[8,1,32]{2,1,0:T(1,128)}), s32[8,1,32]{2,1,0:T(1,128)S(1)}, u32[]{:S(2)}, u32[]{:S(2)}) async-start(s32[8,1,32]{2,1,0:T(1,128)} %broadcast_in_dim.14), calls=%async_computation | async-start | bytes 8192 | tf_op jit(solution)/shard_map/all_to_all | solution.py:378
  11.8 0.9 copy-start.4
  12.7 0.9 %copy-start.6 = (bf16[8,64,256]{2,1,0:T(8,128)(2,1)S(1)}, bf16[8,64,256]{2,1,0:T(8,128)(2,1)}, u32[]{:S(2)}) copy-start(bf16[8,64,256]{2,1,0:T(8,128)(2,1)} %pnos_ref.1) | copy-start | bytes 786436
  13.6 5.7 %copy-start.7 = (bf16[8,64,256]{2,1,0:T(8,128)(2,1)S(1)}, bf16[8,64,256]{2,1,0:T(8,128)(2,1)}, u32[]{:S(2)}) copy-start(bf16[8,64,256]{2,1,0:T(8,128)(2,1)} %pnos_ref.1) | copy-start | bytes 786436
  15.6 31.8 %copy-start.13 = (f32[8,16]{1,0:T(8,128)S(1)}, f32[8,16]{1,0:T(8,128)}, u32[]{:S(2)}) copy-start(f32[8,16]{1,0:T(8,128)} %param.14) | copy-start | bytes 1540
  15.6 31.8 %copy-start.15 = (s32[8]{0:T(128)S(1)}, s32[8]{0:T(128)}, u32[]{:S(2)}) copy-start(s32[8]{0:T(128)} %param.15) | copy-start | bytes 100
  15.6 31.9 %copy-start.11 = (f32[8,64]{1,0:T(8,128)S(1)}, f32[8,64]{1,0:T(8,128)}, u32[]{:S(2)}) copy-start(f32[8,64]{1,0:T(8,128)} %param.12) | copy-start | bytes 6148
  15.6 31.9 %copy-start.14 = (f32[8]{0:T(128)S(1)}, f32[8]{0:T(128)}, u32[]{:S(2)}) copy-start(f32[8]{0:T(128)} %param.13) | copy-start | bytes 100
  15.6 24.6 %all-to-all-start.1 = ((bf16[8,208,256]{2,1,0:T(8,128)(2,1)}), bf16[8,208,256]{2,1,0:T(8,128)(2,1)S(1)}, u32[]{:S(2)}, u32[]{:S(2)}) async-start(bf16[8,208,256]{2,1,0:T(8,128)(2,1)} %pack_payload.2), calls=%async_computation.1 | async-start | bytes 1703936 | tf_op jit(solution)/shard_map/all_to_all | solution.py:386
  19.3 18.9 %collective-permute-start.1 = (bf16[8,64,256]{2,1,0:T(8,128)(2,1)S(1)}, bf16[8,64,256]{2,1,0:T(8,128)(2,1)S(1)}, u32[]{:S(2)}, u32[]{:S(2)}) collective-permute-start(bf16[8,64,256]{2,1,0:T(8,128)(2,1)S(1)} %copy-done.7), channel_id=1, source_target_pairs={{0,8},{8,0},{1,9},{9,1},{2,10},{10,2},{3,11},{11,3},{4,12},{12,4},... | collective-permute-start | bytes 786440 | tf_op jit(solution)/shard_map/ppermute | solution.py:372
  22.0 16.3 %collective-permute-start.2 = (f32[8,4096]{1,0:T(8,128)S(1)}, f32[8,4096]{1,0:T(8,128)S(1)}, u32[]{:S(2)}, u32[]{:S(2)}) collective-permute-start(f32[8,4096]{1,0:T(8,128)S(1)} %copy-done.5), channel_id=1, source_target_pairs={{0,8},{8,0},{1,9},{9,1},{2,10},{10,2},{3,11},{11,3},{4,12},{12,4},... | collective-permute-start | bytes 393224 | tf_op jit(solution)/shard_map/ppermute | solution.py:373
  22.3 15.7 %collective-permute-start.3 = (s32[8,16]{1,0:T(8,128)S(1)}, s32[8,16]{1,0:T(8,128)S(1)}, u32[]{:S(2)}, u32[]{:S(2)}) collective-permute-start(s32[8,16]{1,0:T(8,128)S(1)} %copy-done.12), channel_id=1, source_target_pairs={{0,8},{8,0},{1,9},{9,1},{2,10},{10,2},{3,11},{11,3},{4,12},{12,4},... | collective-permute-start | bytes 1544 | tf_op jit(solution)/shard_map/ppermute | solution.py:375
  40.2 11.2 %copy-start.10 = (f32[8,4096]{1,0:T(8,128)S(1)}, f32[8,4096]{1,0:T(8,128)}, u32[]{:S(2)}) copy-start(f32[8,4096]{1,0:T(8,128)} %param.11) | copy-start | bytes 393220
  40.2 19.4 %all-to-all-start.2 = ((bf16[8,208,256]{2,1,0:T(8,128)(2,1)}), bf16[8,208,256]{2,1,0:T(8,128)(2,1)S(1)}, u32[]{:S(2)}, u32[]{:S(2)}) async-start(bf16[8,208,256]{2,1,0:T(8,128)(2,1)} %pack_payload.3), calls=%async_computation.2 | async-start | bytes 1703936 | tf_op jit(solution)/shard_map/all_to_all | solution.py:390
  47.2 4.3 %copy-start.8 = (s32[8,16]{1,0:T(8,128)S(1)}, s32[8,16]{1,0:T(8,128)}, u32[]{:S(2)}) copy-start(s32[8,16]{1,0:T(8,128)} %position_ref.5) | copy-start | bytes 1540
  48.7 8.9 %collective-permute-start = (s32[8,1,32]{2,1,0:T(1,128)S(1)}, s32[8,1,32]{2,1,0:T(1,128)S(1)}, u32[]{:S(2)}, u32[]{:S(2)}) collective-permute-start(s32[8,1,32]{2,1,0:T(1,128)S(1)} %all-to-all-done.request_ref.here_ref), channel_id=1, source_target_pairs={{0,8},{8,0},{1,9},{9,1},{2,10},{10,2},{3,11},{11,3},{4,12},{12,4},... | collective-permute-start | bytes 3080 | tf_op jit(solution)/shard_map/ppermute | solution.py:379
  55.1 1.4 %copy-start = (bf16[2,8,128,512]{3,2,1,0:T(8,128)(2,1)}, bf16[2,8,128,512]{3,2,1,0:T(8,128)(2,1)S(1)}, u32[]{:S(2)}) copy-start(bf16[2,8,128,512]{3,2,1,0:T(8,128)(2,1)S(1)} %get-tuple-element.7.near_cat_ref) | copy-start | bytes 6291460
  59.6 0.7 copy-start.9
  65.7 1.3 %copy-start.2 = (bf16[2,8,128,512]{3,2,1,0:T(8,128)(2,1)}, bf16[2,8,128,512]{3,2,1,0:T(8,128)(2,1)S(1)}, u32[]{:S(2)}) copy-start(bf16[2,8,128,512]{3,2,1,0:T(8,128)(2,1)S(1)} %get-tuple-element.9.far_cat_ref) | copy-start | bytes 6291460
  67.0 18.6 %all-to-all-start.3 = ((bf16[16,64,256]{2,1,0:T(8,128)(2,1)}), bf16[16,64,256]{2,1,0:T(8,128)(2,1)S(1)}, u32[]{:S(2)}, u32[]{:S(2)}) async-start(bf16[16,64,256]{2,1,0:T(8,128)(2,1)} %get-tuple-element.10), calls=%async_computation.3 | async-start | bytes 1048576 | tf_op jit(solution)/shard_map/all_to_all | solution.py:411
  85.7 1.6 %copy-start.1 = (bf16[2,8,128,512]{3,2,1,0:T(8,128)(2,1)S(1)}, bf16[2,8,128,512]{3,2,1,0:T(8,128)(2,1)}, u32[]{:S(2)}) copy-start(bf16[2,8,128,512]{3,2,1,0:T(8,128)(2,1)} %copy-done) | copy-start | bytes 6291460
  87.3 1.6 %copy-start.3 = (bf16[2,8,128,512]{3,2,1,0:T(8,128)(2,1)S(1)}, bf16[2,8,128,512]{3,2,1,0:T(8,128)(2,1)}, u32[]{:S(2)}) copy-start(bf16[2,8,128,512]{3,2,1,0:T(8,128)(2,1)} %copy-done.2) | copy-start | bytes 6291460

commit v3 on v2

v3 whole, which is shorter than its diff:
```python
import functools
import jax
import jax.numpy as jnp
from jax import lax
from jax.experimental import pallas as pl
from jax.experimental.pallas import tpu as pltpu
from jax.sharding import Mesh, PartitionSpec as P

ATOMS = 32
ONE_STEP = 8
NEAR_STEP = 4
CUTS = 4
CODE_TOP = 32767.0
CODE_ROWS = 16
SMALLEST = 2.0**-100
VMEM_LIMIT = 24 * 1024 * 1024
NT = (((1,), (1,)), ((), ()))


def split(value):
    high = value.astype(jnp.bfloat16)
    low = (value - high.astype(jnp.float32)).astype(jnp.bfloat16)
    return high, low


def store_parts(value, even_ref, odd_ref, p):
    high, low = split(value)
    high, low = high.astype(jnp.float32), low.astype(jnp.float32)
    blank = jnp.zeros_like(high)
    even_ref[p] = jnp.concatenate([high, blank, low, blank], axis=1).astype(jnp.bfloat16)
    odd_ref[p] = jnp.concatenate([blank, high, blank, low], axis=1).astype(jnp.bfloat16)


def store_codes(value, even_ref, odd_ref, p):
    size = value.shape[0]
    top = jnp.maximum(jnp.max(jnp.abs(value), axis=0, keepdims=True), SMALLEST)
    eighths = jnp.ceil(jnp.log2(top) * 8.0)
    codes = jnp.clip(jnp.round(value * (CODE_TOP / scale_of(eighths))), -CODE_TOP, CODE_TOP)
    rows = jnp.concatenate([codes, jnp.broadcast_to(eighths, (CODE_ROWS, size))], axis=0)
    blank = jnp.zeros_like(rows)
    for ref, parts in ((even_ref, [rows, blank]), (odd_ref, [blank, rows])):
        ref[p] = jnp.concatenate(parts, axis=1).astype(jnp.int32).astype(jnp.int16)


def scale_of(eighths):
    return jnp.exp2(eighths * 0.125)


def parts_of_codes(codes):
    rows = codes.astype(jnp.int32).astype(jnp.float32)
    size = rows.shape[0] - CODE_ROWS
    scale = scale_of(rows[size : size + 1, :]) * (1.0 / CODE_TOP)
    return jnp.concatenate(split(rows[:size, :] * scale), axis=1)


def to_blocks(flat_ref, rows_ref, size):
    pairs = flat_ref.shape[0]
    for a in range(0, size, 2):
        both = flat_ref[:, a * size : (a + 2) * size]
        rows_ref[pl.ds(a, pairs, stride=size), :] = both[:, :size]
        rows_ref[pl.ds(a + 1, pairs, stride=size), :] = both[:, size:]


def atoms_of_columns(domains, width):
    count = domains.shape[1]
    entry = lax.broadcasted_iota(jnp.int32, (count, width), 0)
    column = lax.broadcasted_iota(jnp.int32, (count, width), 1)
    spread = (entry == column // (width // count)).astype(jnp.float32).astype(jnp.bfloat16)
    atoms = domains.astype(jnp.float32).astype(jnp.bfloat16)
    return jnp.dot(atoms, spread, preferred_element_type=jnp.float32)


def column_table(atoms, columns):
    width = atoms.shape[1]
    per_atom = columns // ATOMS
    row = lax.broadcasted_iota(jnp.int32, (columns, width), 0)
    column = lax.broadcasted_iota(jnp.int32, (1, width), 1)
    ids = atoms.astype(jnp.int32) * per_atom + column % per_atom
    return (row == ids).astype(jnp.float32).astype(jnp.bfloat16)


def prepare_kernel(
    pnos_ref, domains_ref, amp_ref, integrals_ref, own_ref, current_ref, blocks_ref, atoms_ref
):
    pairs, size, width = pnos_ref.shape
    columns = own_ref.shape[1]
    to_blocks(amp_ref, current_ref, size)
    to_blocks(integrals_ref, blocks_ref, size)
    atoms_ref[...] = atoms_of_columns(domains_ref[...], width)
    for p in range(pairs):
        own_ref[p * size : (p + 1) * size, :] = lax.dot_general(
            pnos_ref[p], column_table(atoms_ref[p : p + 1, :], columns), NT,
            preferred_element_type=jnp.float32,
        ).astype(jnp.bfloat16)


def pack_kernel(
    column_ref, table_ref, pnos_ref, amp_ref, out_ref, rows_ref, even_ref, odd_ref
):
    pairs, size, unused = pnos_ref.shape
    to_blocks(amp_ref, rows_ref, size)
    for p in range(pairs):
        store_parts(rows_ref[p * size : (p + 1) * size, :], even_ref, odd_ref, p)

    def pack(n, carry):
        first = table_ref[n, 0, column_ref[0]]
        second = table_ref[n, 0, column_ref[0] + 1]
        out_ref[n, :size] = pnos_ref[first]
        out_ref[n, size : 2 * size] = pnos_ref[second]
        out_ref[n, 2 * size :] = even_ref[first] + odd_ref[second]
        return carry

    lax.fori_loop(0, out_ref.shape[0], pack, 0)


def slot_weights(base, weight_ref, position_ref, slots, size):
    lane = lax.broadcasted_iota(jnp.int32, (1, slots * size), 1) // size + base
    total = jnp.zeros((weight_ref.shape[0], slots * size), jnp.float32)
    for c in range(weight_ref.shape[1]):
        hit = position_ref[:, c : c + 1] == lane
        total += jnp.where(hit, weight_ref[:, c : c + 1], 0.0)
    return total


def sweep_chunk(weights, amps, cat_ref, left_ref, acc_ref, before, ready=lambda j: None):
    pairs, rows2, lanes = cat_ref.shape
    size = rows2 // 2
    group = lax.broadcasted_iota(jnp.int32, (size, 4 * size), 1) // size
    even = (group % 2 == 0).astype(jnp.float32).astype(jnp.bfloat16)
    odd = (group % 2 == 1).astype(jnp.float32).astype(jnp.bfloat16)
    for j in range(lanes // (2 * size)):
        cols = slice(j * 2 * size, (j + 1) * 2 * size)
        ready(j)
        amp = amps(j)
        first, second = amp * even, amp * odd
        right = jnp.concatenate([first, second, first, second], axis=0)
        high = cat_ref[:, :size, cols].reshape(pairs * size, 2 * size)
        low = cat_ref[:, size:, cols].reshape(pairs * size, 2 * size)
        both = jnp.dot(
            jnp.concatenate([high, low], axis=1), right, preferred_element_type=jnp.float32
        )
        left = (both[:, : 2 * size] + both[:, 2 * size :]).reshape(pairs, size, 2 * size)
        left = left * weights[:, cols].reshape(pairs, 1, 2 * size)
        left_high, left_low = split(left)
        left_ref[:, :size, cols] = left_high
        left_ref[:, size:, cols] = left_low
    for s in range(pairs):
        part = lax.dot_general(left_ref[s], cat_ref[s], NT, preferred_element_type=jnp.float32)
        acc_ref[s] = before(s) + part


def cross_chunk(slot_atoms, own_ready, own_ref, payload_ref, cat_ref, full_ref):
    columns = own_ref.shape[1]
    pairs, rows2, unused = cat_ref.shape
    size = rows2 // 2
    for k in range(2 * payload_ref.shape[0]):
        n, c = k // 2, k % 2
        full_ref[k * size : (k + 1) * size, :] = lax.dot_general(
            payload_ref[n, c * size : (c + 1) * size, :], column_table(slot_atoms(k), columns),
            NT, preferred_element_type=jnp.float32,
        ).astype(jnp.bfloat16)
    own_ready()
    cross = lax.dot_general(own_ref[...], full_ref[...], NT, preferred_element_type=jnp.float32)
    high, low = split(cross)
    cat_ref[:, :size, :] = high.reshape(pairs, size, -1)
    cat_ref[:, size:, :] = low.reshape(pairs, size, -1)


def coupled_of(acc):
    size = acc.shape[0] // 2
    rows = acc[:size] + acc[size:]
    return rows[:, :size] + rows[:, size:]


def near_chunk(
    base, request_ref, table_ref, own_hbm, payload_ref, weight_ref, position_ref, cat_hbm,
    own_ref, cat_ref, full_ref, left_ref, acc_ref, sem_ref,
):
    size = cat_ref.shape[1] // 2
    width = payload_ref.shape[2]
    pairs = weight_ref.shape[0]
    slots = 2 * payload_ref.shape[0]
    step = pl.program_id(0)
    entries = (table_ref.shape[2] - request_ref.shape[1]) // pairs
    own_copy = pltpu.make_async_copy(own_hbm, own_ref, sem_ref.at[0])

    @pl.when(step == 0)
    def fetch():
        own_copy.start()

    def own_ready():
        @pl.when(step == 0)
        def wait():
            own_copy.wait()

    entry = lax.broadcasted_iota(jnp.int32, (1, width), 1) // (width // entries)

    def slot_atoms(k):
        slot = step * slots + k
        start = request_ref.shape[1] + request_ref[0, base + slot] * entries
        atoms = jnp.zeros((1, width), jnp.int32)
        for a in range(entries):
            atoms = jnp.where(entry == a, table_ref[slot // 2, 0, start + a], atoms)
        return atoms

    cross_chunk(slot_atoms, own_ready, own_ref, payload_ref, cat_ref, full_ref)
    cat_copy = pltpu.make_async_copy(cat_ref, cat_hbm.at[step], sem_ref.at[1])
    cat_copy.start()
    weights = slot_weights(base + step * slots, weight_ref, position_ref, slots, size)
    sweep_chunk(
        weights, lambda j: payload_ref[j, 2 * size :, :], cat_ref, left_ref, acc_ref,
        lambda s: jnp.where(step == 0, 0.0, acc_ref[s]),
    )
    cat_copy.wait()


def first_kernel(
    base_ref, request_ref, table_ref, own_hbm, payload_ref, weight_ref, position_ref, cat_hbm,
    acc_hbm, own_ref, cat_ref, full_ref, left_ref, acc_ref, sem_ref,
):
    near_chunk(
        base_ref[0], request_ref, table_ref, own_hbm, payload_ref, weight_ref, position_ref,
        cat_hbm, own_ref, cat_ref, full_ref, left_ref, acc_ref, sem_ref,
    )

    @pl.when(pl.program_id(0) == pl.num_programs(0) - 1)
    def finish():
        copy = pltpu.make_async_copy(acc_ref, acc_hbm, sem_ref.at[2])
        copy.start()
        copy.wait()


def first_end_kernel(
    base_ref, request_ref, here_ref, there_ref, own_hbm, payload_ref, weight_ref, position_ref,
    before_hbm, current_hbm, integrals_hbm, denominator_hbm, cat_hbm, new_hbm, send_hbm, own_ref,
    cat_ref, full_ref, left_ref, acc_ref, sem_ref, before_ref, current_ref, integrals_ref,
    denominator_ref, send_ref, even_ref, odd_ref,
):
    pairs, size, unused = denominator_ref.shape
    near = here_ref.shape[0]
    fetches = [
        pltpu.make_async_copy(hbm, ref, sem_ref.at[2 + i])
        for i, (hbm, ref) in enumerate(
            (
                (before_hbm, before_ref), (current_hbm, current_ref),
                (integrals_hbm, integrals_ref), (denominator_hbm, denominator_ref),
            )
        )
    ]

    @pl.when(pl.program_id(0) == 0)
    def fetch():
        for copy in fetches:
            copy.start()

    near_chunk(
        base_ref[0], request_ref, there_ref, own_hbm, payload_ref, weight_ref, position_ref,
        cat_hbm, own_ref, cat_ref, full_ref, left_ref, acc_ref, sem_ref,
    )

    @pl.when(pl.program_id(0) == pl.num_programs(0) - 1)
    def finish():
        for copy in fetches:
            copy.wait()
        for s in range(pairs):
            rows = slice(s * size, (s + 1) * size)
            current, denominator = current_ref[rows, :], denominator_ref[s]
            coupled = coupled_of(acc_ref[s] + before_ref[s])
            residual = integrals_ref[rows, :] + denominator * current - coupled
            new = current - residual / denominator
            current_ref[rows, :] = new
            store_codes(new, even_ref, odd_ref, s)

        far_start = base_ref[0] // 2
        near_start = near - far_start
        column = base_ref[1]

        def pack(n, carry):
            for start, table_ref in ((near_start, here_ref), (far_start, there_ref)):
                first = table_ref[n, 0, column]
                second = table_ref[n, 0, column + 1]
                send_ref[start + n] = even_ref[first] + odd_ref[second]
            return carry

        lax.fori_loop(0, near, pack, 0)
        copies = [
            pltpu.make_async_copy(send_ref, send_hbm, sem_ref.at[2]),
            pltpu.make_async_copy(current_ref, new_hbm, sem_ref.at[3]),
        ]
        for copy in copies:
            copy.start()
        for copy in copies:
            copy.wait()


def second_kernel(
    base_ref, near_cat_hbm, far_cat_hbm, weight_ref, position_ref, amp_ref, current_hbm,
    integrals_hbm, denominator_hbm, new_ref, residual_ref, cat_ref, left_ref, acc_ref,
    current_ref, integrals_ref, denominator_ref, new_rows_ref, residual_rows_ref, sem_ref,
):
    pairs, size, unused = denominator_ref.shape
    step = pl.program_id(0)
    lanes = cat_ref.shape[3]
    slots = lanes // size
    cats = (near_cat_hbm, far_cat_hbm)
    fetches = [
        pltpu.make_async_copy(hbm, ref, sem_ref.at[i])
        for i, (hbm, ref) in enumerate(
            (
                (current_hbm, current_ref), (integrals_hbm, integrals_ref),
                (denominator_hbm, denominator_ref),
            )
        )
    ]
    cut = lanes // CUTS
    copies = [
        [
            pltpu.make_async_copy(
                cats[part].at[step, :, :, pl.ds(i * cut, cut)],
                cat_ref.at[part, :, :, pl.ds(i * cut, cut)],
                sem_ref.at[3 + part * CUTS + i],
            )
            for i in range(CUTS)
        ]
        for part in range(2)
    ]
    for copy in copies[0] + copies[1]:
        copy.start()

    @pl.when(step == 0)
    def fetch():
        for copy in fetches:
            copy.start()

    for part in range(2):
        first = base_ref[part] + step * slots
        weights = slot_weights(first, weight_ref, position_ref, slots, size)
        if part == 0:
            before = lambda s: jnp.where(step == 0, 0.0, acc_ref[s])
        else:
            before = lambda s: acc_ref[s]

        def ready(j, part=part):
            if j * 2 * size % cut == 0:
                copies[part][j * 2 * size // cut].wait()

        sweep_chunk(
            weights, lambda j: parts_of_codes(amp_ref[first // 2 + j]), cat_ref.at[part], left_ref.at[part],
            acc_ref, before, ready,
        )

    @pl.when(step == pl.num_programs(0) - 1)
    def finish():
        for copy in fetches:
            copy.wait()
        for s in range(pairs):
            rows = slice(s * size, (s + 1) * size)
            current, denominator = current_ref[rows, :], denominator_ref[s]
            residual = integrals_ref[rows, :] + denominator * current - coupled_of(acc_ref[s])
            residual_rows_ref[rows, :] = residual
            new_rows_ref[rows, :] = current - residual / denominator
        for rows_ref, out_ref in ((residual_rows_ref, residual_ref), (new_rows_ref, new_ref)):
            for a in range(0, size, 2):
                out_ref[:, a * size : (a + 2) * size] = jnp.concatenate(
                    [rows_ref[pl.ds(a + i, pairs, stride=size), :] for i in range(2)], axis=1
                )


def smem():
    return pl.BlockSpec(memory_space=pltpu.SMEM)


def vmem():
    return pl.BlockSpec(memory_space=pltpu.VMEM)


def hbm():
    return pl.BlockSpec(memory_space=pltpu.HBM)


def in_hbm(*arrays):
    return [pltpu.with_memory_space_constraint(array, pltpu.HBM) for array in arrays]


def by_step(shape, steps):
    if steps == 1:
        return vmem()
    return pl.BlockSpec(shape, lambda i, *refs: (i,) + (0,) * (len(shape) - 1))


def params():
    return pltpu.CompilerParams(
        dimension_semantics=("arbitrary",), vmem_limit_bytes=VMEM_LIMIT
    )


def prepare(pnos, domains, amplitudes, integrals):
    pairs, size, width = pnos.shape
    own = (pairs * size, ATOMS * (width // domains.shape[1]))
    block = (pairs * size, size)
    return pl.pallas_call(
        prepare_kernel,
        in_specs=[vmem()] * 4,
        out_specs=[vmem()] * 3,
        out_shape=[
            pltpu.HBM(own, jnp.bfloat16), pltpu.HBM(block, jnp.float32),
            pltpu.HBM(block, jnp.float32),
        ],
        scratch_shapes=[pltpu.VMEM((pairs, width), jnp.float32)],
        compiler_params=pltpu.CompilerParams(vmem_limit_bytes=VMEM_LIMIT),
        name="prepare",
    )(pnos, domains, amplitudes, integrals)


def pack_payload(column, table, pnos, amplitudes):
    pairs, size, width = pnos.shape
    near = table.shape[0]
    return pl.pallas_call(
        pack_kernel,
        in_specs=[smem(), smem(), vmem(), vmem()],
        out_specs=vmem(),
        out_shape=jax.ShapeDtypeStruct((near, 3 * size, width), jnp.bfloat16),
        scratch_shapes=[
            pltpu.VMEM((pairs * size, size), jnp.float32),
            pltpu.VMEM((pairs, size, 4 * size), jnp.bfloat16),
            pltpu.VMEM((pairs, size, 4 * size), jnp.bfloat16),
        ],
        compiler_params=pltpu.CompilerParams(vmem_limit_bytes=VMEM_LIMIT),
        name="pack_payload",
    )(column, table, pnos, amplitudes)


def chunk_shapes(own, payload, pairs, size):
    near, rows, width = payload.shape
    step = near if near <= ONE_STEP else NEAR_STEP
    lanes = 2 * step * size
    cat = (near // step, pairs, 2 * size, lanes)
    acc = (pairs, 2 * size, 2 * size)
    scratch = [
        pltpu.VMEM(own.shape, jnp.bfloat16),
        pltpu.VMEM(cat[1:], jnp.bfloat16),
        pltpu.VMEM((lanes, own.shape[1]), jnp.bfloat16),
        pltpu.VMEM((pairs, 2 * size, lanes), jnp.bfloat16),
        pltpu.VMEM(acc, jnp.float32),
        pltpu.SemaphoreType.DMA((6,)),
    ]
    return cat, (step, rows, width), acc, scratch


def first_sweep(base, request, table, own, payload, weight, position, size):
    cat, chunk, acc, scratch = chunk_shapes(own, payload, weight.shape[0], size)
    steps = cat[0]
    return pl.pallas_call(
        first_kernel,
        grid=(steps,),
        in_specs=[smem(), smem(), smem(), hbm(), by_step(chunk, steps), vmem(), vmem()],
        out_specs=[hbm(), hbm()],
        out_shape=[
            pltpu.HBM(cat, jnp.bfloat16), pltpu.HBM(acc, jnp.float32)
        ],
        scratch_shapes=scratch,
        compiler_params=params(),
        name="first_sweep_near",
    )(base, request, table, *in_hbm(own), payload, weight, position)


def first_sweep_end(
    base, request, here, there, own, payload, weight, position, before, current, integrals,
    denominator,
):
    pairs, size, unused = denominator.shape
    cat, chunk, acc, scratch = chunk_shapes(own, payload, pairs, size)
    steps = cat[0]
    parts = (pairs, size + CODE_ROWS, 2 * size)
    send = (2 * here.shape[0],) + parts[1:]
    return pl.pallas_call(
        first_end_kernel,
        grid=(steps,),
        in_specs=[smem()] * 4 + [hbm(), by_step(chunk, steps), vmem(), vmem()] + [hbm()] * 4,
        out_specs=[hbm()] * 3,
        out_shape=[
            pltpu.HBM(cat, jnp.bfloat16), pltpu.HBM(current.shape, jnp.float32),
            pltpu.HBM(send, jnp.int16),
        ],
        scratch_shapes=scratch + [
            pltpu.VMEM(acc, jnp.float32),
            pltpu.VMEM(current.shape, jnp.float32),
            pltpu.VMEM(current.shape, jnp.float32),
            pltpu.VMEM(denominator.shape, jnp.float32),
            pltpu.VMEM(send, jnp.int16),
            pltpu.VMEM(parts, jnp.int16),
            pltpu.VMEM(parts, jnp.int16),
        ],
        compiler_params=params(),
        name="first_sweep_far",
    )(
        base, request, here, there, *in_hbm(own), payload, weight, position,
        *in_hbm(before, current, integrals, denominator),
    )


def second_sweep(
    base, near_cat, far_cat, weight, position, amp, current, integrals, denominator
):
    pairs, size, unused = denominator.shape
    steps, lanes = near_cat.shape[0], near_cat.shape[3]
    flat = (pairs, size * size)
    return pl.pallas_call(
        second_kernel,
        grid=(steps,),
        in_specs=[smem(), hbm(), hbm(), vmem(), vmem(), vmem(), hbm(), hbm(), hbm()],
        out_specs=[vmem(), vmem()],
        out_shape=[jax.ShapeDtypeStruct(flat, jnp.float32)] * 2,
        scratch_shapes=[
            pltpu.VMEM((2,) + near_cat.shape[1:], jnp.bfloat16),
            pltpu.VMEM((2, pairs, 2 * size, lanes), jnp.bfloat16),
            pltpu.VMEM((pairs, 2 * size, 2 * size), jnp.float32),
            pltpu.VMEM(current.shape, jnp.float32),
            pltpu.VMEM(current.shape, jnp.float32),
            pltpu.VMEM(denominator.shape, jnp.float32),
            pltpu.VMEM(current.shape, jnp.float32),
            pltpu.VMEM(current.shape, jnp.float32),
            pltpu.SemaphoreType.DMA((3 + 2 * CUTS,)),
        ],
        compiler_params=params(),
        name="second_sweep",
    )(
        base, *in_hbm(near_cat, far_cat), weight, position, amp,
        *in_hbm(current, integrals, denominator),
    )


def on_device(
    amplitudes, integrals, virtual, occupied, coupling, degree, position, request, pnos, domains
):
    pairs = amplitudes.shape[0]
    size = virtual.shape[1]
    depth = coupling.shape[1]
    width = pnos.shape[2]
    slots = request.shape[1]
    near = slots // 4
    half = lax.axis_index("half").astype(jnp.int32)
    mine = lax.axis_index("near").astype(jnp.int32)
    swap = [(0, 1), (1, 0)]

    far_pnos = lax.ppermute(pnos, "half", swap)
    far_amplitudes = lax.ppermute(amplitudes, "half", swap)
    near_base = half * 2 * near
    far_base = (1 - half) * 2 * near
    near_column = near_base + 2 * mine
    far_column = far_base + 2 * mine

    def near_exchange(request, pnos, amplitudes, domains):
        row = jnp.concatenate([request, domains.reshape(1, -1)], axis=1)
        here = jnp.broadcast_to(row[None], (near, 1, row.shape[1]))
        here = lax.all_to_all(here, "near", split_axis=0, concat_axis=0, tiled=True)
        there = lax.ppermute(here, "half", swap)
        outgoing = pack_payload(near_column.reshape(1), here, pnos, amplitudes)
        payload = lax.all_to_all(outgoing, "near", split_axis=0, concat_axis=0, tiled=True)
        return here, there, payload

    def no_exchange(request, pnos, amplitudes, domains):
        table = jnp.zeros((near, 1, slots + domains.size), jnp.int32)
        return table, table, jnp.zeros((near, 3 * size, width), jnp.bfloat16)

    here, there, near_payload = lax.cond(
        degree[0] > 0, near_exchange, no_exchange, request, pnos, amplitudes, domains
    )
    outgoing = pack_payload(far_column.reshape(1), here, far_pnos, far_amplitudes)
    far_payload = lax.all_to_all(outgoing, "near", split_axis=0, concat_axis=0, tiled=True)

    live = jnp.arange(depth, dtype=jnp.int32)[None, :] < degree[:, None]
    weight = jnp.where(live, coupling, jnp.zeros_like(coupling))
    denominator = virtual[:, :, None] + virtual[:, None, :] - occupied[:, None, None]
    own, current, integrals = prepare(pnos, domains, amplitudes, integrals)
    near_cat, before = first_sweep(
        near_base.reshape(1), request, here, own, near_payload, weight, position, size
    )
    far_cat, current, amp = first_sweep_end(
        jnp.stack([far_base, near_column]), request, here, there, own, far_payload, weight,
        position, before, current, integrals, denominator,
    )
    amp = lax.all_to_all(amp, ("half", "near"), split_axis=0, concat_axis=0, tiled=True)
    new, residual = second_sweep(
        jnp.stack([near_base, far_base]), near_cat, far_cat, weight, position, amp, current,
        integrals, denominator,
    )
    return new, residual


def solution(mesh):
    count = mesh.shape["pair"]
    devices = mesh.devices.reshape(mesh.shape["frag"], 2, count // 2)
    split_mesh = Mesh(devices, ("frag", "half", "near"))
    rows = ("frag", "half", "near")
    return jax.shard_map(
        on_device,
        mesh=split_mesh,
        in_specs=(
            P(rows, None), P(rows, None), P(rows, None), P(rows), P(rows, None),
            P(rows), P(rows, None), P(rows, None), P(rows, None, None), P(rows, None),
        ),
        out_specs=(P(rows, None), P(rows, None)),
        check_vma=False,
    )
```

time: 93.7 us -> 81.8 us (0.87)
  waiting for transfers between devices: 34.4 us -> 22.2 us
  Pallas kernels: 17.1 us -> 26.7 us
  local copies, waits for them, and re-layouts: 10.4 us -> 0.83 us
  blocking collectives: 0 us -> 8.49 us
  starting transfers between devices: 27.6 us -> 19.6 us
  matrix products: 1.08 us -> 0 us
    pallas_call x5 -> x6, Pallas kernels: 17.1 us -> 26.7 us  [the longest x1 7.32 us: first_sweep_end(): pl.pallas_call(first_end_kernel, grid=(steps,), in_specs=[smem()] * 4 + [...]
    all_to_all x0 -> x1, blocking collectives: none -> 8.49 us  [near_exchange(): here = lax.all_to_all(here, 'near', split_axis=0, concat_axis=0, tiled=True)]
    unnamed x32 -> x20, local copies, waits for them, and re-layouts: 8.38 us -> 0.05 us
    ppermute x2 -> x1, waiting for transfers between devices: 14.4 us -> 6.99 us  [near_exchange(): there = lax.ppermute(here, 'half', swap)]
    all_to_all x2 -> x1, starting transfers between devices: 10.6 us -> 4.8 us  [on_device(): lax.all_to_all(outgoing, 'near', split_axis=0, concat_axis=0, tiled=True)]
    all_to_all x1, waiting for transfers between devices: 14.4 us -> 10.8 us  [on_device(): lax.all_to_all(amp, ('half', 'near'), split_axis=0, concat_axis=0, tiled=...]
    ppermute x2 -> x1, starting transfers between devices: 4.53 us -> 2.65 us  [near_exchange(): there = lax.ppermute(here, 'half', swap)]
    broadcast_in_dim x4 -> x1, local copies, waits for them, and re-layouts: 1.51 us -> 0.01 us  [near_exchange(): here = jnp.broadcast_to(row[None], (near, 1, row.shape[1]))]
  transfers between devices with their start and end apart: 8 -> 6, of which waited for: 5 -> 4; matrix products, arithmetic and copies ran while one was open for 4% -> 3% of each run, Pallas kernels for 6% -> 13%
where the time goes in v3:
time: 81.8 us; the launch traced here: 81.2 us
  Pallas kernels  26.7 us (33%)
  waiting for transfers between devices  22.2 us (27%)
  starting transfers between devices  19.6 us (24%)
  blocking collectives  8.49 us (10%)
  other arithmetic  1.8 us (2%)
  between operations  1.57 us (2%)
  local copies, waits for them, and re-layouts  0.83 us (1%)
    all_to_all x1, waiting for transfers between devices, on_device(): lax.all_to_all(amp, ('half', 'near'), split_axis=0, concat_axis=0, tiled=...  10.8 us
    all_to_all x1, blocking collectives, near_exchange(): here = lax.all_to_all(here, 'near', split_axis=0, concat_axis=0, tiled=True)  8.49 us
    pallas_call x1, Pallas kernels, first_sweep_end(): pl.pallas_call(first_end_kernel, grid=(steps,), in_specs=[smem()] * 4 + [...  7.32 us
    ppermute x1, waiting for transfers between devices, near_exchange(): there = lax.ppermute(here, 'half', swap)  6.99 us
    pallas_call x1, Pallas kernels, first_sweep(): pl.pallas_call(first_kernel, grid=(steps,), in_specs=[smem(), smem(), sme...  6.42 us
    pallas_call x1, Pallas kernels, second_sweep(): pl.pallas_call(second_kernel, grid=(steps,), in_specs=[smem(), hbm(), hbm...  6.38 us
    all_to_all x1, starting transfers between devices, on_device(): lax.all_to_all(outgoing, 'near', split_axis=0, concat_axis=0, tiled=True)  4.8 us
    pallas_call x2, Pallas kernels, pack_payload(): pl.pallas_call(pack_kernel, in_specs=[smem(), smem(), vmem(), vmem()], ou...  4.58 us
  transfers between devices with their start and end apart: 6, of which 4 were waited for; matrix products, arithmetic and copies ran while one was open for 3% of the time, Pallas kernels for 13%

profile of v3, /device:TPU:0, one launch (start us, length us, event | category | flops | bytes accessed | tf_op | source)
XLA Modules:
  0.0 81.2 jit_solution(6429443369039725964)
XLA Ops:
  0.6 4.1 %collective-permute-start.1 = (bf16[8,64,256]{2,1,0:T(8,128)(2,1)}, bf16[8,64,256]{2,1,0:T(8,128)(2,1)S(1)}, u32[]{:S(2)}, u32[]{:S(2)}) collective-permute-start(bf16[8,64,256]{2,1,0:T(8,128)(2,1)} %pnos_ref.1), channel_id=1, source_target_pairs={{0,8},{8,0},{1,9},{9,1},{2,10},{10,2},{3,11},{11,3},{4,12},{12,4},... | collective-permute-start | bytes 786440 | tf_op jit(solution)/shard_map/ppermute | solution.py:546
  4.7 0.1 collective-permute-start.2
  5.5 28.4 %conditional.1 = (s32[8,1,160]{2,1,0:T(1,128)}, s32[8,1,160]{2,1,0:T(1,128)}, bf16[8,192,256]{2,1,0:T(8,128)(2,1)}) conditional(s32[]{:T(128)} %bitcast.4, () %tuple.15, (s32[8,16]{1,0:T(8,128)}, s32[1,32]{1,0:T(1,128)}, s32[]{:T(128)}, bf16[8,64,256]{2,1,0:T(8,128)(2,1)}, f32[8,4096]{1,0:T(8,128)}) %tuple.16), branch_computations={%region_0.0_spmd, %region_1.0_spmd} | conditional | flops 160 | bytes 2398176 | solution.py:566
  5.5 0.8 reshape.22
  6.3 0.7 pad_add_fusion
  7.0 8.5 %all_to_all.18.table_ref = s32[8,1,160]{2,1,0:T(1,128)} all-to-all(s32[8,1,160]{2,1,0:T(1,128)S(1)} %broadcast_in_dim.4), channel_id=1, replica_groups=mesh['frag'=2,'half'=2,'near'=8] {'near'}, dimensions={0} | all-to-all | bytes 10240 | tf_op jit(solution)/shard_map/cond/branch_1_fun/all_to_all | solution.py:556
  15.5 2.3 %pack_payload.2 = bf16[8,192,256]{2,1,0:T(8,128)(2,1)} custom-call(s32[1]{0:T(128)} %bitcast.1.column_ref, s32[8,1,160]{2,1,0:T(1,128)} %all_to_all.18.table_ref, bf16[8,64,256]{2,1,0:T(8,128)(2,1)} %get-tuple-element.13.pnos_ref, f32[8,4096]{1,0:T(8,128)} %get-tuple-element.14.amp_ref), custom_call_target="tpu_custom_call" | custom-call | tf_op jit(solution)/shard_map/cond/branch_1_fun/pack_payload/pallas_call | solution.py:418
  17.8 4.2 %all-to-all-start.1 = ((bf16[8,192,256]{2,1,0:T(8,128)(2,1)}), bf16[8,192,256]{2,1,0:T(8,128)(2,1)}, u32[]{:S(2)}, u32[]{:S(2)}) async-start(bf16[8,192,256]{2,1,0:T(8,128)(2,1)} %pack_payload.2), calls=%async_computation.1 | async-start | bytes 1572864 | tf_op jit(solution)/shard_map/cond/branch_1_fun/all_to_all | solution.py:559
  22.0 2.7 %collective-permute-start = (s32[8,1,160]{2,1,0:T(1,128)}, s32[8,1,160]{2,1,0:T(1,128)}, u32[]{:S(2)}, u32[]{:S(2)}) collective-permute-start(s32[8,1,160]{2,1,0:T(1,128)} %all_to_all.18.table_ref), channel_id=1, source_target_pairs={{0,8},{8,0},{1,9},{9,1},{2,10},{10,2},{3,11},{11,3},{4,12},{12,4},... | collective-permute-start | bytes 15368 | tf_op jit(solution)/shard_map/cond/branch_1_fun/ppermute | solution.py:557
  24.7 7.0 %collective-permute-done = s32[8,1,160]{2,1,0:T(1,128)} collective-permute-done((s32[8,1,160]{2,1,0:T(1,128)}, s32[8,1,160]{2,1,0:T(1,128)}, u32[]{:S(2)}, u32[]{:S(2)}) %collective-permute-start) | collective-permute-done | bytes 5152 | tf_op jit(solution)/shard_map/cond/branch_1_fun/ppermute | solution.py:557
  31.7 2.2 %all-to-all-done.1 = bf16[8,192,256]{2,1,0:T(8,128)(2,1)} async-done(((bf16[8,192,256]{2,1,0:T(8,128)(2,1)}), bf16[8,192,256]{2,1,0:T(8,128)(2,1)}, u32[]{:S(2)}, u32[]{:S(2)}) %all-to-all-start.1) | async-done | bytes 786464 | tf_op jit(solution)/shard_map/cond/branch_1_fun/all_to_all | solution.py:559
  33.9 0.0 copy-start.7
  33.9 0.0 copy-start.9
  33.9 0.0 copy-start.1
  33.9 0.0 copy-start.6
  33.9 0.0 collective-permute-done.2.amp_ref
  33.9 0.0 collective-permute-done.1.pnos_ref
  33.9 0.0 copy-start.5
  33.9 0.0 copy-start.8
  33.9 2.3 %pack_payload.3 = bf16[8,192,256]{2,1,0:T(8,128)(2,1)} custom-call(s32[1]{0:T(128)} %bitcast.6.column_ref, s32[8,1,160]{2,1,0:T(1,128)} %get-tuple-element.28.table_ref.here_ref, bf16[8,64,256]{2,1,0:T(8,128)(2,1)S(1)} %collective-permute-done.1.pnos_ref, f32[8,4096]{1,0:T(8,128)S(1)} %collective-permute-done.2.amp_ref), custom_call_target="tpu_custom_call" | custom-call | tf_op jit(solution)/shard_map/pack_payload/pallas_call | solution.py:418
  36.2 4.8 %all-to-all-start.2 = ((bf16[8,192,256]{2,1,0:T(8,128)(2,1)}), bf16[8,192,256]{2,1,0:T(8,128)(2,1)S(1)}, u32[]{:S(2)}, u32[]{:S(2)}) async-start(bf16[8,192,256]{2,1,0:T(8,128)(2,1)} %pack_payload.3), calls=%async_computation.2 | async-start | bytes 1572864 | tf_op jit(solution)/shard_map/all_to_all | solution.py:570
  41.0 2.0 %prepare.1 = (bf16[512,512]{1,0:T(8,128)(2,1)}, f32[512,64]{1,0:T(8,128)}, f32[512,64]{1,0:T(8,128)}) custom-call(bf16[8,64,256]{2,1,0:T(8,128)(2,1)S(1)} %copy-done.2, s32[8,16]{1,0:T(8,128)S(1)} %copy-done.4, f32[8,4096]{1,0:T(8,128)S(1)} %copy-done.3, f32[8,4096]{1,0:T(8,128)S(1)} %copy-done), custom_call_target="tpu_custom_call" | custom-call | tf_op jit(solution)/shard_map/prepare/pallas_call | solution.py:401
  43.0 0.1 fusion.weight_ref
  43.1 6.4 %first_sweep_near.1 = (bf16[1,8,128,1024]{3,2,1,0:T(8,128)(2,1)}, f32[8,128,128]{2,1,0:T(8,128)}) custom-call(s32[1]{0:T(128)} %bitcast.2.base_ref, s32[1,32]{1,0:T(1,128)S(1)} %copy-done.6, s32[8,1,160]{2,1,0:T(1,128)} %get-tuple-element.28.table_ref.here_ref, bf16[512,512]{1,0:T(8,128)(2,1)} %get-tuple-element.29.own_hbm, ...), custom_call_target="tpu_custom_call" | custom-call | tf_op jit(solution)/shard_map/first_sweep_near/pallas_call | solution.py:453
  49.5 0.1 pad_add_fusion.2.base_ref
  49.6 0.8 %add_subtract_fusion.denominator_hbm = f32[8,64,64]{2,1,0:T(8,128)} fusion(f32[8]{0:T(128)S(1)} %copy-done.8, f32[8,64]{1,0:T(8,128)S(1)} %copy-done.5), kind=kLoop, calls=%fused_computation.1 | loop fusion | flops 65536 | bytes 133152 | tf_op jit(solution)/shard_map/sub | solution.py:574
  50.4 2.2 %all-to-all-done.2.payload_ref = bf16[8,192,256]{2,1,0:T(8,128)(2,1)S(1)} async-done(((bf16[8,192,256]{2,1,0:T(8,128)(2,1)}), bf16[8,192,256]{2,1,0:T(8,128)(2,1)S(1)}, u32[]{:S(2)}, u32[]{:S(2)}) %all-to-all-start.2) | async-done | bytes 786464 | tf_op jit(solution)/shard_map/all_to_all | solution.py:570
  52.7 7.3 %first_sweep_far.1 = (bf16[1,8,128,1024]{3,2,1,0:T(8,128)(2,1)}, f32[512,64]{1,0:T(8,128)}, s16[16,80,128]{2,1,0:T(8,128)(2,1)}) custom-call(s32[2]{0:T(128)S(1)} %pad_add_fusion.2.base_ref, s32[1,32]{1,0:T(1,128)S(1)} %copy-done.6, s32[8,1,160]{2,1,0:T(1,128)} %get-tuple-element.28.table_ref.here_ref, s32[8,1,160]{2,1,0:T(1,128)} %get-tuple-element.32.there_ref, ...), custom_call_target="tpu_custom_call" | custom-call | tf_op jit(solution)/shard_map/first_sweep_far/pallas_call | solution.py:476
  60.0 3.7 %all-to-all-start.3 = ((s16[16,80,128]{2,1,0:T(8,128)(2,1)}), s16[16,80,128]{2,1,0:T(8,128)(2,1)S(1)}, u32[]{:S(2)}, u32[]{:S(2)}) async-start(s16[16,80,128]{2,1,0:T(8,128)(2,1)} %get-tuple-element.37), calls=%async_computation.3 | async-start | bytes 655360 | tf_op jit(solution)/shard_map/all_to_all | solution.py:583
  63.7 0.1 pad_add_fusion.1.base_ref
  63.8 10.8 %all-to-all-done.3.amp_ref = s16[16,80,128]{2,1,0:T(8,128)(2,1)S(1)} async-done(((s16[16,80,128]{2,1,0:T(8,128)(2,1)}), s16[16,80,128]{2,1,0:T(8,128)(2,1)S(1)}, u32[]{:S(2)}, u32[]{:S(2)}) %all-to-all-start.3) | async-done | bytes 327712 | tf_op jit(solution)/shard_map/all_to_all | solution.py:583
  74.6 6.4 %second_sweep.1 = (f32[8,4096]{1,0:T(8,128)}, f32[8,4096]{1,0:T(8,128)}) custom-call(s32[2]{0:T(128)S(1)} %pad_add_fusion.1.base_ref, bf16[1,8,128,1024]{3,2,1,0:T(8,128)(2,1)} %get-tuple-element.31.near_cat_hbm, bf16[1,8,128,1024]{3,2,1,0:T(8,128)(2,1)} %get-tuple-element.36.far_cat_hbm, f32[8,16]{1,0:T(8,128)S(1)} %fusion.weight_ref, ...), custom_call_target="tpu_custom_call" | custom-call | tf_op jit(solution)/shard_map/second_sweep/pallas_call | solution.py:508
  (15 shorter events, 0.0 us)
Async XLA Ops:
  0.6 33.3 %collective-permute-start.1 = (bf16[8,64,256]{2,1,0:T(8,128)(2,1)}, bf16[8,64,256]{2,1,0:T(8,128)(2,1)S(1)}, u32[]{:S(2)}, u32[]{:S(2)}) collective-permute-start(bf16[8,64,256]{2,1,0:T(8,128)(2,1)} %pnos_ref.1), channel_id=1, source_target_pairs={{0,8},{8,0},{1,9},{9,1},{2,10},{10,2},{3,11},{11,3},{4,12},{12,4},... | collective-permute-start | bytes 786440 | tf_op jit(solution)/shard_map/ppermute | solution.py:546
  4.7 29.2 %collective-permute-start.2 = (f32[8,4096]{1,0:T(8,128)}, f32[8,4096]{1,0:T(8,128)S(1)}, u32[]{:S(2)}, u32[]{:S(2)}) collective-permute-start(f32[8,4096]{1,0:T(8,128)} %amp_ref.1), channel_id=1, source_target_pairs={{0,8},{8,0},{1,9},{9,1},{2,10},{10,2},{3,11},{11,3},{4,12},{12,4},... | collective-permute-start | bytes 393224 | tf_op jit(solution)/shard_map/ppermute | solution.py:547
  17.8 16.0 %all-to-all-start.1 = ((bf16[8,192,256]{2,1,0:T(8,128)(2,1)}), bf16[8,192,256]{2,1,0:T(8,128)(2,1)}, u32[]{:S(2)}, u32[]{:S(2)}) async-start(bf16[8,192,256]{2,1,0:T(8,128)(2,1)} %pack_payload.2), calls=%async_computation.1 | async-start | bytes 1572864 | tf_op jit(solution)/shard_map/cond/branch_1_fun/all_to_all | solution.py:559
  22.0 9.6 %collective-permute-start = (s32[8,1,160]{2,1,0:T(1,128)}, s32[8,1,160]{2,1,0:T(1,128)}, u32[]{:S(2)}, u32[]{:S(2)}) collective-permute-start(s32[8,1,160]{2,1,0:T(1,128)} %all_to_all.18.table_ref), channel_id=1, source_target_pairs={{0,8},{8,0},{1,9},{9,1},{2,10},{10,2},{3,11},{11,3},{4,12},{12,4},... | collective-permute-start | bytes 15368 | tf_op jit(solution)/shard_map/cond/branch_1_fun/ppermute | solution.py:557
  33.8 7.2 %copy-start = (f32[8,4096]{1,0:T(8,128)S(1)}, f32[8,4096]{1,0:T(8,128)}, u32[]{:S(2)}) copy-start(f32[8,4096]{1,0:T(8,128)} %integrals_ref.1) | copy-start | bytes 393220
  33.8 7.2 %copy-start.2 = (bf16[8,64,256]{2,1,0:T(8,128)(2,1)S(1)}, bf16[8,64,256]{2,1,0:T(8,128)(2,1)}, u32[]{:S(2)}) copy-start(bf16[8,64,256]{2,1,0:T(8,128)(2,1)} %pnos_ref.1) | copy-start | bytes 786436
  33.8 7.2 %copy-start.3 = (f32[8,4096]{1,0:T(8,128)S(1)}, f32[8,4096]{1,0:T(8,128)}, u32[]{:S(2)}) copy-start(f32[8,4096]{1,0:T(8,128)} %amp_ref.1) | copy-start | bytes 393220
  33.8 7.2 %copy-start.4 = (s32[8,16]{1,0:T(8,128)S(1)}, s32[8,16]{1,0:T(8,128)}, u32[]{:S(2)}) copy-start(s32[8,16]{1,0:T(8,128)} %domains_ref.1) | copy-start | bytes 1540
  33.9 9.2 %copy-start.7 = (f32[8,16]{1,0:T(8,128)S(1)}, f32[8,16]{1,0:T(8,128)}, u32[]{:S(2)}) copy-start(f32[8,16]{1,0:T(8,128)} %param.16) | copy-start | bytes 1540
  33.9 9.2 %copy-start.9 = (s32[8]{0:T(128)S(1)}, s32[8]{0:T(128)}, u32[]{:S(2)}) copy-start(s32[8]{0:T(128)} %param.17) | copy-start | bytes 100
  33.9 9.2 %copy-start.1 = (s32[8,16]{1,0:T(8,128)S(1)}, s32[8,16]{1,0:T(8,128)}, u32[]{:S(2)}) copy-start(s32[8,16]{1,0:T(8,128)} %position_ref.5) | copy-start | bytes 1540
  33.9 9.2 %copy-start.6 = (s32[1,32]{1,0:T(1,128)S(1)}, s32[1,32]{1,0:T(1,128)}, u32[]{:S(2)}) copy-start(s32[1,32]{1,0:T(1,128)} %request_ref.3) | copy-start | bytes 388
  33.9 15.7 %copy-start.5 = (f32[8,64]{1,0:T(8,128)S(1)}, f32[8,64]{1,0:T(8,128)}, u32[]{:S(2)}) copy-start(f32[8,64]{1,0:T(8,128)} %param.14) | copy-start | bytes 6148
  33.9 15.7 %copy-start.8 = (f32[8]{0:T(128)S(1)}, f32[8]{0:T(128)}, u32[]{:S(2)}) copy-start(f32[8]{0:T(128)} %param.15) | copy-start | bytes 100
  36.2 16.5 %all-to-all-start.2 = ((bf16[8,192,256]{2,1,0:T(8,128)(2,1)}), bf16[8,192,256]{2,1,0:T(8,128)(2,1)S(1)}, u32[]{:S(2)}, u32[]{:S(2)}) async-start(bf16[8,192,256]{2,1,0:T(8,128)(2,1)} %pack_payload.3), calls=%async_computation.2 | async-start | bytes 1572864 | tf_op jit(solution)/shard_map/all_to_all | solution.py:570
  60.0 14.6 %all-to-all-start.3 = ((s16[16,80,128]{2,1,0:T(8,128)(2,1)}), s16[16,80,128]{2,1,0:T(8,128)(2,1)S(1)}, u32[]{:S(2)}, u32[]{:S(2)}) async-start(s16[16,80,128]{2,1,0:T(8,128)(2,1)} %get-tuple-element.37), calls=%async_computation.3 | async-start | bytes 655360 | tf_op jit(solution)/shard_map/all_to_all | solution.py:583

commit v4 on v3

v4 whole, which is shorter than its diff:
```python
import jax
import jax.numpy as jnp
from jax import lax
from jax.experimental import pallas as pl
from jax.experimental.pallas import tpu as pltpu
from jax.sharding import Mesh, PartitionSpec as P

ATOMS = 32
CHUNK = 4
ONE_STEP = 16
LOG_TOP = 125.0
CODE_TOP = 32767.0
CODE_ROWS = 16
AHEAD = 2
SMALLEST = 2.0**-100
VMEM_LIMIT = 32 * 1024 * 1024
NT = (((1,), (1,)), ((), ()))


def split(value):
    high = value.astype(jnp.bfloat16)
    low = (value - high.astype(jnp.float32)).astype(jnp.bfloat16)
    return high, low


def scale_of(eighths):
    return jnp.exp2(eighths * 0.125)


def eighths_of(value):
    top = jnp.maximum(jnp.max(jnp.abs(value), axis=0, keepdims=True), SMALLEST)
    return jnp.ceil(jnp.log2(top) * 8.0)


def store_codes(value, even_ref, odd_ref, p):
    size = value.shape[0]
    eighths = eighths_of(value)
    codes = jnp.clip(jnp.round(value * (CODE_TOP / scale_of(eighths))), -CODE_TOP, CODE_TOP)
    rows = jnp.concatenate([codes, jnp.broadcast_to(eighths, (CODE_ROWS, size))], axis=0)
    blank = jnp.zeros_like(rows)
    for ref, parts in ((even_ref, [rows, blank]), (odd_ref, [blank, rows])):
        ref[p] = jnp.concatenate(parts, axis=1).astype(jnp.int32).astype(jnp.int16)


def block_of_codes(codes):
    rows = codes.astype(jnp.int32).astype(jnp.float32)
    size = rows.shape[0] - CODE_ROWS
    return rows[:size, :] * (scale_of(rows[size : size + 1, :]) * (1.0 / CODE_TOP))


def log_code(value, eighths):
    power = jnp.clip(value * (LOG_TOP / scale_of(eighths)), -LOG_TOP, LOG_TOP)
    return jnp.exp2(power)


def block_of_logs(logs, eighths):
    rows, lanes = logs.shape[0], logs.shape[1] // 2
    size = lanes // 2
    first, second = logs[:, :lanes], logs[:, lanes:]
    left = lax.broadcasted_iota(jnp.int32, (rows, lanes), 1) < size
    upper = jnp.where(left, first, pltpu.roll(second, size, 1))
    lower = jnp.where(left, pltpu.roll(first, size, 1), second)
    both = jnp.concatenate([upper, lower], axis=0)
    return jnp.log2(both) * (scale_of(eighths) * (1.0 / LOG_TOP))


def to_blocks(flat_ref, rows_ref, size):
    pairs = flat_ref.shape[0]
    for a in range(0, size, 2):
        both = flat_ref[:, a * size : (a + 2) * size]
        rows_ref[pl.ds(a, pairs, stride=size), :] = both[:, :size]
        rows_ref[pl.ds(a + 1, pairs, stride=size), :] = both[:, size:]


def atoms_of_columns(domains, width):
    count = domains.shape[1]
    entry = lax.broadcasted_iota(jnp.int32, (count, width), 0)
    column = lax.broadcasted_iota(jnp.int32, (count, width), 1)
    spread = (entry == column // (width // count)).astype(jnp.float32).astype(jnp.bfloat16)
    atoms = domains.astype(jnp.float32).astype(jnp.bfloat16)
    return jnp.dot(atoms, spread, preferred_element_type=jnp.float32)


def column_table(atoms, columns):
    width = atoms.shape[1]
    per_atom = columns // ATOMS
    row = lax.broadcasted_iota(jnp.int32, (columns, width), 0)
    column = lax.broadcasted_iota(jnp.int32, (1, width), 1)
    ids = atoms.astype(jnp.int32) * per_atom + column % per_atom
    return (row == ids).astype(jnp.float32).astype(jnp.bfloat16)


def prepare_kernel(
    pnos_ref, domains_ref, amp_ref, integrals_ref, own_ref, current_ref, blocks_ref, atoms_ref
):
    pairs, size, width = pnos_ref.shape
    columns = own_ref.shape[1]
    to_blocks(amp_ref, current_ref, size)
    to_blocks(integrals_ref, blocks_ref, size)
    atoms_ref[...] = atoms_of_columns(domains_ref[...], width)
    for p in range(pairs):
        own_ref[p * size : (p + 1) * size, :] = lax.dot_general(
            pnos_ref[p], column_table(atoms_ref[p : p + 1, :], columns), NT,
            preferred_element_type=jnp.float32,
        ).astype(jnp.bfloat16)


def encode_kernel(
    amp_hbm, domains_hbm, request_hbm, logs_ref, table_ref, amp_ref, domains_ref, request_ref,
    rows_ref, sem_ref,
):
    pairs, half_size, lanes = logs_ref.shape
    size = lanes // 2
    copies = [
        pltpu.make_async_copy(amp_hbm, amp_ref, sem_ref.at[0]),
        pltpu.make_async_copy(domains_hbm, domains_ref, sem_ref.at[1]),
        pltpu.make_async_copy(request_hbm, request_ref, sem_ref.at[2]),
    ]
    for copy in copies:
        copy.start()
    for copy in copies:
        copy.wait()
    to_blocks(amp_ref, rows_ref, size)
    scales = []
    for p in range(pairs):
        block = rows_ref[p * size : (p + 1) * size, :]
        eighths = eighths_of(block)
        logs = log_code(block, eighths)
        logs_ref[p] = jnp.concatenate(
            [logs[:half_size, :], logs[half_size:, :]], axis=1
        ).astype(jnp.bfloat16)
        scales.append(eighths)
    scales = jnp.concatenate(scales, axis=0).astype(jnp.int32)
    count = domains_ref.shape[1]
    slots = request_ref.shape[1]
    table_ref[:, :size] = scales
    table_ref[:, size : size + count] = domains_ref[...]
    table_ref[:, size + count :] = jnp.broadcast_to(request_ref[...], (pairs, slots))


def pack_kernel(
    here_ref, there_ref, pnos_ref, logs_ref, far_pnos_ref, far_logs_ref, out_ref
):
    unused, size, width = pnos_ref.shape
    lanes = logs_ref.shape[2]

    def pack(n, carry):
        parts = ((here_ref, pnos_ref, logs_ref), (there_ref, far_pnos_ref, far_logs_ref))
        for part, (wanted_ref, blocks_ref, codes_ref) in enumerate(parts):
            first = wanted_ref[n, 0]
            second = wanted_ref[n, 1]
            out_ref[n, part, :size] = blocks_ref[first]
            out_ref[n, part, size : 2 * size] = blocks_ref[second]
            out_ref[n, part, 2 * size :, :lanes] = codes_ref[first]
            out_ref[n, part, 2 * size :, lanes:] = codes_ref[second]
        return carry

    lax.fori_loop(0, out_ref.shape[0], pack, 0)


def source_of(entry, half, near):
    return (entry % 2 + half) % 2 * near + entry // 2


def slot_weights(half, near, start, weight_ref, position_ref, size):
    slot = lax.broadcasted_iota(jnp.int32, (1, 2 * CHUNK * size), 1) // size
    source = source_of(start + slot // 2, half, near)
    named = source * 2 + slot % 2
    total = jnp.zeros((weight_ref.shape[0], named.shape[1]), jnp.float32)
    for c in range(weight_ref.shape[1]):
        hit = position_ref[:, c : c + 1] == named
        total += jnp.where(hit, weight_ref[:, c : c + 1], 0.0)
    return total


def half_products(weights, amps, cat_ref, left_ref):
    pairs, rows2, lanes = cat_ref.shape
    size = rows2 // 2
    group = lax.broadcasted_iota(jnp.int32, (size, 4 * size), 1) // size
    even = (group % 2 == 0).astype(jnp.float32).astype(jnp.bfloat16)
    odd = (group % 2 == 1).astype(jnp.float32).astype(jnp.bfloat16)
    for j in range(CHUNK):
        cols = slice(j * 2 * size, (j + 1) * 2 * size)
        amp = jnp.concatenate(split(amps(j)), axis=1)
        first, second = amp * even, amp * odd
        right = jnp.concatenate([first, second, first, second], axis=0)
        high = cat_ref[:, :size, cols].reshape(pairs * size, 2 * size)
        low = cat_ref[:, size:, cols].reshape(pairs * size, 2 * size)
        both = jnp.dot(
            jnp.concatenate([high, low], axis=1), right, preferred_element_type=jnp.float32
        )
        left = (both[:, : 2 * size] + both[:, 2 * size :]).reshape(pairs, size, 2 * size)
        left = left * weights[:, cols].reshape(pairs, 1, 2 * size)
        left_high, left_low = split(left)
        left_ref[:, :size, cols] = left_high
        left_ref[:, size:, cols] = left_low


def add_products(first, cat_ref, left_ref, acc_ref):
    for s in range(acc_ref.shape[0]):
        total = jnp.where(first, 0.0, acc_ref[s])
        for c in range(cat_ref.shape[0]):
            total += lax.dot_general(
                left_ref[c, s], cat_ref[c, s], NT, preferred_element_type=jnp.float32
            )
        acc_ref[s] = total


def cross_chunk(atoms, own_ref, payload_ref, cat_ref, full_ref):
    columns = own_ref.shape[1]
    pairs, rows2, unused = cat_ref.shape
    size = rows2 // 2
    for k in range(2 * CHUNK):
        n, c = k // 2, k % 2
        full_ref[k * size : (k + 1) * size, :] = lax.dot_general(
            payload_ref[n, c * size : (c + 1) * size, :],
            column_table(atoms[k : k + 1, :], columns), NT, preferred_element_type=jnp.float32,
        ).astype(jnp.bfloat16)
    cross = lax.dot_general(own_ref[...], full_ref[...], NT, preferred_element_type=jnp.float32)
    high, low = split(cross)
    cat_ref[:, :size, :] = high.reshape(pairs, size, -1)
    cat_ref[:, size:, :] = low.reshape(pairs, size, -1)


def coupled_of(acc):
    size = acc.shape[0] // 2
    rows = acc[:size] + acc[size:]
    return rows[:, :size] + rows[:, size:]


def first_kernel(
    half_ref, request_ref, wanted_ref, table_ref, own_hbm, payload_ref, weight_ref, position_ref,
    current_hbm, integrals_hbm, denominator_hbm, cat_hbm, new_hbm, send_hbm, own_ref, cat_ref,
    full_ref, left_ref, acc_ref, info_ref, current_ref, integrals_ref, denominator_ref, send_ref,
    even_ref, odd_ref, sem_ref, cat_sem_ref,
):
    pairs, size, unused = denominator_ref.shape
    width = payload_ref.shape[2]
    chunks = cat_ref.shape[0]
    near = wanted_ref.shape[0] // 2
    half = half_ref[0]
    step = pl.program_id(0)
    count = table_ref.shape[2] - size - request_ref.shape[1]
    fetches = [
        pltpu.make_async_copy(hbm, ref, sem_ref.at[i])
        for i, (hbm, ref) in enumerate(
            (
                (own_hbm, own_ref), (current_hbm, current_ref), (integrals_hbm, integrals_ref),
                (denominator_hbm, denominator_ref),
            )
        )
    ]

    @pl.when(step == 0)
    def fetch():
        for copy in fetches:
            copy.start()

    entries = CHUNK * chunks
    lanes = table_ref.shape[2]
    for k in range(2 * entries):
        source = source_of(step * entries + k // 2, half, near)
        row = request_ref[0, source * 2 + k % 2]
        info_ref[k : k + 1, :lanes] = table_ref[source, pl.ds(row, 1), :lanes]
    atoms = atoms_of_columns(info_ref[:, size : size + count], width)
    scales = info_ref[:, : 2 * size].astype(jnp.float32)
    moved = pltpu.roll(scales, size, 1)
    left_lanes = lax.broadcasted_iota(jnp.int32, (1, 2 * size), 1) < size

    @pl.when(step == 0)
    def own_ready():
        fetches[0].wait()

    cat_copies = []
    for c in range(chunks):
        blocks = payload_ref.at[pl.ds(c * CHUNK, CHUNK)]
        cross_chunk(
            atoms[c * 2 * CHUNK : (c + 1) * 2 * CHUNK], own_ref, blocks, cat_ref.at[c],
            full_ref.at[c],
        )
        copy = pltpu.make_async_copy(
            cat_ref.at[c], cat_hbm.at[step * chunks + c], cat_sem_ref.at[c]
        )
        copy.start()
        cat_copies.append(copy)
        start = step * entries + c * CHUNK
        weights = slot_weights(half, near, start, weight_ref, position_ref, size)

        def amps(j, c=c, blocks=blocks):
            k = 2 * (c * CHUNK + j)
            eighths = jnp.where(left_lanes, scales[k : k + 1, :], moved[k + 1 : k + 2, :])
            logs = blocks[j, 2 * size :, :].astype(jnp.float32)
            return block_of_logs(logs, eighths)

        half_products(weights, amps, cat_ref.at[c], left_ref.at[c])
    add_products(step == 0, cat_ref, left_ref, acc_ref)

    @pl.when(step == pl.num_programs(0) - 1)
    def finish():
        for copy in fetches[1:]:
            copy.wait()
        for s in range(pairs):
            rows = slice(s * size, (s + 1) * size)
            current, denominator = current_ref[rows, :], denominator_ref[s]
            residual = integrals_ref[rows, :] + denominator * current - coupled_of(acc_ref[s])
            new = current - residual / denominator
            current_ref[rows, :] = new
            store_codes(new, even_ref, odd_ref, s)

        def pack(d, carry):
            send_ref[d] = even_ref[wanted_ref[d, 0]] + odd_ref[wanted_ref[d, 1]]
            return carry

        lax.fori_loop(0, send_ref.shape[0], pack, 0)
        copies = [
            pltpu.make_async_copy(send_ref, send_hbm, sem_ref.at[0]),
            pltpu.make_async_copy(current_ref, new_hbm, sem_ref.at[1]),
        ]
        for copy in copies:
            copy.start()
        for copy in copies:
            copy.wait()

    for copy in cat_copies:
        copy.wait()


def second_kernel(
    half_ref, cat_hbm, weight_ref, position_ref, amp_ref, current_hbm, integrals_hbm,
    denominator_hbm, new_ref, residual_ref, cat_ref, left_ref, acc_ref, current_ref,
    integrals_ref, denominator_ref, new_rows_ref, residual_rows_ref, sem_ref, cat_sem_ref,
):
    pairs, size, unused = denominator_ref.shape
    step = pl.program_id(0)
    half = half_ref[0]
    near = amp_ref.shape[0] // 2
    chunks = cat_ref.shape[0]
    fetches = [
        pltpu.make_async_copy(hbm, ref, sem_ref.at[i])
        for i, (hbm, ref) in enumerate(
            (
                (current_hbm, current_ref), (integrals_hbm, integrals_ref),
                (denominator_hbm, denominator_ref),
            )
        )
    ]
    copies = [
        pltpu.make_async_copy(
            cat_hbm.at[step * chunks + c], cat_ref.at[c], cat_sem_ref.at[c]
        )
        for c in range(chunks)
    ]
    for copy in copies[:AHEAD]:
        copy.start()
    for c in range(chunks):
        start = (step * chunks + c) * CHUNK
        weights = slot_weights(half, near, start, weight_ref, position_ref, size)
        copies[c].wait()
        if c + AHEAD < chunks:
            copies[c + AHEAD].start()
        elif c + AHEAD == chunks or c == chunks - 1 and chunks < AHEAD:
            @pl.when(step == pl.num_programs(0) - 1)
            def fetch():
                for copy in fetches:
                    copy.start()

        half_products(
            weights, lambda j: block_of_codes(amp_ref[source_of(start + j, half, near)]),
            cat_ref.at[c], left_ref.at[c],
        )
    add_products(step == 0, cat_ref, left_ref, acc_ref)

    @pl.when(step == pl.num_programs(0) - 1)
    def finish():
        for copy in fetches:
            copy.wait()
        for s in range(pairs):
            rows = slice(s * size, (s + 1) * size)
            current, denominator = current_ref[rows, :], denominator_ref[s]
            residual = integrals_ref[rows, :] + denominator * current - coupled_of(acc_ref[s])
            residual_rows_ref[rows, :] = residual
            new_rows_ref[rows, :] = current - residual / denominator
        for rows_ref, out_ref in ((residual_rows_ref, residual_ref), (new_rows_ref, new_ref)):
            for a in range(0, size, 2):
                out_ref[:, a * size : (a + 2) * size] = jnp.concatenate(
                    [rows_ref[pl.ds(a + i, pairs, stride=size), :] for i in range(2)], axis=1
                )


def smem():
    return pl.BlockSpec(memory_space=pltpu.SMEM)


def vmem():
    return pl.BlockSpec(memory_space=pltpu.VMEM)


def hbm():
    return pl.BlockSpec(memory_space=pltpu.HBM)


def in_hbm(*arrays):
    return [pltpu.with_memory_space_constraint(array, pltpu.HBM) for array in arrays]


def params():
    return pltpu.CompilerParams(
        dimension_semantics=("arbitrary",), vmem_limit_bytes=VMEM_LIMIT
    )


def limit():
    return pltpu.CompilerParams(vmem_limit_bytes=VMEM_LIMIT)


def prepare(pnos, domains, amplitudes, integrals):
    pairs, size, width = pnos.shape
    own = (pairs * size, ATOMS * (width // domains.shape[1]))
    block = (pairs * size, size)
    return pl.pallas_call(
        prepare_kernel,
        in_specs=[vmem()] * 4,
        out_specs=[vmem()] * 3,
        out_shape=[
            pltpu.HBM(own, jnp.bfloat16), pltpu.HBM(block, jnp.float32),
            pltpu.HBM(block, jnp.float32),
        ],
        scratch_shapes=[pltpu.VMEM((pairs, width), jnp.float32)],
        compiler_params=limit(),
        name="prepare",
    )(pnos, domains, amplitudes, integrals)


def encode(amplitudes, domains, request, size):
    pairs = amplitudes.shape[0]
    lanes = size + domains.shape[1] + request.shape[1]
    return pl.pallas_call(
        encode_kernel,
        in_specs=[hbm()] * 3,
        out_specs=[vmem()] * 2,
        out_shape=[
            jax.ShapeDtypeStruct((pairs, size // 2, 2 * size), jnp.bfloat16),
            jax.ShapeDtypeStruct((pairs, lanes), jnp.int32),
        ],
        scratch_shapes=[
            pltpu.VMEM(amplitudes.shape, jnp.float32), pltpu.VMEM(domains.shape, jnp.int32),
            pltpu.VMEM(request.shape, jnp.int32), pltpu.VMEM((pairs * size, size), jnp.float32),
            pltpu.SemaphoreType.DMA((3,)),
        ],
        compiler_params=limit(),
        name="encode",
    )(*in_hbm(amplitudes, domains, request))


def pack_payload(here, there, pnos, logs, far_pnos, far_logs):
    unused, size, width = pnos.shape
    rows = 2 * size + logs.shape[1]
    return pl.pallas_call(
        pack_kernel,
        in_specs=[smem(), smem()] + [vmem()] * 4,
        out_specs=vmem(),
        out_shape=jax.ShapeDtypeStruct((here.shape[0], 2, rows, width), jnp.bfloat16),
        compiler_params=limit(),
        name="pack_payload",
    )(here, there, pnos, logs, far_pnos, far_logs)


def sweep_shapes(entries, pairs, size):
    chunks = entries // CHUNK if entries <= ONE_STEP else 1
    cat = (entries // CHUNK, pairs, 2 * size, 2 * CHUNK * size)
    held = (chunks,) + cat[1:]
    scratch = [
        pltpu.VMEM(held, jnp.bfloat16), pltpu.VMEM(held, jnp.bfloat16),
        pltpu.VMEM((pairs, 2 * size, 2 * size), jnp.float32),
    ]
    return cat[0] // chunks, chunks, cat, scratch


def first_sweep(
    half, request, wanted, table, own, payload, weight, position, current, integrals, denominator
):
    pairs, size, unused = denominator.shape
    entries, rows, width = payload.shape
    steps, chunks, cat, (cats, lefts, acc) = sweep_shapes(entries, pairs, size)
    block = (CHUNK * chunks, rows, width)
    blocks = vmem() if steps == 1 else pl.BlockSpec(block, lambda i: (i, 0, 0))
    parts = (pairs, size + CODE_ROWS, 2 * size)
    send = (entries,) + parts[1:]
    return pl.pallas_call(
        first_kernel,
        grid=(steps,),
        in_specs=[smem()] * 3 + [vmem(), hbm(), blocks, vmem(), vmem()] + [hbm()] * 3,
        out_specs=[hbm()] * 3,
        out_shape=[
            pltpu.HBM(cat, jnp.bfloat16), pltpu.HBM(current.shape, jnp.float32),
            pltpu.HBM(send, jnp.int16),
        ],
        scratch_shapes=[
            pltpu.VMEM(own.shape, jnp.bfloat16),
            cats,
            pltpu.VMEM((chunks, cat[3], own.shape[1]), jnp.bfloat16),
            lefts,
            acc,
            pltpu.VMEM((2 * CHUNK * chunks, max(table.shape[2], 2 * size)), jnp.int32),
            pltpu.VMEM(current.shape, jnp.float32),
            pltpu.VMEM(current.shape, jnp.float32),
            pltpu.VMEM(denominator.shape, jnp.float32),
            pltpu.VMEM(send, jnp.int16),
            pltpu.VMEM(parts, jnp.int16),
            pltpu.VMEM(parts, jnp.int16),
            pltpu.SemaphoreType.DMA((4,)),
            pltpu.SemaphoreType.DMA((chunks,)),
        ],
        compiler_params=params(),
        name="first_sweep",
    )(
        half, request, wanted, table, *in_hbm(own), payload, weight, position,
        *in_hbm(current, integrals, denominator),
    )


def second_sweep(half, cat, weight, position, amp, current, integrals, denominator):
    pairs, size, unused = denominator.shape
    steps, chunks, unused, scratch = sweep_shapes(amp.shape[0], pairs, size)
    flat = (pairs, size * size)
    return pl.pallas_call(
        second_kernel,
        grid=(steps,),
        in_specs=[smem(), hbm(), vmem(), vmem(), vmem(), hbm(), hbm(), hbm()],
        out_specs=[vmem(), vmem()],
        out_shape=[jax.ShapeDtypeStruct(flat, jnp.float32)] * 2,
        scratch_shapes=scratch + [
            pltpu.VMEM(current.shape, jnp.float32),
            pltpu.VMEM(current.shape, jnp.float32),
            pltpu.VMEM(denominator.shape, jnp.float32),
            pltpu.VMEM(current.shape, jnp.float32),
            pltpu.VMEM(current.shape, jnp.float32),
            pltpu.SemaphoreType.DMA((3,)),
            pltpu.SemaphoreType.DMA((chunks,)),
        ],
        compiler_params=params(),
        name="second_sweep",
    )(
        half, *in_hbm(cat), weight, position, amp, *in_hbm(current, integrals, denominator),
    )


def on_device(
    amplitudes, integrals, virtual, occupied, coupling, degree, position, request, pnos, domains
):
    pairs = amplitudes.shape[0]
    size = virtual.shape[1]
    depth = coupling.shape[1]
    slots = request.shape[1]
    entries = slots // 2
    near = entries // 2
    half = lax.axis_index("half").astype(jnp.int32)
    mine = lax.axis_index("near").astype(jnp.int32)
    swap = [(0, 1), (1, 0)]
    both = ("half", "near")

    far_pnos = lax.ppermute(pnos, "half", swap)
    logs, table = encode(amplitudes, domains, request, size)
    far_logs = lax.ppermute(logs, "half", swap)

    def gather(row):
        rows = jnp.broadcast_to(row[None], (entries,) + row.shape)
        return lax.all_to_all(rows, both, split_axis=0, concat_axis=0, tiled=True)

    def nothing(row):
        return jnp.zeros((entries,) + row.shape, jnp.int32)

    table = lax.cond(degree[0] > 0, gather, nothing, table)
    column = table.shape[2] - slots + 2 * mine
    wanted = lax.dynamic_slice(
        table, (0, 0, column + half * 2 * near), (entries, 1, 2)
    ).reshape(entries, 2)
    here = lax.dynamic_slice(wanted, (half * near, 0), (near, 2))
    there = lax.dynamic_slice(
        table, (half * near, 0, column + (1 - half) * 2 * near), (near, 1, 2)
    ).reshape(near, 2)

    payload = pack_payload(here, there, pnos, logs, far_pnos, far_logs)
    payload = lax.all_to_all(payload, "near", split_axis=0, concat_axis=0, tiled=True)
    payload = payload.reshape((entries,) + payload.shape[2:])

    live = jnp.arange(depth, dtype=jnp.int32)[None, :] < degree[:, None]
    weight = jnp.where(live, coupling, jnp.zeros_like(coupling))
    denominator = virtual[:, :, None] + virtual[:, None, :] - occupied[:, None, None]
    own, current, integrals = prepare(pnos, domains, amplitudes, integrals)
    half = half.reshape(1)
    cat, current, amp = first_sweep(
        half, request, wanted, table, own, payload, weight, position, current, integrals,
        denominator,
    )
    amp = lax.all_to_all(amp, both, split_axis=0, concat_axis=0, tiled=True)
    new, residual = second_sweep(
        half, cat, weight, position, amp, current, integrals, denominator
    )
    return new, residual


def solution(mesh):
    count = mesh.shape["pair"]
    devices = mesh.devices.reshape(mesh.shape["frag"], 2, count // 2)
    split_mesh = Mesh(devices, ("frag", "half", "near"))
    rows = ("frag", "half", "near")
    return jax.shard_map(
        on_device,
        mesh=split_mesh,
        in_specs=(
            P(rows, None), P(rows, None), P(rows, None), P(rows), P(rows, None),
            P(rows), P(rows, None), P(rows, None), P(rows, None, None), P(rows, None),
        ),
        out_specs=(P(rows, None), P(rows, None)),
        check_vma=False,
    )
```

time: 81.8 us -> 77.7 us (0.950)
  blocking collectives: 8.49 us -> 31.3 us
  starting transfers between devices: 19.6 us -> 7.9 us
  waiting for transfers between devices: 22.2 us -> 14.2 us
  Pallas kernels: 26.7 us -> 20.3 us
  other arithmetic: 1.8 us -> 0.91 us
    all_to_all x1 -> x2, blocking collectives: 8.49 us -> 31.3 us  [the longest x1 16.3 us: on_device(): amp = lax.all_to_all(amp, both, split_axis=0, concat_axis=0, tiled=True)]
    all_to_all x3 -> x1, starting transfers between devices: 12.7 us -> 3.71 us  [on_device(): lax.all_to_all(payload, 'near', split_axis=0, concat_axis=0, tiled=True)]
    ppermute x2 -> x1, waiting for transfers between devices: 6.99 us -> 0.01 us  [on_device(): far_logs = lax.ppermute(logs, 'half', swap)]
    pallas_call x5 -> x4, Pallas kernels: 24.7 us -> 18.4 us  [the longest x1 9.49 us: first_sweep(): pl.pallas_call(first_kernel, grid=(steps,), in_specs=[smem()] * 3 + [vmem...]
    ppermute x2 -> x1, starting transfers between devices: 2.73 us -> 0.09 us  [on_device(): far_logs = lax.ppermute(logs, 'half', swap)]
    all_to_all x3 -> x1, waiting for transfers between devices: 15.2 us -> 14.2 us  [on_device(): lax.all_to_all(payload, 'near', split_axis=0, concat_axis=0, tiled=True)]
    unnamed x20 -> x22, local copies, waits for them, and re-layouts: 0.05 us -> 1 us
  transfers between devices with their start and end apart: 6 -> 3, of which waited for: 4 -> 1; matrix products, arithmetic and copies ran while one was open for 3% -> 1% of each run, Pallas kernels for 13% -> 4%
where the time goes in v4:
time: 77.7 us; the launch traced here: 77.3 us
  blocking collectives  31.3 us (40%)
  Pallas kernels  20.3 us (26%)
  waiting for transfers between devices  14.2 us (18%)
  starting transfers between devices  7.9 us (10%)
  between operations  1.45 us (2%)
  local copies, waits for them, and re-layouts  1.16 us (1%)
  other arithmetic  0.91 us (1%)
    all_to_all x1, blocking collectives, on_device(): amp = lax.all_to_all(amp, both, split_axis=0, concat_axis=0, tiled=True)  16.3 us
    all_to_all x1, blocking collectives, gather(): return lax.all_to_all(rows, both, split_axis=0, concat_axis=0, tiled=True)  15.1 us
    all_to_all x1, waiting for transfers between devices, on_device(): lax.all_to_all(payload, 'near', split_axis=0, concat_axis=0, tiled=True)  14.2 us
    pallas_call x1, Pallas kernels, first_sweep(): pl.pallas_call(first_kernel, grid=(steps,), in_specs=[smem()] * 3 + [vmem...  9.49 us
    pallas_call x1, Pallas kernels, second_sweep(): pl.pallas_call(second_kernel, grid=(steps,), in_specs=[smem(), hbm(), vme...  5.72 us
    ppermute x1, starting transfers between devices, on_device(): far_pnos = lax.ppermute(pnos, 'half', swap)  4.1 us
    all_to_all x1, starting transfers between devices, on_device(): lax.all_to_all(payload, 'near', split_axis=0, concat_axis=0, tiled=True)  3.71 us
    pallas_call x1, Pallas kernels, prepare(): pl.pallas_call(prepare_kernel, in_specs=[vmem()] * 4, out_specs=[vmem()]...  1.93 us
  transfers between devices with their start and end apart: 3, of which 1 were waited for; matrix products, arithmetic and copies ran while one was open for 1% of the time, Pallas kernels for 4%

profile of v4, /device:TPU:0, one launch (start us, length us, event | category | flops | bytes accessed | tf_op | source)
XLA Modules:
  0.0 77.3 jit_solution(6598964491749985391)
XLA Ops:
  0.6 4.1 %collective-permute-start = (bf16[8,64,256]{2,1,0:T(8,128)(2,1)}, bf16[8,64,256]{2,1,0:T(8,128)(2,1)S(1)}, u32[]{:S(2)}, u32[]{:S(2)}) collective-permute-start(bf16[8,64,256]{2,1,0:T(8,128)(2,1)} %pnos_ref.3), channel_id=1, source_target_pairs={{0,8},{8,0},{1,9},{9,1},{2,10},{10,2},{3,11},{11,3},{4,12},{12,4},... | collective-permute-start | bytes 786440 | tf_op jit(solution)/shard_map/ppermute | solution.py:562
  4.7 1.2 %encode.1 = (bf16[8,32,128]{2,1,0:T(8,128)(2,1)S(1)}, s32[8,112]{1,0:T(8,128)S(1)}) custom-call(f32[8,4096]{1,0:T(8,128)} %amp_ref.1, s32[8,16]{1,0:T(8,128)} %domains_ref.1, s32[1,32]{1,0:T(1,128)} %request_ref.1), custom_call_target="tpu_custom_call" | custom-call | tf_op jit(solution)/shard_map/encode/pallas_call | solution.py:437
  6.0 0.1 collective-permute-start.1
  6.7 15.1 %conditional.1 = (s32[16,8,112]{2,1,0:T(8,128)S(1)}) conditional(s32[]{:T(128)} %bitcast.1, () %tuple.13, s32[8,112]{1,0:T(8,128)S(1)} %get-tuple-element.14), branch_computations={%region_0.0_spmd, %region_1.0_spmd} | conditional | bytes 175624 | solution.py:573
  6.8 15.1 %all_to_all.14 = s32[16,8,112]{2,1,0:T(8,128)S(1)} all-to-all(s32[16,8,112]{2,1,0:T(8,128)S(1)} %broadcast_in_dim.0), channel_id=1, replica_groups=mesh['frag'=2,'half'=2,'near'=8] {'half','near'}, dimensions={0} | all-to-all | bytes 114688 | tf_op jit(solution)/shard_map/cond/branch_1_fun/all_to_all | solution.py:568
  21.8 0.1 constant_dynamic-slice_fusion
  21.9 0.0 collective-permute-done.1.far_logs_ref
  21.9 0.0 collective-permute-done.far_pnos_ref
  21.9 0.0 copy-start
  21.9 0.9 %copy-done = bf16[8,64,256]{2,1,0:T(8,128)(2,1)S(1)} copy-done((bf16[8,64,256]{2,1,0:T(8,128)(2,1)S(1)}, bf16[8,64,256]{2,1,0:T(8,128)(2,1)}, u32[]{:S(2)}) %copy-start) | copy-done | bytes 262168
  22.9 1.9 %pack_payload.1 = bf16[8,2,160,256]{3,2,1,0:T(8,128)(2,1)} custom-call(s32[8,2]{1,0:T(8,128)S(1)} %bitcast.10, s32[8,2]{1,0:T(8,128)S(1)} %bitcast.9, bf16[8,64,256]{2,1,0:T(8,128)(2,1)S(1)} %copy-done, bf16[8,32,128]{2,1,0:T(8,128)(2,1)S(1)} %get-tuple-element.16.logs_ref, bf16[8,64,256]{2,1,0:T(8,128)(2,1)S(1)} %collective-permute-done.far_pnos_ref, ...), custom_call_target="tpu_custom_call" | custom-call | tf_op jit(solution)/shard_map/pack_payload/pallas_call | solution.py:458
  24.8 0.0 copy-start.8
  24.8 0.0 copy-start.10
  24.8 0.0 copy-start.7
  24.8 0.0 copy-start.9
  24.8 0.0 copy-start.5
  24.8 0.0 copy-start.6
  24.9 3.7 %all-to-all-start.1 = ((bf16[8,2,160,256]{3,2,1,0:T(8,128)(2,1)}), bf16[8,2,160,256]{3,2,1,0:T(8,128)(2,1)S(1)}, u32[]{:S(2)}, u32[]{:S(2)}) async-start(bf16[8,2,160,256]{3,2,1,0:T(8,128)(2,1)} %pack_payload.1), calls=%async_computation.1 | async-start | bytes 2621440 | tf_op jit(solution)/shard_map/all_to_all | solution.py:584
  28.6 0.0 copy-done.1
  28.6 0.0 copy-done.2
  28.6 0.0 copy-done.3
  28.6 1.9 %prepare.1 = (bf16[512,512]{1,0:T(8,128)(2,1)}, f32[512,64]{1,0:T(8,128)}, f32[512,64]{1,0:T(8,128)}) custom-call(bf16[8,64,256]{2,1,0:T(8,128)(2,1)S(1)} %copy-done.1, s32[8,16]{1,0:T(8,128)S(1)} %copy-done.4, f32[8,4096]{1,0:T(8,128)S(1)} %copy-done.2, f32[8,4096]{1,0:T(8,128)S(1)} %copy-done.3), custom_call_target="tpu_custom_call" | custom-call | tf_op jit(solution)/shard_map/prepare/pallas_call | solution.py:420
  30.6 0.1 constant_dynamic-slice_fusion.2
  30.6 0.0 copy-done.10
  30.6 0.1 fusion.weight_ref
  30.7 0.0 copy-done.9
  30.7 0.8 %add_subtract_fusion.denominator_hbm = f32[8,64,64]{2,1,0:T(8,128)} fusion(f32[8]{0:T(128)S(1)} %copy-done.9, f32[8,64]{1,0:T(8,128)S(1)} %copy-done.7), kind=kLoop, calls=%fused_computation | loop fusion | flops 65536 | bytes 133152 | tf_op jit(solution)/shard_map/sub | solution.py:589
  31.6 14.2 %all-to-all-done.1 = bf16[8,2,160,256]{3,2,1,0:T(8,128)(2,1)S(1)} async-done(((bf16[8,2,160,256]{3,2,1,0:T(8,128)(2,1)}), bf16[8,2,160,256]{3,2,1,0:T(8,128)(2,1)S(1)}, u32[]{:S(2)}, u32[]{:S(2)}) %all-to-all-start.1) | async-done | bytes 1310752 | tf_op jit(solution)/shard_map/all_to_all | solution.py:584
  45.8 0.0 copy-done.5
  45.8 9.5 %first_sweep.1 = (bf16[4,8,128,512]{3,2,1,0:T(8,128)(2,1)}, f32[512,64]{1,0:T(8,128)}, s16[16,80,128]{2,1,0:T(8,128)(2,1)}) custom-call(s32[1]{0:T(128)} %bitcast.half_ref, s32[1,32]{1,0:T(1,128)S(1)} %copy-done.6, s32[16,2]{1,0:T(8,128)S(1)} %bitcast.8, s32[16,8,112]{2,1,0:T(8,128)S(1)} %get-tuple-element.24.table_ref, ...), custom_call_target="tpu_custom_call" | custom-call | tf_op jit(solution)/shard_map/first_sweep/pallas_call | solution.py:489
  55.3 16.3 %all_to_all.15.amp_ref = s16[16,80,128]{2,1,0:T(8,128)(2,1)S(1)} all-to-all(s16[16,80,128]{2,1,0:T(8,128)(2,1)} %get-tuple-element.20), channel_id=1, replica_groups=mesh['frag'=2,'half'=2,'near'=8] {'half','near'}, dimensions={0} | all-to-all | bytes 655360 | tf_op jit(solution)/shard_map/all_to_all | solution.py:596
  71.5 5.7 %second_sweep.1 = (f32[8,4096]{1,0:T(8,128)}, f32[8,4096]{1,0:T(8,128)}) custom-call(s32[1]{0:T(128)} %bitcast.half_ref, bf16[4,8,128,512]{3,2,1,0:T(8,128)(2,1)} %get-tuple-element.19.cat_hbm, f32[8,16]{1,0:T(8,128)S(1)} %fusion.weight_ref, s32[8,16]{1,0:T(8,128)S(1)} %copy-done.5, s16[16,80,128]{2,1,0:T(8,128)(2,1)S(1)} %all_to_all.15.amp_ref, ...), custom_call_target="tpu_custom_call" | custom-call | tf_op jit(solution)/shard_map/second_sweep/pallas_call | solution.py:526
  (9 shorter events, 0.0 us)
Async XLA Ops:
  0.6 21.3 %collective-permute-start = (bf16[8,64,256]{2,1,0:T(8,128)(2,1)}, bf16[8,64,256]{2,1,0:T(8,128)(2,1)S(1)}, u32[]{:S(2)}, u32[]{:S(2)}) collective-permute-start(bf16[8,64,256]{2,1,0:T(8,128)(2,1)} %pnos_ref.3), channel_id=1, source_target_pairs={{0,8},{8,0},{1,9},{9,1},{2,10},{10,2},{3,11},{11,3},{4,12},{12,4},... | collective-permute-start | bytes 786440 | tf_op jit(solution)/shard_map/ppermute | solution.py:562
  6.0 15.9 %collective-permute-start.1 = (bf16[8,32,128]{2,1,0:T(8,128)(2,1)S(1)}, bf16[8,32,128]{2,1,0:T(8,128)(2,1)S(1)}, u32[]{:S(2)}, u32[]{:S(2)}) collective-permute-start(bf16[8,32,128]{2,1,0:T(8,128)(2,1)S(1)} %get-tuple-element.16.logs_ref), channel_id=1, source_target_pairs={{0,8},{8,0},{1,9},{9,1},{2,10},{10,2},{3,11},{11,3},{4,12},{12,4},... | collective-permute-start | bytes 196616 | tf_op jit(solution)/shard_map/ppermute | solution.py:564
  21.9 1.0 %copy-start = (bf16[8,64,256]{2,1,0:T(8,128)(2,1)S(1)}, bf16[8,64,256]{2,1,0:T(8,128)(2,1)}, u32[]{:S(2)}) copy-start(bf16[8,64,256]{2,1,0:T(8,128)(2,1)} %pnos_ref.3) | copy-start | bytes 786436
  24.8 3.8 %copy-start.1 = (bf16[8,64,256]{2,1,0:T(8,128)(2,1)S(1)}, bf16[8,64,256]{2,1,0:T(8,128)(2,1)}, u32[]{:S(2)}) copy-start(bf16[8,64,256]{2,1,0:T(8,128)(2,1)} %pnos_ref.3) | copy-start | bytes 786436
  24.8 3.8 %copy-start.2 = (f32[8,4096]{1,0:T(8,128)S(1)}, f32[8,4096]{1,0:T(8,128)}, u32[]{:S(2)}) copy-start(f32[8,4096]{1,0:T(8,128)} %amp_ref.1) | copy-start | bytes 393220
  24.8 3.8 %copy-start.3 = (f32[8,4096]{1,0:T(8,128)S(1)}, f32[8,4096]{1,0:T(8,128)}, u32[]{:S(2)}) copy-start(f32[8,4096]{1,0:T(8,128)} %integrals_ref.1) | copy-start | bytes 393220
  24.8 3.8 %copy-start.4 = (s32[8,16]{1,0:T(8,128)S(1)}, s32[8,16]{1,0:T(8,128)}, u32[]{:S(2)}) copy-start(s32[8,16]{1,0:T(8,128)} %domains_ref.1) | copy-start | bytes 1540
  24.8 5.8 %copy-start.8 = (f32[8,16]{1,0:T(8,128)S(1)}, f32[8,16]{1,0:T(8,128)}, u32[]{:S(2)}) copy-start(f32[8,16]{1,0:T(8,128)} %param.16) | copy-start | bytes 1540
  24.8 5.8 %copy-start.10 = (s32[8]{0:T(128)S(1)}, s32[8]{0:T(128)}, u32[]{:S(2)}) copy-start(s32[8]{0:T(128)} %param.17) | copy-start | bytes 100
  24.8 5.9 %copy-start.7 = (f32[8,64]{1,0:T(8,128)S(1)}, f32[8,64]{1,0:T(8,128)}, u32[]{:S(2)}) copy-start(f32[8,64]{1,0:T(8,128)} %param.14) | copy-start | bytes 6148
  24.8 5.9 %copy-start.9 = (f32[8]{0:T(128)S(1)}, f32[8]{0:T(128)}, u32[]{:S(2)}) copy-start(f32[8]{0:T(128)} %param.15) | copy-start | bytes 100
  24.8 20.9 %copy-start.5 = (s32[8,16]{1,0:T(8,128)S(1)}, s32[8,16]{1,0:T(8,128)}, u32[]{:S(2)}) copy-start(s32[8,16]{1,0:T(8,128)} %position_ref.3) | copy-start | bytes 1540
  24.8 20.9 %copy-start.6 = (s32[1,32]{1,0:T(1,128)S(1)}, s32[1,32]{1,0:T(1,128)}, u32[]{:S(2)}) copy-start(s32[1,32]{1,0:T(1,128)} %request_ref.1) | copy-start | bytes 388
  24.9 20.9 %all-to-all-start.1 = ((bf16[8,2,160,256]{3,2,1,0:T(8,128)(2,1)}), bf16[8,2,160,256]{3,2,1,0:T(8,128)(2,1)S(1)}, u32[]{:S(2)}, u32[]{:S(2)}) async-start(bf16[8,2,160,256]{3,2,1,0:T(8,128)(2,1)} %pack_payload.1), calls=%async_computation.1 | async-start | bytes 2621440 | tf_op jit(solution)/shard_map/all_to_all | solution.py:584

commit v5 on v4

--- a/solution.py
+++ b/solution.py
@@ -11,7 +11,6 @@
 LOG_TOP = 125.0
 CODE_TOP = 32767.0
 CODE_ROWS = 16
-AHEAD = 2
 SMALLEST = 2.0**-100
 VMEM_LIMIT = 32 * 1024 * 1024
 NT = (((1,), (1,)), ((), ()))
@@ -84,10 +83,10 @@
 def column_table(atoms, columns):
     width = atoms.shape[1]
     per_atom = columns // ATOMS
-    row = lax.broadcasted_iota(jnp.int32, (columns, width), 0)
+    row = lax.broadcasted_iota(jnp.int32, (columns, width), 0).astype(jnp.int16)
     column = lax.broadcasted_iota(jnp.int32, (1, width), 1)
-    ids = atoms.astype(jnp.int32) * per_atom + column % per_atom
-    return (row == ids).astype(jnp.float32).astype(jnp.bfloat16)
+    ids = (atoms.astype(jnp.int32) * per_atom + column % per_atom).astype(jnp.int16)
+    return jnp.where(row == ids, jnp.ones((), jnp.bfloat16), jnp.zeros((), jnp.bfloat16))
 
 
 def prepare_kernel(
@@ -229,10 +228,9 @@
 
 
 def first_kernel(
-    half_ref, request_ref, wanted_ref, table_ref, own_hbm, payload_ref, weight_ref, position_ref,
-    current_hbm, integrals_hbm, denominator_hbm, cat_hbm, new_hbm, send_hbm, own_ref, cat_ref,
-    full_ref, left_ref, acc_ref, info_ref, current_ref, integrals_ref, denominator_ref, send_ref,
-    even_ref, odd_ref, sem_ref, cat_sem_ref,
+    half_ref, request_ref, wanted_ref, table_ref, own_ref, payload_ref, weight_ref, position_ref,
+    current_ref, integrals_ref, denominator_ref, cat_ref, new_ref, send_hbm, full_ref, left_ref,
+    acc_ref, info_ref, send_ref, even_ref, odd_ref, sem_ref,
 ):
     pairs, size, unused = denominator_ref.shape
     width = payload_ref.shape[2]
@@ -241,21 +239,6 @@
     half = half_ref[0]
     step = pl.program_id(0)
     count = table_ref.shape[2] - size - request_ref.shape[1]
-    fetches = [
-        pltpu.make_async_copy(hbm, ref, sem_ref.at[i])
-        for i, (hbm, ref) in enumerate(
-            (
-                (own_hbm, own_ref), (current_hbm, current_ref), (integrals_hbm, integrals_ref),
-                (denominator_hbm, denominator_ref),
-            )
-        )
-    ]
-
-    @pl.when(step == 0)
-    def fetch():
-        for copy in fetches:
-            copy.start()
-
     entries = CHUNK * chunks
     lanes = table_ref.shape[2]
     for k in range(2 * entries):
@@ -267,22 +250,12 @@
     moved = pltpu.roll(scales, size, 1)
     left_lanes = lax.broadcasted_iota(jnp.int32, (1, 2 * size), 1) < size
 
-    @pl.when(step == 0)
-    def own_ready():
-        fetches[0].wait()
-
-    cat_copies = []
     for c in range(chunks):
         blocks = payload_ref.at[pl.ds(c * CHUNK, CHUNK)]
         cross_chunk(
             atoms[c * 2 * CHUNK : (c + 1) * 2 * CHUNK], own_ref, blocks, cat_ref.at[c],
             full_ref.at[c],
         )
-        copy = pltpu.make_async_copy(
-            cat_ref.at[c], cat_hbm.at[step * chunks + c], cat_sem_ref.at[c]
-        )
-        copy.start()
-        cat_copies.append(copy)
         start = step * entries + c * CHUNK
         weights = slot_weights(half, near, start, weight_ref, position_ref, size)
 
@@ -297,14 +270,12 @@
 
     @pl.when(step == pl.num_programs(0) - 1)
     def finish():
-        for copy in fetches[1:]:
-            copy.wait()
         for s in range(pairs):
             rows = slice(s * size, (s + 1) * size)
             current, denominator = current_ref[rows, :], denominator_ref[s]
             residual = integrals_ref[rows, :] + denominator * current - coupled_of(acc_ref[s])
             new = current - residual / denominator
-            current_ref[rows, :] = new
+            new_ref[rows, :] = new
             store_codes(new, even_ref, odd_ref, s)
 
         def pack(d, carry):
@@ -312,58 +283,23 @@
             return carry
 
         lax.fori_loop(0, send_ref.shape[0], pack, 0)
-        copies = [
-            pltpu.make_async_copy(send_ref, send_hbm, sem_ref.at[0]),
-            pltpu.make_async_copy(current_ref, new_hbm, sem_ref.at[1]),
-        ]
-        for copy in copies:
-            copy.start()
-        for copy in copies:
-            copy.wait()
-
-    for copy in cat_copies:
+        copy = pltpu.make_async_copy(send_ref, send_hbm, sem_ref.at[0])
+        copy.start()
         copy.wait()
 
 
 def second_kernel(
-    half_ref, cat_hbm, weight_ref, position_ref, amp_ref, current_hbm, integrals_hbm,
-    denominator_hbm, new_ref, residual_ref, cat_ref, left_ref, acc_ref, current_ref,
-    integrals_ref, denominator_ref, new_rows_ref, residual_rows_ref, sem_ref, cat_sem_ref,
+    half_ref, cat_ref, weight_ref, position_ref, amp_ref, current_ref, integrals_ref,
+    denominator_ref, new_ref, residual_ref, left_ref, acc_ref, new_rows_ref, residual_rows_ref,
 ):
     pairs, size, unused = denominator_ref.shape
     step = pl.program_id(0)
     half = half_ref[0]
     near = amp_ref.shape[0] // 2
     chunks = cat_ref.shape[0]
-    fetches = [
-        pltpu.make_async_copy(hbm, ref, sem_ref.at[i])
-        for i, (hbm, ref) in enumerate(
-            (
-                (current_hbm, current_ref), (integrals_hbm, integrals_ref),
-                (denominator_hbm, denominator_ref),
-            )
-        )
-    ]
-    copies = [
-        pltpu.make_async_copy(
-            cat_hbm.at[step * chunks + c], cat_ref.at[c], cat_sem_ref.at[c]
-        )
-        for c in range(chunks)
-    ]
-    for copy in copies[:AHEAD]:
-        copy.start()
     for c in range(chunks):
         start = (step * chunks + c) * CHUNK
         weights = slot_weights(half, near, start, weight_ref, position_ref, size)
-        copies[c].wait()
-        if c + AHEAD < chunks:
-            copies[c + AHEAD].start()
-        elif c + AHEAD == chunks or c == chunks - 1 and chunks < AHEAD:
-            @pl.when(step == pl.num_programs(0) - 1)
-            def fetch():
-                for copy in fetches:
-                    copy.start()
-
         half_products(
             weights, lambda j: block_of_codes(amp_ref[source_of(start + j, half, near)]),
             cat_ref.at[c], left_ref.at[c],
@@ -372,8 +308,6 @@
 
     @pl.when(step == pl.num_programs(0) - 1)
     def finish():
-        for copy in fetches:
-            copy.wait()
         for s in range(pairs):
             rows = slice(s * size, (s + 1) * size)
             current, denominator = current_ref[rows, :], denominator_ref[s]
@@ -422,8 +356,8 @@
         in_specs=[vmem()] * 4,
         out_specs=[vmem()] * 3,
         out_shape=[
-            pltpu.HBM(own, jnp.bfloat16), pltpu.HBM(block, jnp.float32),
-            pltpu.HBM(block, jnp.float32),
+            jax.ShapeDtypeStruct(own, jnp.bfloat16), jax.ShapeDtypeStruct(block, jnp.float32),
+            jax.ShapeDtypeStruct(block, jnp.float32),
         ],
         scratch_shapes=[pltpu.VMEM((pairs, width), jnp.float32)],
         compiler_params=limit(),
@@ -476,6 +410,12 @@
     return cat[0] // chunks, chunks, cat, scratch
 
 
+def cat_spec(steps, chunks, cat):
+    if steps == 1:
+        return vmem()
+    return pl.BlockSpec((chunks,) + cat[1:], lambda i: (i, 0, 0, 0))
+
+
 def first_sweep(
     half, request, wanted, table, own, payload, weight, position, current, integrals, denominator
 ):
@@ -484,64 +424,55 @@
     steps, chunks, cat, (cats, lefts, acc) = sweep_shapes(entries, pairs, size)
     block = (CHUNK * chunks, rows, width)
     blocks = vmem() if steps == 1 else pl.BlockSpec(block, lambda i: (i, 0, 0))
+    kept = cat_spec(steps, chunks, cat)
     parts = (pairs, size + CODE_ROWS, 2 * size)
     send = (entries,) + parts[1:]
     return pl.pallas_call(
         first_kernel,
         grid=(steps,),
-        in_specs=[smem()] * 3 + [vmem(), hbm(), blocks, vmem(), vmem()] + [hbm()] * 3,
-        out_specs=[hbm()] * 3,
+        in_specs=[smem()] * 3 + [vmem(), vmem(), blocks] + [vmem()] * 5,
+        out_specs=[kept, vmem(), hbm()],
         out_shape=[
-            pltpu.HBM(cat, jnp.bfloat16), pltpu.HBM(current.shape, jnp.float32),
+            jax.ShapeDtypeStruct(cat, jnp.bfloat16),
+            jax.ShapeDtypeStruct(current.shape, jnp.float32),
             pltpu.HBM(send, jnp.int16),
         ],
         scratch_shapes=[
-            pltpu.VMEM(own.shape, jnp.bfloat16),
-            cats,
             pltpu.VMEM((chunks, cat[3], own.shape[1]), jnp.bfloat16),
             lefts,
             acc,
             pltpu.VMEM((2 * CHUNK * chunks, max(table.shape[2], 2 * size)), jnp.int32),
-            pltpu.VMEM(current.shape, jnp.float32),
-            pltpu.VMEM(current.shape, jnp.float32),
-            pltpu.VMEM(denominator.shape, jnp.float32),
             pltpu.VMEM(send, jnp.int16),
             pltpu.VMEM(parts, jnp.int16),
             pltpu.VMEM(parts, jnp.int16),
-            pltpu.SemaphoreType.DMA((4,)),
-            pltpu.SemaphoreType.DMA((chunks,)),
+            pltpu.SemaphoreType.DMA((1,)),
         ],
         compiler_params=params(),
         name="first_sweep",
     )(
-        half, request, wanted, table, *in_hbm(own), payload, weight, position,
-        *in_hbm(current, integrals, denominator),
+        half, request, wanted, table, own, payload, weight, position, current, integrals,
+        denominator,
     )
 
 
 def second_sweep(half, cat, weight, position, amp, current, integrals, denominator):
     pairs, size, unused = denominator.shape
-    steps, chunks, unused, scratch = sweep_shapes(amp.shape[0], pairs, size)
+    steps, chunks, shape, scratch = sweep_shapes(amp.shape[0], pairs, size)
     flat = (pairs, size * size)
     return pl.pallas_call(
         second_kernel,
         grid=(steps,),
-        in_specs=[smem(), hbm(), vmem(), vmem(), vmem(), hbm(), hbm(), hbm()],
+        in_specs=[smem(), cat_spec(steps, chunks, shape)] + [vmem()] * 6,
         out_specs=[vmem(), vmem()],
         out_shape=[jax.ShapeDtypeStruct(flat, jnp.float32)] * 2,
-        scratch_shapes=scratch + [
+        scratch_shapes=scratch[1:] + [
             pltpu.VMEM(current.shape, jnp.float32),
             pltpu.VMEM(current.shape, jnp.float32),
-            pltpu.VMEM(denominator.shape, jnp.float32),
-            pltpu.VMEM(current.shape, jnp.float32),
-            pltpu.VMEM(current.shape, jnp.float32),
-            pltpu.SemaphoreType.DMA((3,)),
-            pltpu.SemaphoreType.DMA((chunks,)),
         ],
         compiler_params=params(),
         name="second_sweep",
     )(
-        half, *in_hbm(cat), weight, position, amp, *in_hbm(current, integrals, denominator),
+        half, cat, weight, position, amp, current, integrals, denominator
     )
 
 

time: 77.7 us -> 74.1 us (0.954)
  Pallas kernels: 20.3 us -> 15.8 us
  waiting for transfers between devices: 14.2 us -> 15.8 us
    pallas_call x1, Pallas kernels: 5.72 us -> 3.57 us  [second_sweep(): pl.pallas_call(second_kernel, grid=(steps,), in_specs=[smem(), cat_spec(s...]
    all_to_all x1, waiting for transfers between devices: 14.2 us -> 15.8 us  [on_device(): lax.all_to_all(payload, 'near', split_axis=0, concat_axis=0, tiled=True)]
    pallas_call x1, Pallas kernels: 9.49 us -> 8.08 us  [first_sweep(): pl.pallas_call(first_kernel, grid=(steps,), in_specs=[smem()] * 3 + [vmem...]
    pallas_call x1, Pallas kernels: 1.93 us -> 1.03 us  [prepare(): pl.pallas_call(prepare_kernel, in_specs=[vmem()] * 4, out_specs=[vmem()]...]
  transfers between devices with their start and end apart: 3 -> 3, of which waited for: 1 -> 1; matrix products, arithmetic and copies ran while one was open for 1% -> 1% of each run, Pallas kernels for 4% -> 3%
where the time goes in v5:
time: 74.1 us; the launch traced here: 73.7 us
  blocking collectives  31.3 us (42%)
  Pallas kernels  15.8 us (21%)
  waiting for transfers between devices  15.8 us (21%)
  starting transfers between devices  7.9 us (11%)
  between operations  1.46 us (2%)
  local copies, waits for them, and re-layouts  1.16 us (2%)
    all_to_all x1, blocking collectives, on_device(): amp = lax.all_to_all(amp, both, split_axis=0, concat_axis=0, tiled=True)  16.3 us
    all_to_all x1, waiting for transfers between devices, on_device(): lax.all_to_all(payload, 'near', split_axis=0, concat_axis=0, tiled=True)  15.8 us
    all_to_all x1, blocking collectives, gather(): return lax.all_to_all(rows, both, split_axis=0, concat_axis=0, tiled=True)  15.1 us
    pallas_call x1, Pallas kernels, first_sweep(): pl.pallas_call(first_kernel, grid=(steps,), in_specs=[smem()] * 3 + [vmem...  8.08 us
    ppermute x1, starting transfers between devices, on_device(): far_pnos = lax.ppermute(pnos, 'half', swap)  4.1 us
    all_to_all x1, starting transfers between devices, on_device(): lax.all_to_all(payload, 'near', split_axis=0, concat_axis=0, tiled=True)  3.71 us
    pallas_call x1, Pallas kernels, second_sweep(): pl.pallas_call(second_kernel, grid=(steps,), in_specs=[smem(), cat_spec(s...  3.57 us
    pallas_call x1, Pallas kernels, pack_payload(): pl.pallas_call(pack_kernel, in_specs=[smem(), smem()] + [vmem()] * 4, out...  1.9 us
  transfers between devices with their start and end apart: 3, of which 1 were waited for; matrix products, arithmetic and copies ran while one was open for 1% of the time, Pallas kernels for 3%

profile of v5, /device:TPU:0, one launch (start us, length us, event | category | flops | bytes accessed | tf_op | source)
XLA Modules:
  0.0 73.7 jit_solution(10570427416043521118)
XLA Ops:
  0.6 4.1 %collective-permute-start = (bf16[8,64,256]{2,1,0:T(8,128)(2,1)}, bf16[8,64,256]{2,1,0:T(8,128)(2,1)S(1)}, u32[]{:S(2)}, u32[]{:S(2)}) collective-permute-start(bf16[8,64,256]{2,1,0:T(8,128)(2,1)} %pnos_ref.3), channel_id=1, source_target_pairs={{0,8},{8,0},{1,9},{9,1},{2,10},{10,2},{3,11},{11,3},{4,12},{12,4},... | collective-permute-start | bytes 786440 | tf_op jit(solution)/shard_map/ppermute | solution.py:493
  4.7 1.2 %encode.1 = (bf16[8,32,128]{2,1,0:T(8,128)(2,1)S(1)}, s32[8,112]{1,0:T(8,128)S(1)}) custom-call(f32[8,4096]{1,0:T(8,128)} %amp_ref.1, s32[8,16]{1,0:T(8,128)} %domains_ref.1, s32[1,32]{1,0:T(1,128)} %request_ref.1), custom_call_target="tpu_custom_call" | custom-call | tf_op jit(solution)/shard_map/encode/pallas_call | solution.py:371
  6.0 0.1 collective-permute-start.1
  6.7 15.1 %conditional.1 = (s32[16,8,112]{2,1,0:T(8,128)S(1)}) conditional(s32[]{:T(128)} %bitcast.1, () %tuple.13, s32[8,112]{1,0:T(8,128)S(1)} %get-tuple-element.14), branch_computations={%region_0.0_spmd, %region_1.0_spmd} | conditional | bytes 175624 | solution.py:504
  6.8 15.1 %all_to_all.14 = s32[16,8,112]{2,1,0:T(8,128)S(1)} all-to-all(s32[16,8,112]{2,1,0:T(8,128)S(1)} %broadcast_in_dim.0), channel_id=1, replica_groups=mesh['frag'=2,'half'=2,'near'=8] {'half','near'}, dimensions={0} | all-to-all | bytes 114688 | tf_op jit(solution)/shard_map/cond/branch_1_fun/all_to_all | solution.py:499
  21.8 0.1 constant_dynamic-slice_fusion
  21.9 0.0 collective-permute-done.1.far_logs_ref
  21.9 0.0 collective-permute-done.far_pnos_ref
  21.9 0.0 copy-start
  21.9 0.9 %copy-done = bf16[8,64,256]{2,1,0:T(8,128)(2,1)S(1)} copy-done((bf16[8,64,256]{2,1,0:T(8,128)(2,1)S(1)}, bf16[8,64,256]{2,1,0:T(8,128)(2,1)}, u32[]{:S(2)}) %copy-start) | copy-done | bytes 262168
  22.9 1.9 %pack_payload.1 = bf16[8,2,160,256]{3,2,1,0:T(8,128)(2,1)} custom-call(s32[8,2]{1,0:T(8,128)S(1)} %bitcast.10, s32[8,2]{1,0:T(8,128)S(1)} %bitcast.9, bf16[8,64,256]{2,1,0:T(8,128)(2,1)S(1)} %copy-done, bf16[8,32,128]{2,1,0:T(8,128)(2,1)S(1)} %get-tuple-element.16.logs_ref, bf16[8,64,256]{2,1,0:T(8,128)(2,1)S(1)} %collective-permute-done.far_pnos_ref, ...), custom_call_target="tpu_custom_call" | custom-call | tf_op jit(solution)/shard_map/pack_payload/pallas_call | solution.py:392
  24.8 0.0 copy-start.8
  24.8 0.0 copy-start.10
  24.8 0.0 copy-start.7
  24.8 0.0 copy-start.9
  24.8 0.0 copy-start.5
  24.8 0.0 copy-start.6
  24.9 3.7 %all-to-all-start.1 = ((bf16[8,2,160,256]{3,2,1,0:T(8,128)(2,1)}), bf16[8,2,160,256]{3,2,1,0:T(8,128)(2,1)S(1)}, u32[]{:S(2)}, u32[]{:S(2)}) async-start(bf16[8,2,160,256]{3,2,1,0:T(8,128)(2,1)} %pack_payload.1), calls=%async_computation.1 | async-start | bytes 2621440 | tf_op jit(solution)/shard_map/all_to_all | solution.py:515
  28.6 0.0 copy-done.1
  28.6 0.0 copy-done.2
  28.6 0.0 copy-done.3
  28.6 0.0 copy-done.4
  28.6 1.0 %prepare.1 = (bf16[512,512]{1,0:T(8,128)(2,1)S(1)}, f32[512,64]{1,0:T(8,128)S(1)}, f32[512,64]{1,0:T(8,128)S(1)}) custom-call(bf16[8,64,256]{2,1,0:T(8,128)(2,1)S(1)} %copy-done.1, s32[8,16]{1,0:T(8,128)S(1)} %copy-done.4, f32[8,4096]{1,0:T(8,128)S(1)} %copy-done.2, f32[8,4096]{1,0:T(8,128)S(1)} %copy-done.3), custom_call_target="tpu_custom_call" | custom-call | tf_op jit(solution)/shard_map/prepare/pallas_call | solution.py:354
  29.7 0.1 constant_dynamic-slice_fusion.2
  29.7 0.0 copy-done.10
  29.8 0.1 fusion.weight_ref
  29.8 0.0 copy-done.9
  29.8 0.1 add_subtract_fusion.denominator_ref
  30.0 15.8 %all-to-all-done.1 = bf16[8,2,160,256]{3,2,1,0:T(8,128)(2,1)S(1)} async-done(((bf16[8,2,160,256]{3,2,1,0:T(8,128)(2,1)}), bf16[8,2,160,256]{3,2,1,0:T(8,128)(2,1)S(1)}, u32[]{:S(2)}, u32[]{:S(2)}) %all-to-all-start.1) | async-done | bytes 1310752 | tf_op jit(solution)/shard_map/all_to_all | solution.py:515
  45.8 8.1 %first_sweep.1 = (bf16[4,8,128,512]{3,2,1,0:T(8,128)(2,1)S(1)}, f32[512,64]{1,0:T(8,128)S(1)}, s16[16,80,128]{2,1,0:T(8,128)(2,1)}) custom-call(s32[1]{0:T(128)} %bitcast.half_ref, s32[1,32]{1,0:T(1,128)S(1)} %copy-done.6, s32[16,2]{1,0:T(8,128)S(1)} %bitcast.8, s32[16,8,112]{2,1,0:T(8,128)S(1)} %get-tuple-element.24.table_ref, ...), custom_call_target="tpu_custom_call" | custom-call | tf_op jit(solution)/shard_map/first_sweep/pallas_call | solution.py:430
  53.9 16.3 %all_to_all.15.amp_ref = s16[16,80,128]{2,1,0:T(8,128)(2,1)S(1)} all-to-all(s16[16,80,128]{2,1,0:T(8,128)(2,1)} %get-tuple-element.20), channel_id=1, replica_groups=mesh['frag'=2,'half'=2,'near'=8] {'half','near'}, dimensions={0} | all-to-all | bytes 655360 | tf_op jit(solution)/shard_map/all_to_all | solution.py:527
  70.1 3.6 %second_sweep.1 = (f32[8,4096]{1,0:T(8,128)}, f32[8,4096]{1,0:T(8,128)}) custom-call(s32[1]{0:T(128)} %bitcast.half_ref, bf16[4,8,128,512]{3,2,1,0:T(8,128)(2,1)S(1)} %get-tuple-element.19.cat_ref, f32[8,16]{1,0:T(8,128)S(1)} %fusion.weight_ref, s32[8,16]{1,0:T(8,128)S(1)} %copy-done.5, s16[16,80,128]{2,1,0:T(8,128)(2,1)S(1)} %all_to_all.15.amp_ref, ...), custom_call_target="tpu_custom_call" | custom-call | tf_op jit(solution)/shard_map/second_sweep/pallas_call | solution.py:462
  (9 shorter events, 0.0 us)
Async XLA Ops:
  0.6 21.3 %collective-permute-start = (bf16[8,64,256]{2,1,0:T(8,128)(2,1)}, bf16[8,64,256]{2,1,0:T(8,128)(2,1)S(1)}, u32[]{:S(2)}, u32[]{:S(2)}) collective-permute-start(bf16[8,64,256]{2,1,0:T(8,128)(2,1)} %pnos_ref.3), channel_id=1, source_target_pairs={{0,8},{8,0},{1,9},{9,1},{2,10},{10,2},{3,11},{11,3},{4,12},{12,4},... | collective-permute-start | bytes 786440 | tf_op jit(solution)/shard_map/ppermute | solution.py:493
  6.0 15.9 %collective-permute-start.1 = (bf16[8,32,128]{2,1,0:T(8,128)(2,1)S(1)}, bf16[8,32,128]{2,1,0:T(8,128)(2,1)S(1)}, u32[]{:S(2)}, u32[]{:S(2)}) collective-permute-start(bf16[8,32,128]{2,1,0:T(8,128)(2,1)S(1)} %get-tuple-element.16.logs_ref), channel_id=1, source_target_pairs={{0,8},{8,0},{1,9},{9,1},{2,10},{10,2},{3,11},{11,3},{4,12},{12,4},... | collective-permute-start | bytes 196616 | tf_op jit(solution)/shard_map/ppermute | solution.py:495
  21.9 1.0 %copy-start = (bf16[8,64,256]{2,1,0:T(8,128)(2,1)S(1)}, bf16[8,64,256]{2,1,0:T(8,128)(2,1)}, u32[]{:S(2)}) copy-start(bf16[8,64,256]{2,1,0:T(8,128)(2,1)} %pnos_ref.3) | copy-start | bytes 786436
  24.8 3.8 %copy-start.1 = (bf16[8,64,256]{2,1,0:T(8,128)(2,1)S(1)}, bf16[8,64,256]{2,1,0:T(8,128)(2,1)}, u32[]{:S(2)}) copy-start(bf16[8,64,256]{2,1,0:T(8,128)(2,1)} %pnos_ref.3) | copy-start | bytes 786436
  24.8 3.8 %copy-start.2 = (f32[8,4096]{1,0:T(8,128)S(1)}, f32[8,4096]{1,0:T(8,128)}, u32[]{:S(2)}) copy-start(f32[8,4096]{1,0:T(8,128)} %amp_ref.1) | copy-start | bytes 393220
  24.8 3.8 %copy-start.3 = (f32[8,4096]{1,0:T(8,128)S(1)}, f32[8,4096]{1,0:T(8,128)}, u32[]{:S(2)}) copy-start(f32[8,4096]{1,0:T(8,128)} %integrals_ref.1) | copy-start | bytes 393220
  24.8 3.8 %copy-start.4 = (s32[8,16]{1,0:T(8,128)S(1)}, s32[8,16]{1,0:T(8,128)}, u32[]{:S(2)}) copy-start(s32[8,16]{1,0:T(8,128)} %domains_ref.1) | copy-start | bytes 1540
  24.8 4.9 %copy-start.8 = (f32[8,16]{1,0:T(8,128)S(1)}, f32[8,16]{1,0:T(8,128)}, u32[]{:S(2)}) copy-start(f32[8,16]{1,0:T(8,128)} %param.16) | copy-start | bytes 1540
  24.8 4.9 %copy-start.10 = (s32[8]{0:T(128)S(1)}, s32[8]{0:T(128)}, u32[]{:S(2)}) copy-start(s32[8]{0:T(128)} %param.17) | copy-start | bytes 100
  24.8 5.0 %copy-start.7 = (f32[8,64]{1,0:T(8,128)S(1)}, f32[8,64]{1,0:T(8,128)}, u32[]{:S(2)}) copy-start(f32[8,64]{1,0:T(8,128)} %param.14) | copy-start | bytes 6148
  24.8 5.0 %copy-start.9 = (f32[8]{0:T(128)S(1)}, f32[8]{0:T(128)}, u32[]{:S(2)}) copy-start(f32[8]{0:T(128)} %param.15) | copy-start | bytes 100
  24.8 20.9 %copy-start.5 = (s32[8,16]{1,0:T(8,128)S(1)}, s32[8,16]{1,0:T(8,128)}, u32[]{:S(2)}) copy-start(s32[8,16]{1,0:T(8,128)} %position_ref.3) | copy-start | bytes 1540
  24.8 20.9 %copy-start.6 = (s32[1,32]{1,0:T(1,128)S(1)}, s32[1,32]{1,0:T(1,128)}, u32[]{:S(2)}) copy-start(s32[1,32]{1,0:T(1,128)} %request_ref.1) | copy-start | bytes 388
  24.9 20.9 %all-to-all-start.1 = ((bf16[8,2,160,256]{3,2,1,0:T(8,128)(2,1)}), bf16[8,2,160,256]{3,2,1,0:T(8,128)(2,1)S(1)}, u32[]{:S(2)}, u32[]{:S(2)}) async-start(bf16[8,2,160,256]{3,2,1,0:T(8,128)(2,1)} %pack_payload.1), calls=%async_computation.1 | async-start | bytes 2621440 | tf_op jit(solution)/shard_map/all_to_all | solution.py:515

commit v6 on v5

--- a/solution.py
+++ b/solution.py
@@ -52,14 +52,16 @@
     return jnp.exp2(power)
 
 
-def block_of_logs(logs, eighths):
-    rows, lanes = logs.shape[0], logs.shape[1] // 2
+def block_of_logs(first, second, eighths):
+    rows, lanes = first.shape[0], eighths.shape[1]
     size = lanes // 2
-    first, second = logs[:, :lanes], logs[:, lanes:]
     left = lax.broadcasted_iota(jnp.int32, (rows, lanes), 1) < size
-    upper = jnp.where(left, first, pltpu.roll(second, size, 1))
-    lower = jnp.where(left, pltpu.roll(first, size, 1), second)
-    both = jnp.concatenate([upper, lower], axis=0)
+    quarters = []
+    for start in range(0, 2 * lanes, lanes):
+        a, b = first[:, start : start + lanes], second[:, start : start + lanes]
+        quarters.append(jnp.where(left, a, pltpu.roll(b, size, 1)))
+        quarters.append(jnp.where(left, pltpu.roll(a, size, 1), b))
+    both = jnp.concatenate(quarters, axis=0)
     return jnp.log2(both) * (scale_of(eighths) * (1.0 / LOG_TOP))
 
 
@@ -90,34 +92,59 @@
 
 
 def prepare_kernel(
-    pnos_ref, domains_ref, amp_ref, integrals_ref, own_ref, current_ref, blocks_ref, atoms_ref
+    half_ref, request_ref, table_ref, pnos_ref, domains_ref, amp_ref, integrals_ref, weight_ref,
+    position_ref, own_ref, current_ref, blocks_ref, atoms_ref, scales_ref, weights_ref, mask_ref,
+    own_atoms_ref, info_ref,
 ):
     pairs, size, width = pnos_ref.shape
     columns = own_ref.shape[1]
+    entries = scales_ref.shape[0]
+    half = half_ref[0]
     to_blocks(amp_ref, current_ref, size)
     to_blocks(integrals_ref, blocks_ref, size)
-    atoms_ref[...] = atoms_of_columns(domains_ref[...], width)
+    own_atoms_ref[...] = atoms_of_columns(domains_ref[...], width)
     for p in range(pairs):
         own_ref[p * size : (p + 1) * size, :] = lax.dot_general(
-            pnos_ref[p], column_table(atoms_ref[p : p + 1, :], columns), NT,
+            pnos_ref[p], column_table(own_atoms_ref[p : p + 1, :], columns), NT,
             preferred_element_type=jnp.float32,
         ).astype(jnp.bfloat16)
 
+    count = domains_ref.shape[1]
+    lanes = table_ref.shape[2]
+    for k in range(2 * entries):
+        source = source_of(k // 2, half, entries // 2)
+        row = request_ref[0, source * 2 + k % 2]
+        info_ref[k : k + 1, :lanes] = table_ref[source, pl.ds(row, 1), :]
+    atoms_ref[...] = atoms_of_columns(info_ref[:, size : size + count], width)
+    scales = info_ref[:, : 2 * size].astype(jnp.float32)
+    moved = pltpu.roll(scales, size, 1)
+    left_lanes = lax.broadcasted_iota(jnp.int32, (1, 2 * size), 1) < size
+    for e in range(entries):
+        scales_ref[e : e + 1, :] = jnp.where(
+            left_lanes, scales[2 * e : 2 * e + 1, :], moved[2 * e + 1 : 2 * e + 2, :]
+        )
+    for c in range(weights_ref.shape[0]):
+        weights_ref[c] = slot_weights(
+            half, entries // 2, c * CHUNK, weight_ref, position_ref, size
+        )
+    mask_ref[...] = jnp.full_like(mask_ref, half)
+
 
 def encode_kernel(
-    amp_hbm, domains_hbm, request_hbm, logs_ref, table_ref, amp_ref, domains_ref, request_ref,
-    rows_ref, sem_ref,
-):
-    pairs, half_size, lanes = logs_ref.shape
-    size = lanes // 2
+    pnos_hbm, amp_hbm, domains_hbm, request_hbm, pnos_ref, logs_ref, table_ref, amp_ref,
+    domains_ref, request_ref, rows_ref, sem_ref,
+):
+    pairs, size, unused = pnos_hbm.shape
+    quarter = logs_ref.shape[1]
     copies = [
         pltpu.make_async_copy(amp_hbm, amp_ref, sem_ref.at[0]),
         pltpu.make_async_copy(domains_hbm, domains_ref, sem_ref.at[1]),
         pltpu.make_async_copy(request_hbm, request_ref, sem_ref.at[2]),
+        pltpu.make_async_copy(pnos_hbm, pnos_ref, sem_ref.at[3]),
     ]
     for copy in copies:
         copy.start()
-    for copy in copies:
+    for copy in copies[:3]:
         copy.wait()
     to_blocks(amp_ref, rows_ref, size)
     scales = []
@@ -126,7 +153,7 @@
         eighths = eighths_of(block)
         logs = log_code(block, eighths)
         logs_ref[p] = jnp.concatenate(
-            [logs[:half_size, :], logs[half_size:, :]], axis=1
+            [logs[q : q + quarter, :] for q in range(0, size, quarter)], axis=1
         ).astype(jnp.bfloat16)
         scales.append(eighths)
     scales = jnp.concatenate(scales, axis=0).astype(jnp.int32)
@@ -135,26 +162,31 @@
     table_ref[:, :size] = scales
     table_ref[:, size : size + count] = domains_ref[...]
     table_ref[:, size + count :] = jnp.broadcast_to(request_ref[...], (pairs, slots))
+    copies[3].wait()
 
 
 def pack_kernel(
-    here_ref, there_ref, pnos_ref, logs_ref, far_pnos_ref, far_logs_ref, out_ref
+    here_ref, there_ref, pnos_ref, logs_ref, far_pnos_ref, far_logs_ref, out_hbm, sem_ref
 ):
     unused, size, width = pnos_ref.shape
-    lanes = logs_ref.shape[2]
+    quarter = logs_ref.shape[1]
 
     def pack(n, carry):
         parts = ((here_ref, pnos_ref, logs_ref), (there_ref, far_pnos_ref, far_logs_ref))
         for part, (wanted_ref, blocks_ref, codes_ref) in enumerate(parts):
-            first = wanted_ref[n, 0]
-            second = wanted_ref[n, 1]
-            out_ref[n, part, :size] = blocks_ref[first]
-            out_ref[n, part, size : 2 * size] = blocks_ref[second]
-            out_ref[n, part, 2 * size :, :lanes] = codes_ref[first]
-            out_ref[n, part, 2 * size :, lanes:] = codes_ref[second]
+            for c in range(2):
+                pair = wanted_ref[n, c]
+                to = out_hbm.at[n, part, c]
+                pltpu.make_async_copy(
+                    blocks_ref.at[pair], to.at[pl.ds(0, size)], sem_ref.at[0]
+                ).start()
+                pltpu.make_async_copy(
+                    codes_ref.at[pair], to.at[pl.ds(size, quarter)], sem_ref.at[0]
+                ).start()
         return carry
 
-    lax.fori_loop(0, out_ref.shape[0], pack, 0)
+    lax.fori_loop(0, out_hbm.shape[0], pack, 0)
+    pltpu.make_async_copy(out_hbm, out_hbm, sem_ref.at[0]).wait()
 
 
 def source_of(entry, half, near):
@@ -212,7 +244,7 @@
     for k in range(2 * CHUNK):
         n, c = k // 2, k % 2
         full_ref[k * size : (k + 1) * size, :] = lax.dot_general(
-            payload_ref[n, c * size : (c + 1) * size, :],
+            payload_ref[n, c, :size, :],
             column_table(atoms[k : k + 1, :], columns), NT, preferred_element_type=jnp.float32,
         ).astype(jnp.bfloat16)
     cross = lax.dot_general(own_ref[...], full_ref[...], NT, preferred_element_type=jnp.float32)
@@ -228,44 +260,31 @@
 
 
 def first_kernel(
-    half_ref, request_ref, wanted_ref, table_ref, own_ref, payload_ref, weight_ref, position_ref,
-    current_ref, integrals_ref, denominator_ref, cat_ref, new_ref, send_hbm, full_ref, left_ref,
-    acc_ref, info_ref, send_ref, even_ref, odd_ref, sem_ref,
+    wanted_hbm, own_ref, payload_ref, atoms_ref, scales_ref, weights_ref, current_ref,
+    integrals_ref, denominator_ref, cat_ref, new_ref, send_hbm, full_ref, left_ref, acc_ref,
+    send_ref, even_ref, odd_ref, wanted_ref, sem_ref,
 ):
     pairs, size, unused = denominator_ref.shape
-    width = payload_ref.shape[2]
     chunks = cat_ref.shape[0]
-    near = wanted_ref.shape[0] // 2
-    half = half_ref[0]
     step = pl.program_id(0)
-    count = table_ref.shape[2] - size - request_ref.shape[1]
-    entries = CHUNK * chunks
-    lanes = table_ref.shape[2]
-    for k in range(2 * entries):
-        source = source_of(step * entries + k // 2, half, near)
-        row = request_ref[0, source * 2 + k % 2]
-        info_ref[k : k + 1, :lanes] = table_ref[source, pl.ds(row, 1), :lanes]
-    atoms = atoms_of_columns(info_ref[:, size : size + count], width)
-    scales = info_ref[:, : 2 * size].astype(jnp.float32)
-    moved = pltpu.roll(scales, size, 1)
-    left_lanes = lax.broadcasted_iota(jnp.int32, (1, 2 * size), 1) < size
+    wanted_copy = pltpu.make_async_copy(wanted_hbm, wanted_ref, sem_ref.at[0])
+
+    @pl.when(step == 0)
+    def fetch():
+        wanted_copy.start()
 
     for c in range(chunks):
         blocks = payload_ref.at[pl.ds(c * CHUNK, CHUNK)]
-        cross_chunk(
-            atoms[c * 2 * CHUNK : (c + 1) * 2 * CHUNK], own_ref, blocks, cat_ref.at[c],
-            full_ref.at[c],
-        )
-        start = step * entries + c * CHUNK
-        weights = slot_weights(half, near, start, weight_ref, position_ref, size)
-
-        def amps(j, c=c, blocks=blocks):
-            k = 2 * (c * CHUNK + j)
-            eighths = jnp.where(left_lanes, scales[k : k + 1, :], moved[k + 1 : k + 2, :])
-            logs = blocks[j, 2 * size :, :].astype(jnp.float32)
-            return block_of_logs(logs, eighths)
-
-        half_products(weights, amps, cat_ref.at[c], left_ref.at[c])
+        chunk = step * chunks + c
+        atoms = atoms_ref[pl.ds(chunk * 2 * CHUNK, 2 * CHUNK), :]
+        cross_chunk(atoms, own_ref, blocks, cat_ref.at[c], full_ref.at[c])
+
+        def amps(j, chunk=chunk, blocks=blocks):
+            eighths = scales_ref[pl.ds(chunk * CHUNK + j, 1), :]
+            logs = [blocks[j, i, size:, :].astype(jnp.float32) for i in range(2)]
+            return block_of_logs(*logs, eighths)
+
+        half_products(weights_ref[chunk], amps, cat_ref.at[c], left_ref.at[c])
     add_products(step == 0, cat_ref, left_ref, acc_ref)
 
     @pl.when(step == pl.num_programs(0) - 1)
@@ -278,6 +297,8 @@
             new_ref[rows, :] = new
             store_codes(new, even_ref, odd_ref, s)
 
+        wanted_copy.wait()
+
         def pack(d, carry):
             send_ref[d] = even_ref[wanted_ref[d, 0]] + odd_ref[wanted_ref[d, 1]]
             return carry
@@ -289,21 +310,24 @@
 
 
 def second_kernel(
-    half_ref, cat_ref, weight_ref, position_ref, amp_ref, current_ref, integrals_ref,
-    denominator_ref, new_ref, residual_ref, left_ref, acc_ref, new_rows_ref, residual_rows_ref,
+    mask_ref, cat_ref, weights_ref, amp_ref, current_ref, integrals_ref, denominator_ref,
+    new_ref, residual_ref, left_ref, acc_ref, new_rows_ref, residual_rows_ref,
 ):
     pairs, size, unused = denominator_ref.shape
     step = pl.program_id(0)
-    half = half_ref[0]
     near = amp_ref.shape[0] // 2
     chunks = cat_ref.shape[0]
+    upper = mask_ref[:1, :] > 0
     for c in range(chunks):
-        start = (step * chunks + c) * CHUNK
-        weights = slot_weights(half, near, start, weight_ref, position_ref, size)
-        half_products(
-            weights, lambda j: block_of_codes(amp_ref[source_of(start + j, half, near)]),
-            cat_ref.at[c], left_ref.at[c],
-        )
+        chunk = step * chunks + c
+
+        def amps(j, chunk=chunk):
+            entry = chunk * CHUNK + j
+            low = block_of_codes(amp_ref[entry // 2])
+            high = block_of_codes(amp_ref[near + entry // 2])
+            return jnp.where(upper, low, high) if j % 2 else jnp.where(upper, high, low)
+
+        half_products(weights_ref[chunk], amps, cat_ref.at[c], left_ref.at[c])
     add_products(step == 0, cat_ref, left_ref, acc_ref)
 
     @pl.when(step == pl.num_programs(0) - 1)
@@ -347,53 +371,62 @@
     return pltpu.CompilerParams(vmem_limit_bytes=VMEM_LIMIT)
 
 
-def prepare(pnos, domains, amplitudes, integrals):
+def prepare(half, request, table, pnos, domains, amplitudes, integrals, weight, position):
     pairs, size, width = pnos.shape
+    entries = request.shape[1] // 2
     own = (pairs * size, ATOMS * (width // domains.shape[1]))
     block = (pairs * size, size)
+    out = (
+        (own, jnp.bfloat16), (block, jnp.float32), (block, jnp.float32),
+        ((2 * entries, width), jnp.float32), ((entries, 2 * size), jnp.float32),
+        ((entries // CHUNK, pairs, 2 * CHUNK * size), jnp.float32), ((8, 2 * size), jnp.int32),
+    )
     return pl.pallas_call(
         prepare_kernel,
-        in_specs=[vmem()] * 4,
-        out_specs=[vmem()] * 3,
-        out_shape=[
-            jax.ShapeDtypeStruct(own, jnp.bfloat16), jax.ShapeDtypeStruct(block, jnp.float32),
-            jax.ShapeDtypeStruct(block, jnp.float32),
+        in_specs=[smem()] * 2 + [vmem()] * 7,
+        out_specs=[vmem()] * len(out),
+        out_shape=[jax.ShapeDtypeStruct(shape, dtype) for shape, dtype in out],
+        scratch_shapes=[
+            pltpu.VMEM((pairs, width), jnp.float32),
+            pltpu.VMEM((2 * entries, max(table.shape[2], 2 * size)), jnp.int32),
         ],
-        scratch_shapes=[pltpu.VMEM((pairs, width), jnp.float32)],
         compiler_params=limit(),
         name="prepare",
-    )(pnos, domains, amplitudes, integrals)
-
-
-def encode(amplitudes, domains, request, size):
-    pairs = amplitudes.shape[0]
+    )(half, request, table, pnos, domains, amplitudes, integrals, weight, position)
+
+
+def encode(pnos, amplitudes, domains, request):
+    pairs, size, width = pnos.shape
+    quarter = size * size // width
     lanes = size + domains.shape[1] + request.shape[1]
     return pl.pallas_call(
         encode_kernel,
-        in_specs=[hbm()] * 3,
-        out_specs=[vmem()] * 2,
+        in_specs=[hbm()] * 4,
+        out_specs=[vmem()] * 3,
         out_shape=[
-            jax.ShapeDtypeStruct((pairs, size // 2, 2 * size), jnp.bfloat16),
+            jax.ShapeDtypeStruct(pnos.shape, jnp.bfloat16),
+            jax.ShapeDtypeStruct((pairs, quarter, width), jnp.bfloat16),
             jax.ShapeDtypeStruct((pairs, lanes), jnp.int32),
         ],
         scratch_shapes=[
             pltpu.VMEM(amplitudes.shape, jnp.float32), pltpu.VMEM(domains.shape, jnp.int32),
             pltpu.VMEM(request.shape, jnp.int32), pltpu.VMEM((pairs * size, size), jnp.float32),
-            pltpu.SemaphoreType.DMA((3,)),
+            pltpu.SemaphoreType.DMA((4,)),
         ],
         compiler_params=limit(),
         name="encode",
-    )(*in_hbm(amplitudes, domains, request))
+    )(*in_hbm(pnos, amplitudes, domains, request))
 
 
 def pack_payload(here, there, pnos, logs, far_pnos, far_logs):
     unused, size, width = pnos.shape
-    rows = 2 * size + logs.shape[1]
+    out = (here.shape[0], 2, 2, size + logs.shape[1], width)
     return pl.pallas_call(
         pack_kernel,
         in_specs=[smem(), smem()] + [vmem()] * 4,
-        out_specs=vmem(),
-        out_shape=jax.ShapeDtypeStruct((here.shape[0], 2, rows, width), jnp.bfloat16),
+        out_specs=hbm(),
+        out_shape=pltpu.HBM(out, pnos.dtype),
+        scratch_shapes=[pltpu.SemaphoreType.DMA((1,))],
         compiler_params=limit(),
         name="pack_payload",
     )(here, there, pnos, logs, far_pnos, far_logs)
@@ -417,20 +450,20 @@
 
 
 def first_sweep(
-    half, request, wanted, table, own, payload, weight, position, current, integrals, denominator
+    wanted, own, payload, atoms, scales, weights, current, integrals, denominator
 ):
     pairs, size, unused = denominator.shape
-    entries, rows, width = payload.shape
+    entries = payload.shape[0]
     steps, chunks, cat, (cats, lefts, acc) = sweep_shapes(entries, pairs, size)
-    block = (CHUNK * chunks, rows, width)
-    blocks = vmem() if steps == 1 else pl.BlockSpec(block, lambda i: (i, 0, 0))
+    block = (CHUNK * chunks,) + payload.shape[1:]
+    blocks = vmem() if steps == 1 else pl.BlockSpec(block, lambda i: (i, 0, 0, 0))
     kept = cat_spec(steps, chunks, cat)
     parts = (pairs, size + CODE_ROWS, 2 * size)
     send = (entries,) + parts[1:]
     return pl.pallas_call(
         first_kernel,
         grid=(steps,),
-        in_specs=[smem()] * 3 + [vmem(), vmem(), blocks] + [vmem()] * 5,
+        in_specs=[hbm(), vmem(), blocks] + [vmem()] * 6,
         out_specs=[kept, vmem(), hbm()],
         out_shape=[
             jax.ShapeDtypeStruct(cat, jnp.bfloat16),
@@ -441,28 +474,27 @@
             pltpu.VMEM((chunks, cat[3], own.shape[1]), jnp.bfloat16),
             lefts,
             acc,
-            pltpu.VMEM((2 * CHUNK * chunks, max(table.shape[2], 2 * size)), jnp.int32),
             pltpu.VMEM(send, jnp.int16),
             pltpu.VMEM(parts, jnp.int16),
             pltpu.VMEM(parts, jnp.int16),
+            pltpu.SMEM(wanted.shape, jnp.int32),
             pltpu.SemaphoreType.DMA((1,)),
         ],
         compiler_params=params(),
         name="first_sweep",
     )(
-        half, request, wanted, table, own, payload, weight, position, current, integrals,
-        denominator,
-    )
-
-
-def second_sweep(half, cat, weight, position, amp, current, integrals, denominator):
+        *in_hbm(wanted), own, payload, atoms, scales, weights, current, integrals, denominator
+    )
+
+
+def second_sweep(mask, cat, weights, amp, current, integrals, denominator):
     pairs, size, unused = denominator.shape
     steps, chunks, shape, scratch = sweep_shapes(amp.shape[0], pairs, size)
     flat = (pairs, size * size)
     return pl.pallas_call(
         second_kernel,
         grid=(steps,),
-        in_specs=[smem(), cat_spec(steps, chunks, shape)] + [vmem()] * 6,
+        in_specs=[vmem(), cat_spec(steps, chunks, shape)] + [vmem()] * 5,
         out_specs=[vmem(), vmem()],
         out_shape=[jax.ShapeDtypeStruct(flat, jnp.float32)] * 2,
         scratch_shapes=scratch[1:] + [
@@ -472,7 +504,7 @@
         compiler_params=params(),
         name="second_sweep",
     )(
-        half, cat, weight, position, amp, current, integrals, denominator
+        mask, cat, weights, amp, current, integrals, denominator
     )
 
 
@@ -491,7 +523,7 @@
     both = ("half", "near")
 
     far_pnos = lax.ppermute(pnos, "half", swap)
-    logs, table = encode(amplitudes, domains, request, size)
+    near_pnos, logs, table = encode(pnos, amplitudes, domains, request)
     far_logs = lax.ppermute(logs, "half", swap)
 
     def gather(row):
@@ -511,23 +543,21 @@
         table, (half * near, 0, column + (1 - half) * 2 * near), (near, 1, 2)
     ).reshape(near, 2)
 
-    payload = pack_payload(here, there, pnos, logs, far_pnos, far_logs)
+    payload = pack_payload(here, there, near_pnos, logs, far_pnos, far_logs)
     payload = lax.all_to_all(payload, "near", split_axis=0, concat_axis=0, tiled=True)
     payload = payload.reshape((entries,) + payload.shape[2:])
 
     live = jnp.arange(depth, dtype=jnp.int32)[None, :] < degree[:, None]
     weight = jnp.where(live, coupling, jnp.zeros_like(coupling))
     denominator = virtual[:, :, None] + virtual[:, None, :] - occupied[:, None, None]
-    own, current, integrals = prepare(pnos, domains, amplitudes, integrals)
-    half = half.reshape(1)
+    own, current, integrals, atoms, scales, weights, mask = prepare(
+        half.reshape(1), request, table, pnos, domains, amplitudes, integrals, weight, position
+    )
     cat, current, amp = first_sweep(
-        half, request, wanted, table, own, payload, weight, position, current, integrals,
-        denominator,
+        wanted, own, payload, atoms, scales, weights, current, integrals, denominator
     )
     amp = lax.all_to_all(amp, both, split_axis=0, concat_axis=0, tiled=True)
-    new, residual = second_sweep(
-        half, cat, weight, position, amp, current, integrals, denominator
-    )
+    new, residual = second_sweep(mask, cat, weights, amp, current, integrals, denominator)
     return new, residual
 
 

time: 74.1 us -> 72.7 us (0.981)
  waiting for transfers between devices: 15.8 us -> 14.6 us
    all_to_all x1, waiting for transfers between devices: 15.8 us -> 14.6 us  [on_device(): lax.all_to_all(payload, 'near', split_axis=0, concat_axis=0, tiled=True)]
    unnamed x22 -> x20, local copies, waits for them, and re-layouts: 1 us -> 0.06 us
  transfers between devices with their start and end apart: 3 -> 3, of which waited for: 1 -> 1; matrix products, arithmetic and copies ran while one was open for 1% -> 1% of each run, Pallas kernels for 3% -> 4%
where the time goes in v6:
time: 72.7 us; the launch traced here: 72.3 us
  blocking collectives  31.3 us (43%)
  Pallas kernels  16 us (22%)
  waiting for transfers between devices  14.6 us (20%)
  starting transfers between devices  7.9 us (11%)
  between operations  1.48 us (2%)
  local copies, waits for them, and re-layouts  0.84 us (1%)
    all_to_all x1, blocking collectives, on_device(): amp = lax.all_to_all(amp, both, split_axis=0, concat_axis=0, tiled=True)  16.3 us
    all_to_all x1, blocking collectives, gather(): return lax.all_to_all(rows, both, split_axis=0, concat_axis=0, tiled=True)  15 us
    all_to_all x1, waiting for transfers between devices, on_device(): lax.all_to_all(payload, 'near', split_axis=0, concat_axis=0, tiled=True)  14.6 us
    pallas_call x1, Pallas kernels, first_sweep(): pl.pallas_call(first_kernel, grid=(steps,), in_specs=[hbm(), vmem(), bloc...  7.87 us
    ppermute x1, starting transfers between devices, on_device(): far_pnos = lax.ppermute(pnos, 'half', swap)  4.1 us
    all_to_all x1, starting transfers between devices, on_device(): lax.all_to_all(payload, 'near', split_axis=0, concat_axis=0, tiled=True)  3.71 us
    pallas_call x1, Pallas kernels, second_sweep(): pl.pallas_call(second_kernel, grid=(steps,), in_specs=[vmem(), cat_spec(s...  3.43 us
    pallas_call x1, Pallas kernels, pack_payload(): pl.pallas_call(pack_kernel, in_specs=[smem(), smem()] + [vmem()] * 4, out...  1.77 us
  transfers between devices with their start and end apart: 3, of which 1 were waited for; matrix products, arithmetic and copies ran while one was open for 1% of the time, Pallas kernels for 4%

profile of v6, /device:TPU:0, one launch (start us, length us, event | category | flops | bytes accessed | tf_op | source)
XLA Modules:
  0.0 72.3 jit_solution(2294192780456736676)
XLA Ops:
  0.6 4.1 %collective-permute-start = (bf16[8,64,256]{2,1,0:T(8,128)(2,1)}, bf16[8,64,256]{2,1,0:T(8,128)(2,1)S(1)}, u32[]{:S(2)}, u32[]{:S(2)}) collective-permute-start(bf16[8,64,256]{2,1,0:T(8,128)(2,1)} %pnos_ref.1), channel_id=1, source_target_pairs={{0,8},{8,0},{1,9},{9,1},{2,10},{10,2},{3,11},{11,3},{4,12},{12,4},... | collective-permute-start | bytes 786440 | tf_op jit(solution)/shard_map/ppermute | solution.py:525
  4.7 1.2 %encode.1 = (bf16[8,64,256]{2,1,0:T(8,128)(2,1)S(1)}, bf16[8,16,256]{2,1,0:T(8,128)(2,1)S(1)}, s32[8,112]{1,0:T(8,128)S(1)}) custom-call(bf16[8,64,256]{2,1,0:T(8,128)(2,1)} %pnos_ref.1, f32[8,4096]{1,0:T(8,128)} %amp_ref.1, s32[8,16]{1,0:T(8,128)} %domains_ref.1, s32[1,32]{1,0:T(1,128)} %request_ref.1), custom_call_target="tpu_custom_call" | custom-call | tf_op jit(solution)/shard_map/encode/pallas_call | solution.py:402
  6.0 0.1 collective-permute-start.1
  6.7 15.1 %conditional.1 = (s32[16,8,112]{2,1,0:T(8,128)S(1)}) conditional(s32[]{:T(128)} %bitcast.1, () %tuple.13, s32[8,112]{1,0:T(8,128)S(1)} %get-tuple-element.19), branch_computations={%region_0.0_spmd, %region_1.0_spmd} | conditional | bytes 175624 | solution.py:536
  6.8 15.0 %all_to_all.14 = s32[16,8,112]{2,1,0:T(8,128)S(1)} all-to-all(s32[16,8,112]{2,1,0:T(8,128)S(1)} %broadcast_in_dim.0), channel_id=1, replica_groups=mesh['frag'=2,'half'=2,'near'=8] {'half','near'}, dimensions={0} | all-to-all | bytes 114688 | tf_op jit(solution)/shard_map/cond/branch_1_fun/all_to_all | solution.py:531
  21.8 0.1 constant_dynamic-slice_fusion
  21.9 0.0 collective-permute-done.1.far_logs_ref
  21.9 0.0 collective-permute-done.far_pnos_ref
  21.9 1.8 %pack_payload.1 = bf16[8,2,2,80,256]{4,3,2,1,0:T(8,128)(2,1)} custom-call(s32[8,2]{1,0:T(8,128)S(1)} %bitcast.9, s32[8,2]{1,0:T(8,128)S(1)} %bitcast.8, bf16[8,64,256]{2,1,0:T(8,128)(2,1)S(1)} %get-tuple-element.22.pnos_ref, bf16[8,16,256]{2,1,0:T(8,128)(2,1)S(1)} %get-tuple-element.23.logs_ref, bf16[8,64,256]{2,1,0:T(8,128)(2,1)S(1)} %collective-permute-done.far_pnos_ref, ...), custom_call_target="tpu_custom_call" | custom-call | tf_op jit(solution)/shard_map/pack_payload/pallas_call | solution.py:424
  23.7 0.0 copy-start.7
  23.7 0.0 copy-start.9
  23.7 0.0 copy-start
  23.7 0.0 copy-start.1
  23.7 0.0 copy-start.2
  23.8 0.0 copy-start.3
  23.8 0.0 copy-start.4
  23.8 0.0 copy-start.5
  23.8 0.0 copy-start.6
  23.8 0.0 copy-start.8
  23.8 3.7 %all-to-all-start.1 = ((bf16[8,2,2,80,256]{4,3,2,1,0:T(8,128)(2,1)}), bf16[8,2,2,80,256]{4,3,2,1,0:T(8,128)(2,1)S(1)}, u32[]{:S(2)}, u32[]{:S(2)}) async-start(bf16[8,2,2,80,256]{4,3,2,1,0:T(8,128)(2,1)} %pack_payload.1), calls=%async_computation.1 | async-start | bytes 2621440 | tf_op jit(solution)/shard_map/all_to_all | solution.py:547
  27.5 0.0 copy-done.7
  27.5 0.0 copy-done.9
  27.6 0.1 fusion.weight_ref
  27.6 0.0 copy-done
  27.6 0.0 copy-done.1
  27.7 1.6 %prepare.1 = (bf16[512,512]{1,0:T(8,128)(2,1)S(1)}, f32[512,64]{1,0:T(8,128)S(1)}, f32[512,64]{1,0:T(8,128)S(1)}, f32[32,256]{1,0:T(8,128)S(1)}, f32[16,128]{1,0...) custom-call(s32[1]{0:T(128)} %bitcast.half_ref, s32[1,32]{1,0:T(1,128)S(1)} %copy-done.5, ...), custom_call_target="tpu_custom_call" | custom-call | tf_op jit(solution)/shard_map/prepare/pallas_call | solution.py:384
  29.3 0.7 constant_dynamic-slice_fusion.2
  30.0 0.1 add_subtract_fusion.denominator_ref
  30.2 14.6 %all-to-all-done.1 = bf16[8,2,2,80,256]{4,3,2,1,0:T(8,128)(2,1)S(1)} async-done(((bf16[8,2,2,80,256]{4,3,2,1,0:T(8,128)(2,1)}), bf16[8,2,2,80,256]{4,3,2,1,0:T(8,128)(2,1)S(1)}, u32[]{:S(2)}, u32[]{:S(2)}) %all-to-all-start.1) | async-done | bytes 1310752 | tf_op jit(solution)/shard_map/all_to_all | solution.py:547
  44.7 7.9 %first_sweep.1 = (bf16[4,8,128,512]{3,2,1,0:T(8,128)(2,1)S(1)}, f32[512,64]{1,0:T(8,128)S(1)}, s16[16,80,128]{2,1,0:T(8,128)(2,1)}) custom-call(s32[16,2]{1,0:T(8,128)} %bitcast.10, bf16[512,512]{1,0:T(8,128)(2,1)S(1)} %get-tuple-element.21.own_ref, bf16[16,2,80,256]{3,2,1,0:T(8,128)(2,1)S(1)} %bitcast.7, f32[32,256]{1,0:T(8,128)S(1)} %get-tuple-element.24.atoms_ref, ...), custom_call_target="tpu_custom_call" | custom-call | tf_op jit(solution)/shard_map/first_sweep/pallas_call | solution.py:463
  52.6 16.3 %all_to_all.15.amp_ref = s16[16,80,128]{2,1,0:T(8,128)(2,1)S(1)} all-to-all(s16[16,80,128]{2,1,0:T(8,128)(2,1)} %get-tuple-element.30), channel_id=1, replica_groups=mesh['frag'=2,'half'=2,'near'=8] {'half','near'}, dimensions={0} | all-to-all | bytes 655360 | tf_op jit(solution)/shard_map/all_to_all | solution.py:559
  68.9 3.4 %second_sweep.1 = (f32[8,4096]{1,0:T(8,128)}, f32[8,4096]{1,0:T(8,128)}) custom-call(s32[8,128]{1,0:T(8,128)S(1)} %get-tuple-element.20.mask_ref, bf16[4,8,128,512]{3,2,1,0:T(8,128)(2,1)S(1)} %get-tuple-element.29.cat_ref, f32[4,8,512]{2,1,0:T(8,128)S(1)} %get-tuple-element.26.weights_ref, s16[16,80,128]{2,1,0:T(8,128)(2,1)S(1)} %all_to_all.15.amp_ref, ...), custom_call_target="tpu_custom_call" | custom-call | tf_op jit(solution)/shard_map/second_sweep/pallas_call | solution.py:494
  (7 shorter events, 0.0 us)
Async XLA Ops:
  0.6 21.3 %collective-permute-start = (bf16[8,64,256]{2,1,0:T(8,128)(2,1)}, bf16[8,64,256]{2,1,0:T(8,128)(2,1)S(1)}, u32[]{:S(2)}, u32[]{:S(2)}) collective-permute-start(bf16[8,64,256]{2,1,0:T(8,128)(2,1)} %pnos_ref.1), channel_id=1, source_target_pairs={{0,8},{8,0},{1,9},{9,1},{2,10},{10,2},{3,11},{11,3},{4,12},{12,4},... | collective-permute-start | bytes 786440 | tf_op jit(solution)/shard_map/ppermute | solution.py:525
  6.0 15.9 %collective-permute-start.1 = (bf16[8,16,256]{2,1,0:T(8,128)(2,1)S(1)}, bf16[8,16,256]{2,1,0:T(8,128)(2,1)S(1)}, u32[]{:S(2)}, u32[]{:S(2)}) collective-permute-start(bf16[8,16,256]{2,1,0:T(8,128)(2,1)S(1)} %get-tuple-element.23.logs_ref), channel_id=1, source_target_pairs={{0,8},{8,0},{1,9},{9,1},{2,10},{10,2},{3,11},{11,3},{4,12},{12,4},... | collective-permute-start | bytes 196616 | tf_op jit(solution)/shard_map/ppermute | solution.py:527
  23.7 3.8 %copy-start.7 = (f32[8,16]{1,0:T(8,128)S(1)}, f32[8,16]{1,0:T(8,128)}, u32[]{:S(2)}) copy-start(f32[8,16]{1,0:T(8,128)} %param.16) | copy-start | bytes 1540
  23.7 3.8 %copy-start.9 = (s32[8]{0:T(128)S(1)}, s32[8]{0:T(128)}, u32[]{:S(2)}) copy-start(s32[8]{0:T(128)} %param.17) | copy-start | bytes 100
  23.7 3.9 %copy-start = (bf16[8,64,256]{2,1,0:T(8,128)(2,1)S(1)}, bf16[8,64,256]{2,1,0:T(8,128)(2,1)}, u32[]{:S(2)}) copy-start(bf16[8,64,256]{2,1,0:T(8,128)(2,1)} %pnos_ref.1) | copy-start | bytes 786436
  23.7 3.9 %copy-start.1 = (f32[8,4096]{1,0:T(8,128)S(1)}, f32[8,4096]{1,0:T(8,128)}, u32[]{:S(2)}) copy-start(f32[8,4096]{1,0:T(8,128)} %amp_ref.1) | copy-start | bytes 393220
  23.7 3.9 %copy-start.2 = (f32[8,4096]{1,0:T(8,128)S(1)}, f32[8,4096]{1,0:T(8,128)}, u32[]{:S(2)}) copy-start(f32[8,4096]{1,0:T(8,128)} %integrals_ref.1) | copy-start | bytes 393220
  23.8 3.9 %copy-start.3 = (s32[8,16]{1,0:T(8,128)S(1)}, s32[8,16]{1,0:T(8,128)}, u32[]{:S(2)}) copy-start(s32[8,16]{1,0:T(8,128)} %domains_ref.1) | copy-start | bytes 1540
  23.8 3.9 %copy-start.4 = (s32[8,16]{1,0:T(8,128)S(1)}, s32[8,16]{1,0:T(8,128)}, u32[]{:S(2)}) copy-start(s32[8,16]{1,0:T(8,128)} %position_ref.1) | copy-start | bytes 1540
  23.8 3.9 %copy-start.5 = (s32[1,32]{1,0:T(1,128)S(1)}, s32[1,32]{1,0:T(1,128)}, u32[]{:S(2)}) copy-start(s32[1,32]{1,0:T(1,128)} %request_ref.1) | copy-start | bytes 388
  23.8 6.2 %copy-start.6 = (f32[8,64]{1,0:T(8,128)S(1)}, f32[8,64]{1,0:T(8,128)}, u32[]{:S(2)}) copy-start(f32[8,64]{1,0:T(8,128)} %param.14) | copy-start | bytes 6148
  23.8 6.2 %copy-start.8 = (f32[8]{0:T(128)S(1)}, f32[8]{0:T(128)}, u32[]{:S(2)}) copy-start(f32[8]{0:T(128)} %param.15) | copy-start | bytes 100
  23.8 20.9 %all-to-all-start.1 = ((bf16[8,2,2,80,256]{4,3,2,1,0:T(8,128)(2,1)}), bf16[8,2,2,80,256]{4,3,2,1,0:T(8,128)(2,1)S(1)}, u32[]{:S(2)}, u32[]{:S(2)}) async-start(bf16[8,2,2,80,256]{4,3,2,1,0:T(8,128)(2,1)} %pack_payload.1), calls=%async_computation.1 | async-start | bytes 2621440 | tf_op jit(solution)/shard_map/all_to_all | solution.py:547

commit v7 on v6

--- a/solution.py
+++ b/solution.py
@@ -526,14 +526,8 @@
     near_pnos, logs, table = encode(pnos, amplitudes, domains, request)
     far_logs = lax.ppermute(logs, "half", swap)
 
-    def gather(row):
-        rows = jnp.broadcast_to(row[None], (entries,) + row.shape)
-        return lax.all_to_all(rows, both, split_axis=0, concat_axis=0, tiled=True)
-
-    def nothing(row):
-        return jnp.zeros((entries,) + row.shape, jnp.int32)
-
-    table = lax.cond(degree[0] > 0, gather, nothing, table)
+    table = jnp.broadcast_to(table[None], (entries,) + table.shape)
+    table = lax.all_to_all(table, both, split_axis=0, concat_axis=0, tiled=True)
     column = table.shape[2] - slots + 2 * mine
     wanted = lax.dynamic_slice(
         table, (0, 0, column + half * 2 * near), (entries, 1, 2)

time: 72.7 us -> 71.9 us (0.989)
  blocking collectives: 31.3 us -> 16.1 us
  waiting for transfers between devices: 14.6 us -> 22.3 us
  starting transfers between devices: 7.9 us -> 14.6 us
    all_to_all x1 -> x0, blocking collectives: 15 us -> none  [gather(): return lax.all_to_all(rows, both, split_axis=0, concat_axis=0, tiled=True)]
    all_to_all x0 -> x1, waiting for transfers between devices: none -> 7.75 us  [on_device(): table = lax.all_to_all(table, both, split_axis=0, concat_axis=0, tiled=True)]
    all_to_all x0 -> x1, starting transfers between devices: none -> 3.91 us  [on_device(): table = lax.all_to_all(table, both, split_axis=0, concat_axis=0, tiled=True)]
    ppermute x1, starting transfers between devices: 0.09 us -> 2.83 us  [on_device(): far_logs = lax.ppermute(logs, 'half', swap)]
  transfers between devices with their start and end apart: 3 -> 4, of which waited for: 1 -> 2; matrix products, arithmetic and copies ran while one was open for 1% -> 2% of each run, Pallas kernels for 4% -> 4%
where the time goes in v7:
time: 71.9 us; the launch traced here: 71.4 us
  waiting for transfers between devices  22.3 us (31%)
  blocking collectives  16.1 us (22%)
  Pallas kernels  16 us (22%)
  starting transfers between devices  14.6 us (20%)
  local copies, waits for them, and re-layouts  1.47 us (2%)
  between operations  0.84 us (1%)
    all_to_all x1, blocking collectives, on_device(): amp = lax.all_to_all(amp, both, split_axis=0, concat_axis=0, tiled=True)  16.1 us
    all_to_all x1, waiting for transfers between devices, on_device(): lax.all_to_all(payload, 'near', split_axis=0, concat_axis=0, tiled=True)  14.6 us
    pallas_call x1, Pallas kernels, first_sweep(): pl.pallas_call(first_kernel, grid=(steps,), in_specs=[hbm(), vmem(), bloc...  7.9 us
    all_to_all x1, waiting for transfers between devices, on_device(): table = lax.all_to_all(table, both, split_axis=0, concat_axis=0, tiled=True)  7.75 us
    ppermute x1, starting transfers between devices, on_device(): far_pnos = lax.ppermute(pnos, 'half', swap)  4.1 us
    all_to_all x1, starting transfers between devices, on_device(): table = lax.all_to_all(table, both, split_axis=0, concat_axis=0, tiled=True)  3.91 us
    all_to_all x1, starting transfers between devices, on_device(): lax.all_to_all(payload, 'near', split_axis=0, concat_axis=0, tiled=True)  3.71 us
    pallas_call x1, Pallas kernels, second_sweep(): pl.pallas_call(second_kernel, grid=(steps,), in_specs=[vmem(), cat_spec(s...  3.42 us
  transfers between devices with their start and end apart: 4, of which 2 were waited for; matrix products, arithmetic and copies ran while one was open for 2% of the time, Pallas kernels for 4%

profile of v7, /device:TPU:0, one launch (start us, length us, event | category | flops | bytes accessed | tf_op | source)
XLA Modules:
  0.0 71.4 jit_solution(14586822059317733806)
XLA Ops:
  0.6 4.1 %collective-permute-start = (bf16[8,64,256]{2,1,0:T(8,128)(2,1)}, bf16[8,64,256]{2,1,0:T(8,128)(2,1)S(1)}, u32[]{:S(2)}, u32[]{:S(2)}) collective-permute-start(bf16[8,64,256]{2,1,0:T(8,128)(2,1)} %pnos_ref.1), channel_id=1, source_target_pairs={{0,8},{8,0},{1,9},{9,1},{2,10},{10,2},{3,11},{11,3},{4,12},{12,4},... | collective-permute-start | bytes 786440 | tf_op jit(solution)/shard_map/ppermute | solution.py:525
  4.7 1.2 %encode.1 = (bf16[8,64,256]{2,1,0:T(8,128)(2,1)S(1)}, bf16[8,16,256]{2,1,0:T(8,128)(2,1)S(1)}, s32[8,112]{1,0:T(8,128)S(1)}) custom-call(bf16[8,64,256]{2,1,0:T(8,128)(2,1)} %pnos_ref.1, f32[8,4096]{1,0:T(8,128)} %amp_ref.1, s32[8,16]{1,0:T(8,128)} %domains_ref.1, s32[1,32]{1,0:T(1,128)} %request_ref.1), custom_call_target="tpu_custom_call" | custom-call | tf_op jit(solution)/shard_map/encode/pallas_call | solution.py:402
  6.0 0.6 broadcast_in_dim.4
  6.6 3.9 %all-to-all-start = ((s32[16,8,112]{2,1,0:T(8,128)}), s32[16,8,112]{2,1,0:T(8,128)S(1)}, u32[]{:S(2)}, u32[]{:S(2)}) async-start(s32[16,8,112]{2,1,0:T(8,128)} %broadcast_in_dim.4), calls=%async_computation | async-start | bytes 131072 | tf_op jit(solution)/shard_map/all_to_all | solution.py:530
  10.5 2.8 %collective-permute-start.1 = (bf16[8,16,256]{2,1,0:T(8,128)(2,1)S(1)}, bf16[8,16,256]{2,1,0:T(8,128)(2,1)S(1)}, u32[]{:S(2)}, u32[]{:S(2)}) collective-permute-start(bf16[8,16,256]{2,1,0:T(8,128)(2,1)S(1)} %get-tuple-element.19.logs_ref), channel_id=1, source_target_pairs={{0,8},{8,0},{1,9},{9,1},{2,10},{10,2},{3,11},{11,3},{4,12},{12,4},... | collective-permute-start | bytes 196616 | tf_op jit(solution)/shard_map/ppermute | solution.py:527
  13.4 7.7 %all-to-all-done.table_ref = s32[16,8,112]{2,1,0:T(8,128)S(1)} async-done(((s32[16,8,112]{2,1,0:T(8,128)}), s32[16,8,112]{2,1,0:T(8,128)S(1)}, u32[]{:S(2)}, u32[]{:S(2)}) %all-to-all-start) | async-done | bytes 57376 | tf_op jit(solution)/shard_map/all_to_all | solution.py:530
  21.1 0.1 constant_dynamic-slice_fusion
  21.2 0.0 collective-permute-done.1.far_logs_ref
  21.2 0.0 collective-permute-done.far_pnos_ref
  21.2 1.8 %pack_payload.1 = bf16[8,2,2,80,256]{4,3,2,1,0:T(8,128)(2,1)} custom-call(s32[8,2]{1,0:T(8,128)S(1)} %bitcast.7, s32[8,2]{1,0:T(8,128)S(1)} %bitcast.6, bf16[8,64,256]{2,1,0:T(8,128)(2,1)S(1)} %get-tuple-element.18.pnos_ref, bf16[8,16,256]{2,1,0:T(8,128)(2,1)S(1)} %get-tuple-element.19.logs_ref, bf16[8,64,256]{2,1,0:T(8,128)(2,1)S(1)} %collective-permute-done.far_pnos_ref, ...), custom_call_target="tpu_custom_call" | custom-call | tf_op jit(solution)/shard_map/pack_payload/pallas_call | solution.py:424
  23.0 0.0 copy-start.7
  23.0 0.0 copy-start.9
  23.0 0.0 copy-start.6
  23.0 0.0 copy-start.8
  23.0 0.0 copy-start
  23.0 0.0 copy-start.1
  23.1 0.0 copy-start.2
  23.1 0.0 copy-start.3
  23.1 0.0 copy-start.4
  23.1 0.0 copy-start.5
  23.1 3.7 %all-to-all-start.1 = ((bf16[8,2,2,80,256]{4,3,2,1,0:T(8,128)(2,1)}), bf16[8,2,2,80,256]{4,3,2,1,0:T(8,128)(2,1)S(1)}, u32[]{:S(2)}, u32[]{:S(2)}) async-start(bf16[8,2,2,80,256]{4,3,2,1,0:T(8,128)(2,1)} %pack_payload.1), calls=%async_computation.1 | async-start | bytes 2621440 | tf_op jit(solution)/shard_map/all_to_all | solution.py:541
  26.8 0.0 copy-done.7
  26.8 0.0 copy-done.9
  26.8 0.1 fusion.weight_ref
  26.9 0.0 copy-done.8
  26.9 0.1 add_subtract_fusion.denominator_ref
  27.1 1.6 %prepare.1 = (bf16[512,512]{1,0:T(8,128)(2,1)S(1)}, f32[512,64]{1,0:T(8,128)S(1)}, f32[512,64]{1,0:T(8,128)S(1)}, f32[32,256]{1,0:T(8,128)S(1)}, f32[16,128]{1,0...) custom-call(s32[1]{0:T(128)} %bitcast.half_ref, s32[1,32]{1,0:T(1,128)S(1)} %copy-done.5, ...), custom_call_target="tpu_custom_call" | custom-call | tf_op jit(solution)/shard_map/prepare/pallas_call | solution.py:384
  28.8 0.7 constant_dynamic-slice_fusion.2
  29.5 14.6 %all-to-all-done.1 = bf16[8,2,2,80,256]{4,3,2,1,0:T(8,128)(2,1)S(1)} async-done(((bf16[8,2,2,80,256]{4,3,2,1,0:T(8,128)(2,1)}), bf16[8,2,2,80,256]{4,3,2,1,0:T(8,128)(2,1)S(1)}, u32[]{:S(2)}, u32[]{:S(2)}) %all-to-all-start.1) | async-done | bytes 1310752 | tf_op jit(solution)/shard_map/all_to_all | solution.py:541
  44.0 7.9 %first_sweep.1 = (bf16[4,8,128,512]{3,2,1,0:T(8,128)(2,1)S(1)}, f32[512,64]{1,0:T(8,128)S(1)}, s16[16,80,128]{2,1,0:T(8,128)(2,1)}) custom-call(s32[16,2]{1,0:T(8,128)} %bitcast.8, bf16[512,512]{1,0:T(8,128)(2,1)S(1)} %get-tuple-element.17.own_ref, bf16[16,2,80,256]{3,2,1,0:T(8,128)(2,1)S(1)} %bitcast.5, f32[32,256]{1,0:T(8,128)S(1)} %get-tuple-element.20.atoms_ref, ...), custom_call_target="tpu_custom_call" | custom-call | tf_op jit(solution)/shard_map/first_sweep/pallas_call | solution.py:463
  51.9 16.1 %all_to_all.15.amp_ref = s16[16,80,128]{2,1,0:T(8,128)(2,1)S(1)} all-to-all(s16[16,80,128]{2,1,0:T(8,128)(2,1)} %get-tuple-element.26), channel_id=1, replica_groups=mesh['frag'=2,'half'=2,'near'=8] {'half','near'}, dimensions={0} | all-to-all | bytes 655360 | tf_op jit(solution)/shard_map/all_to_all | solution.py:553
  68.0 3.4 %second_sweep.1 = (f32[8,4096]{1,0:T(8,128)}, f32[8,4096]{1,0:T(8,128)}) custom-call(s32[8,128]{1,0:T(8,128)S(1)} %get-tuple-element.16.mask_ref, bf16[4,8,128,512]{3,2,1,0:T(8,128)(2,1)S(1)} %get-tuple-element.25.cat_ref, f32[4,8,512]{2,1,0:T(8,128)S(1)} %get-tuple-element.22.weights_ref, s16[16,80,128]{2,1,0:T(8,128)(2,1)S(1)} %all_to_all.15.amp_ref, ...), custom_call_target="tpu_custom_call" | custom-call | tf_op jit(solution)/shard_map/second_sweep/pallas_call | solution.py:494
  (7 shorter events, 0.0 us)
Async XLA Ops:
  0.6 20.6 %collective-permute-start = (bf16[8,64,256]{2,1,0:T(8,128)(2,1)}, bf16[8,64,256]{2,1,0:T(8,128)(2,1)S(1)}, u32[]{:S(2)}, u32[]{:S(2)}) collective-permute-start(bf16[8,64,256]{2,1,0:T(8,128)(2,1)} %pnos_ref.1), channel_id=1, source_target_pairs={{0,8},{8,0},{1,9},{9,1},{2,10},{10,2},{3,11},{11,3},{4,12},{12,4},... | collective-permute-start | bytes 786440 | tf_op jit(solution)/shard_map/ppermute | solution.py:525
  6.6 14.5 %all-to-all-start = ((s32[16,8,112]{2,1,0:T(8,128)}), s32[16,8,112]{2,1,0:T(8,128)S(1)}, u32[]{:S(2)}, u32[]{:S(2)}) async-start(s32[16,8,112]{2,1,0:T(8,128)} %broadcast_in_dim.4), calls=%async_computation | async-start | bytes 131072 | tf_op jit(solution)/shard_map/all_to_all | solution.py:530
  10.5 10.7 %collective-permute-start.1 = (bf16[8,16,256]{2,1,0:T(8,128)(2,1)S(1)}, bf16[8,16,256]{2,1,0:T(8,128)(2,1)S(1)}, u32[]{:S(2)}, u32[]{:S(2)}) collective-permute-start(bf16[8,16,256]{2,1,0:T(8,128)(2,1)S(1)} %get-tuple-element.19.logs_ref), channel_id=1, source_target_pairs={{0,8},{8,0},{1,9},{9,1},{2,10},{10,2},{3,11},{11,3},{4,12},{12,4},... | collective-permute-start | bytes 196616 | tf_op jit(solution)/shard_map/ppermute | solution.py:527
  23.0 3.8 %copy-start.7 = (f32[8,16]{1,0:T(8,128)S(1)}, f32[8,16]{1,0:T(8,128)}, u32[]{:S(2)}) copy-start(f32[8,16]{1,0:T(8,128)} %param.14) | copy-start | bytes 1540
  23.0 3.8 %copy-start.9 = (s32[8]{0:T(128)S(1)}, s32[8]{0:T(128)}, u32[]{:S(2)}) copy-start(s32[8]{0:T(128)} %param.15) | copy-start | bytes 100
  23.0 3.9 %copy-start.6 = (f32[8,64]{1,0:T(8,128)S(1)}, f32[8,64]{1,0:T(8,128)}, u32[]{:S(2)}) copy-start(f32[8,64]{1,0:T(8,128)} %param.12) | copy-start | bytes 6148
  23.0 3.9 %copy-start.8 = (f32[8]{0:T(128)S(1)}, f32[8]{0:T(128)}, u32[]{:S(2)}) copy-start(f32[8]{0:T(128)} %param.13) | copy-start | bytes 100
  23.0 4.0 %copy-start = (bf16[8,64,256]{2,1,0:T(8,128)(2,1)S(1)}, bf16[8,64,256]{2,1,0:T(8,128)(2,1)}, u32[]{:S(2)}) copy-start(bf16[8,64,256]{2,1,0:T(8,128)(2,1)} %pnos_ref.1) | copy-start | bytes 786436
  23.0 4.0 %copy-start.1 = (f32[8,4096]{1,0:T(8,128)S(1)}, f32[8,4096]{1,0:T(8,128)}, u32[]{:S(2)}) copy-start(f32[8,4096]{1,0:T(8,128)} %amp_ref.1) | copy-start | bytes 393220
  23.1 4.0 %copy-start.2 = (f32[8,4096]{1,0:T(8,128)S(1)}, f32[8,4096]{1,0:T(8,128)}, u32[]{:S(2)}) copy-start(f32[8,4096]{1,0:T(8,128)} %integrals_ref.1) | copy-start | bytes 393220
  23.1 4.0 %copy-start.3 = (s32[8,16]{1,0:T(8,128)S(1)}, s32[8,16]{1,0:T(8,128)}, u32[]{:S(2)}) copy-start(s32[8,16]{1,0:T(8,128)} %domains_ref.1) | copy-start | bytes 1540
  23.1 4.0 %copy-start.4 = (s32[8,16]{1,0:T(8,128)S(1)}, s32[8,16]{1,0:T(8,128)}, u32[]{:S(2)}) copy-start(s32[8,16]{1,0:T(8,128)} %position_ref.1) | copy-start | bytes 1540
  23.1 4.0 %copy-start.5 = (s32[1,32]{1,0:T(1,128)S(1)}, s32[1,32]{1,0:T(1,128)}, u32[]{:S(2)}) copy-start(s32[1,32]{1,0:T(1,128)} %request_ref.1) | copy-start | bytes 388
  23.1 20.9 %all-to-all-start.1 = ((bf16[8,2,2,80,256]{4,3,2,1,0:T(8,128)(2,1)}), bf16[8,2,2,80,256]{4,3,2,1,0:T(8,128)(2,1)S(1)}, u32[]{:S(2)}, u32[]{:S(2)}) async-start(bf16[8,2,2,80,256]{4,3,2,1,0:T(8,128)(2,1)} %pack_payload.1), calls=%async_computation.1 | async-start | bytes 2621440 | tf_op jit(solution)/shard_map/all_to_all | solution.py:541

commit v8 on v7

--- a/solution.py
+++ b/solution.py
@@ -526,8 +526,9 @@
     near_pnos, logs, table = encode(pnos, amplitudes, domains, request)
     far_logs = lax.ppermute(logs, "half", swap)
 
-    table = jnp.broadcast_to(table[None], (entries,) + table.shape)
+    table = jnp.broadcast_to(table[None].astype(jnp.int16), (entries,) + table.shape)
     table = lax.all_to_all(table, both, split_axis=0, concat_axis=0, tiled=True)
+    table = table.astype(jnp.int32)
     column = table.shape[2] - slots + 2 * mine
     wanted = lax.dynamic_slice(
         table, (0, 0, column + half * 2 * near), (entries, 1, 2)

time: 71.9 us -> 71.1 us (0.989)
  no operation moved by 1% of the time
where the time goes in v8:
time: 71.1 us; the launch traced here: 70.7 us
  waiting for transfers between devices  21.8 us (31%)
  Pallas kernels  15.9 us (22%)
  blocking collectives  15.9 us (22%)
  starting transfers between devices  14.6 us (21%)
  local copies, waits for them, and re-layouts  1.46 us (2%)
  between operations  0.85 us (1%)
    all_to_all x1, blocking collectives, on_device(): amp = lax.all_to_all(amp, both, split_axis=0, concat_axis=0, tiled=True)  15.9 us
    all_to_all x1, waiting for transfers between devices, on_device(): lax.all_to_all(payload, 'near', split_axis=0, concat_axis=0, tiled=True)  14.6 us
    pallas_call x1, Pallas kernels, first_sweep(): pl.pallas_call(first_kernel, grid=(steps,), in_specs=[hbm(), vmem(), bloc...  7.86 us
    all_to_all x1, waiting for transfers between devices, on_device(): table = lax.all_to_all(table, both, split_axis=0, concat_axis=0, tiled=True)  7.2 us
    ppermute x1, starting transfers between devices, on_device(): far_pnos = lax.ppermute(pnos, 'half', swap)  4.1 us
    all_to_all x1, starting transfers between devices, on_device(): table = lax.all_to_all(table, both, split_axis=0, concat_axis=0, tiled=True)  3.91 us
    all_to_all x1, starting transfers between devices, on_device(): lax.all_to_all(payload, 'near', split_axis=0, concat_axis=0, tiled=True)  3.71 us
    pallas_call x1, Pallas kernels, second_sweep(): pl.pallas_call(second_kernel, grid=(steps,), in_specs=[vmem(), cat_spec(s...  3.42 us
  transfers between devices with their start and end apart: 4, of which 2 were waited for; matrix products, arithmetic and copies ran while one was open for 2% of the time, Pallas kernels for 4%

profile of v8, /device:TPU:0, one launch (start us, length us, event | category | flops | bytes accessed | tf_op | source)
XLA Modules:
  0.0 70.7 jit_solution(13184095513770800332)
XLA Ops:
  0.6 4.1 %collective-permute-start = (bf16[8,64,256]{2,1,0:T(8,128)(2,1)}, bf16[8,64,256]{2,1,0:T(8,128)(2,1)S(1)}, u32[]{:S(2)}, u32[]{:S(2)}) collective-permute-start(bf16[8,64,256]{2,1,0:T(8,128)(2,1)} %pnos_ref.1), channel_id=1, source_target_pairs={{0,8},{8,0},{1,9},{9,1},{2,10},{10,2},{3,11},{11,3},{4,12},{12,4},... | collective-permute-start | bytes 786440 | tf_op jit(solution)/shard_map/ppermute | solution.py:525
  4.7 1.2 %encode.1 = (bf16[8,64,256]{2,1,0:T(8,128)(2,1)S(1)}, bf16[8,16,256]{2,1,0:T(8,128)(2,1)S(1)}, s32[8,112]{1,0:T(8,128)S(1)}) custom-call(bf16[8,64,256]{2,1,0:T(8,128)(2,1)} %pnos_ref.1, f32[8,4096]{1,0:T(8,128)} %amp_ref.1, s32[8,16]{1,0:T(8,128)} %domains_ref.1, s32[1,32]{1,0:T(1,128)} %request_ref.1), custom_call_target="tpu_custom_call" | custom-call | tf_op jit(solution)/shard_map/encode/pallas_call | solution.py:402
  6.0 0.6 broadcast_in_dim.4
  6.6 3.9 %all-to-all-start = ((s16[16,8,112]{2,1,0:T(8,128)(2,1)}), s16[16,8,112]{2,1,0:T(8,128)(2,1)S(1)}, u32[]{:S(2)}, u32[]{:S(2)}) async-start(s16[16,8,112]{2,1,0:T(8,128)(2,1)} %broadcast_in_dim.4), calls=%async_computation | async-start | bytes 65536 | tf_op jit(solution)/shard_map/all_to_all | solution.py:530
  10.5 2.8 %collective-permute-start.1 = (bf16[8,16,256]{2,1,0:T(8,128)(2,1)S(1)}, bf16[8,16,256]{2,1,0:T(8,128)(2,1)S(1)}, u32[]{:S(2)}, u32[]{:S(2)}) collective-permute-start(bf16[8,16,256]{2,1,0:T(8,128)(2,1)S(1)} %get-tuple-element.19.logs_ref), channel_id=1, source_target_pairs={{0,8},{8,0},{1,9},{9,1},{2,10},{10,2},{3,11},{11,3},{4,12},{12,4},... | collective-permute-start | bytes 196616 | tf_op jit(solution)/shard_map/ppermute | solution.py:527
  13.4 7.2 %all-to-all-done = s16[16,8,112]{2,1,0:T(8,128)(2,1)S(1)} async-done(((s16[16,8,112]{2,1,0:T(8,128)(2,1)}), s16[16,8,112]{2,1,0:T(8,128)(2,1)S(1)}, u32[]{:S(2)}, u32[]{:S(2)}) %all-to-all-start) | async-done | bytes 28704 | tf_op jit(solution)/shard_map/all_to_all | solution.py:530
  20.6 0.1 constant_dynamic-slice_fusion
  20.7 0.0 collective-permute-done.1.far_logs_ref
  20.7 0.0 collective-permute-done.far_pnos_ref
  20.7 1.8 %pack_payload.1 = bf16[8,2,2,80,256]{4,3,2,1,0:T(8,128)(2,1)} custom-call(s32[8,2]{1,0:T(8,128)S(1)} %bitcast.7, s32[8,2]{1,0:T(8,128)S(1)} %bitcast.6, bf16[8,64,256]{2,1,0:T(8,128)(2,1)S(1)} %get-tuple-element.18.pnos_ref, bf16[8,16,256]{2,1,0:T(8,128)(2,1)S(1)} %get-tuple-element.19.logs_ref, bf16[8,64,256]{2,1,0:T(8,128)(2,1)S(1)} %collective-permute-done.far_pnos_ref, ...), custom_call_target="tpu_custom_call" | custom-call | tf_op jit(solution)/shard_map/pack_payload/pallas_call | solution.py:424
  22.5 0.0 copy-start.7
  22.5 0.0 copy-start.9
  22.5 0.0 copy-start.6
  22.5 0.0 copy-start.8
  22.5 0.0 copy-start
  22.5 0.0 copy-start.1
  22.5 0.0 copy-start.2
  22.5 0.0 copy-start.3
  22.6 0.0 copy-start.4
  22.6 0.0 copy-start.5
  22.6 3.7 %all-to-all-start.1 = ((bf16[8,2,2,80,256]{4,3,2,1,0:T(8,128)(2,1)}), bf16[8,2,2,80,256]{4,3,2,1,0:T(8,128)(2,1)S(1)}, u32[]{:S(2)}, u32[]{:S(2)}) async-start(bf16[8,2,2,80,256]{4,3,2,1,0:T(8,128)(2,1)} %pack_payload.1), calls=%async_computation.1 | async-start | bytes 2621440 | tf_op jit(solution)/shard_map/all_to_all | solution.py:542
  26.3 0.1 fusion.weight_ref
  26.4 0.0 copy-done.8
  26.4 0.1 add_subtract_fusion.denominator_ref
  26.5 0.0 copy-done
  26.6 0.0 copy-done.1
  26.6 1.6 %prepare.1 = (bf16[512,512]{1,0:T(8,128)(2,1)S(1)}, f32[512,64]{1,0:T(8,128)S(1)}, f32[512,64]{1,0:T(8,128)S(1)}, f32[32,256]{1,0:T(8,128)S(1)}, f32[16,128]{1,0...) custom-call(s32[1]{0:T(128)} %bitcast.half_ref, s32[1,32]{1,0:T(1,128)S(1)} %copy-done.5, ...), custom_call_target="tpu_custom_call" | custom-call | tf_op jit(solution)/shard_map/prepare/pallas_call | solution.py:384
  28.2 0.7 constant_dynamic-slice_fusion.2
  28.9 14.6 %all-to-all-done.1 = bf16[8,2,2,80,256]{4,3,2,1,0:T(8,128)(2,1)S(1)} async-done(((bf16[8,2,2,80,256]{4,3,2,1,0:T(8,128)(2,1)}), bf16[8,2,2,80,256]{4,3,2,1,0:T(8,128)(2,1)S(1)}, u32[]{:S(2)}, u32[]{:S(2)}) %all-to-all-start.1) | async-done | bytes 1310752 | tf_op jit(solution)/shard_map/all_to_all | solution.py:542
  43.5 7.9 %first_sweep.1 = (bf16[4,8,128,512]{3,2,1,0:T(8,128)(2,1)S(1)}, f32[512,64]{1,0:T(8,128)S(1)}, s16[16,80,128]{2,1,0:T(8,128)(2,1)}) custom-call(s32[16,2]{1,0:T(8,128)} %bitcast.8, bf16[512,512]{1,0:T(8,128)(2,1)S(1)} %get-tuple-element.17.own_ref, bf16[16,2,80,256]{3,2,1,0:T(8,128)(2,1)S(1)} %bitcast.5, f32[32,256]{1,0:T(8,128)S(1)} %get-tuple-element.20.atoms_ref, ...), custom_call_target="tpu_custom_call" | custom-call | tf_op jit(solution)/shard_map/first_sweep/pallas_call | solution.py:463
  51.4 15.9 %all_to_all.15.amp_ref = s16[16,80,128]{2,1,0:T(8,128)(2,1)S(1)} all-to-all(s16[16,80,128]{2,1,0:T(8,128)(2,1)} %get-tuple-element.26), channel_id=1, replica_groups=mesh['frag'=2,'half'=2,'near'=8] {'half','near'}, dimensions={0} | all-to-all | bytes 655360 | tf_op jit(solution)/shard_map/all_to_all | solution.py:554
  67.3 3.4 %second_sweep.1 = (f32[8,4096]{1,0:T(8,128)}, f32[8,4096]{1,0:T(8,128)}) custom-call(s32[8,128]{1,0:T(8,128)S(1)} %get-tuple-element.16.mask_ref, bf16[4,8,128,512]{3,2,1,0:T(8,128)(2,1)S(1)} %get-tuple-element.25.cat_ref, f32[4,8,512]{2,1,0:T(8,128)S(1)} %get-tuple-element.22.weights_ref, s16[16,80,128]{2,1,0:T(8,128)(2,1)S(1)} %all_to_all.15.amp_ref, ...), custom_call_target="tpu_custom_call" | custom-call | tf_op jit(solution)/shard_map/second_sweep/pallas_call | solution.py:494
  (9 shorter events, 0.0 us)
Async XLA Ops:
  0.6 20.1 %collective-permute-start = (bf16[8,64,256]{2,1,0:T(8,128)(2,1)}, bf16[8,64,256]{2,1,0:T(8,128)(2,1)S(1)}, u32[]{:S(2)}, u32[]{:S(2)}) collective-permute-start(bf16[8,64,256]{2,1,0:T(8,128)(2,1)} %pnos_ref.1), channel_id=1, source_target_pairs={{0,8},{8,0},{1,9},{9,1},{2,10},{10,2},{3,11},{11,3},{4,12},{12,4},... | collective-permute-start | bytes 786440 | tf_op jit(solution)/shard_map/ppermute | solution.py:525
  6.6 13.9 %all-to-all-start = ((s16[16,8,112]{2,1,0:T(8,128)(2,1)}), s16[16,8,112]{2,1,0:T(8,128)(2,1)S(1)}, u32[]{:S(2)}, u32[]{:S(2)}) async-start(s16[16,8,112]{2,1,0:T(8,128)(2,1)} %broadcast_in_dim.4), calls=%async_computation | async-start | bytes 65536 | tf_op jit(solution)/shard_map/all_to_all | solution.py:530
  10.5 10.1 %collective-permute-start.1 = (bf16[8,16,256]{2,1,0:T(8,128)(2,1)S(1)}, bf16[8,16,256]{2,1,0:T(8,128)(2,1)S(1)}, u32[]{:S(2)}, u32[]{:S(2)}) collective-permute-start(bf16[8,16,256]{2,1,0:T(8,128)(2,1)S(1)} %get-tuple-element.19.logs_ref), channel_id=1, source_target_pairs={{0,8},{8,0},{1,9},{9,1},{2,10},{10,2},{3,11},{11,3},{4,12},{12,4},... | collective-permute-start | bytes 196616 | tf_op jit(solution)/shard_map/ppermute | solution.py:527
  22.5 3.8 %copy-start.7 = (f32[8,16]{1,0:T(8,128)S(1)}, f32[8,16]{1,0:T(8,128)}, u32[]{:S(2)}) copy-start(f32[8,16]{1,0:T(8,128)} %param.14) | copy-start | bytes 1540
  22.5 3.8 %copy-start.9 = (s32[8]{0:T(128)S(1)}, s32[8]{0:T(128)}, u32[]{:S(2)}) copy-start(s32[8]{0:T(128)} %param.15) | copy-start | bytes 100
  22.5 3.9 %copy-start.6 = (f32[8,64]{1,0:T(8,128)S(1)}, f32[8,64]{1,0:T(8,128)}, u32[]{:S(2)}) copy-start(f32[8,64]{1,0:T(8,128)} %param.12) | copy-start | bytes 6148
  22.5 3.9 %copy-start.8 = (f32[8]{0:T(128)S(1)}, f32[8]{0:T(128)}, u32[]{:S(2)}) copy-start(f32[8]{0:T(128)} %param.13) | copy-start | bytes 100
  22.5 4.0 %copy-start = (bf16[8,64,256]{2,1,0:T(8,128)(2,1)S(1)}, bf16[8,64,256]{2,1,0:T(8,128)(2,1)}, u32[]{:S(2)}) copy-start(bf16[8,64,256]{2,1,0:T(8,128)(2,1)} %pnos_ref.1) | copy-start | bytes 786436
  22.5 4.0 %copy-start.1 = (f32[8,4096]{1,0:T(8,128)S(1)}, f32[8,4096]{1,0:T(8,128)}, u32[]{:S(2)}) copy-start(f32[8,4096]{1,0:T(8,128)} %amp_ref.1) | copy-start | bytes 393220
  22.5 4.0 %copy-start.2 = (f32[8,4096]{1,0:T(8,128)S(1)}, f32[8,4096]{1,0:T(8,128)}, u32[]{:S(2)}) copy-start(f32[8,4096]{1,0:T(8,128)} %integrals_ref.1) | copy-start | bytes 393220
  22.5 4.0 %copy-start.3 = (s32[8,16]{1,0:T(8,128)S(1)}, s32[8,16]{1,0:T(8,128)}, u32[]{:S(2)}) copy-start(s32[8,16]{1,0:T(8,128)} %domains_ref.1) | copy-start | bytes 1540
  22.6 4.0 %copy-start.4 = (s32[8,16]{1,0:T(8,128)S(1)}, s32[8,16]{1,0:T(8,128)}, u32[]{:S(2)}) copy-start(s32[8,16]{1,0:T(8,128)} %position_ref.1) | copy-start | bytes 1540
  22.6 4.0 %copy-start.5 = (s32[1,32]{1,0:T(1,128)S(1)}, s32[1,32]{1,0:T(1,128)}, u32[]{:S(2)}) copy-start(s32[1,32]{1,0:T(1,128)} %request_ref.1) | copy-start | bytes 388
  22.6 20.9 %all-to-all-start.1 = ((bf16[8,2,2,80,256]{4,3,2,1,0:T(8,128)(2,1)}), bf16[8,2,2,80,256]{4,3,2,1,0:T(8,128)(2,1)S(1)}, u32[]{:S(2)}, u32[]{:S(2)}) async-start(bf16[8,2,2,80,256]{4,3,2,1,0:T(8,128)(2,1)} %pack_payload.1), calls=%async_computation.1 | async-start | bytes 2621440 | tf_op jit(solution)/shard_map/all_to_all | solution.py:542
